TPU v7x, 32 devices: a whole 2x2x4 slice. The times are simulated.
32 devices in a mesh: rel: 4 (over y, x), node: 8 (over z, core).
Axes of the slice: x: 2, y: 2, z: 4, core: 2. Of those that a mesh axis runs over, the one named last changes fastest.
Arguments:
- out_adjoint: bfloat16 [8, 1024, 512], P('node', 'rel'), may hold values from -6 to 6
- layer_input: bfloat16 [8, 1024, 512], P('node'), may hold values from -0.15625 to 0.15625
- rel_weights: bfloat16 [8, 512, 512], P('rel'), may hold values from -0.25 to 0.25
- self_weight: bfloat16 [512, 512], replicated, may hold values from -0.25 to 0.25
- tile_values: bfloat16 [4, 256, 128, 128], P('rel', 'node'), may hold values from 0 to 0.039794922
- tile_rel: int32 [4, 256], P('rel', 'node'), may hold values from 0 to 1
- tile_target: int32 [4, 256], P('rel', 'node'), may hold values from 0 to 7
- tile_src: int32 [4, 256], P('rel', 'node'), may hold values from 0 to 7
- tile_dest: int32 [4, 256, 1], P('rel', 'node'), may hold values from 0 to 7; in each aligned block of 32 rows (0 to 31, 32 to 63, ..., all dimensions but the last counted through in order) at most 8 rows name the same one
Outputs:
- rel_weight_grad: float32 [8, 512, 512], P('rel', 'node')
- d_source: bfloat16 [8, 1024, 512], P('node', 'rel')
Inputs may be any that keep to these rules, and one draw needn't show every extreme that they name: `tile_dest`: among the 32 tiles of one device, at most 8 name the same node shard, and some node shard is named by exactly 8 of them.
All inputs are finite; a program needn't handle non-finite values.
Results may differ from a plain program's by a relative error of at most 0.0056.
Values may be sent and summed in bfloat16 or wider, within the bound.
No kernel may reach another device: no remote copies, remote signals or barrier semaphores. Data moves between devices by JAX's collectives and lax.ppermute only.
A program may use at most 128 MiB of HBM per device.

v0:
```python
import jax
import jax.numpy as jnp
from jax import lax
from jax.sharding import PartitionSpec as P


def on_device(
    out_adjoint,
    layer_input,
    rel_weights,
    self_weight,
    tile_values,
    tile_rel,
    tile_target,
    tile_src,
    tile_dest,
):
    shard_count = lax.axis_size("node")
    tile_edge = tile_values.shape[-1]
    row_count = layer_input.shape[1]
    feature = layer_input.shape[2]
    blocks = row_count // tile_edge
    relations = rel_weights.shape[0]
    tile_count = tile_values.shape[1]
    capacity = 2 * tile_count // shard_count
    slot_count = shard_count * capacity
    adjoint = lax.all_gather(out_adjoint, "rel", axis=1, tiled=True)[0]
    owners = tile_dest[0, :, 0]
    relation = tile_rel[0]
    target = tile_target[0]
    source = tile_src[0]
    shared = owners[:, None] == owners[None, :]
    indices = jnp.arange(tile_count)
    earlier = indices[None, :] < indices[:, None]
    position = jnp.sum(jnp.logical_and(shared, earlier).astype(jnp.int32), axis=1)
    slot_of = owners * capacity + position
    placed = jnp.arange(slot_count)[:, None] == slot_of[None, :]
    placing = placed.astype(jnp.bfloat16)
    group_rows = lax.all_gather(adjoint[None], "node", axis=0, tiled=True)
    packed = relation * (blocks * blocks) + target * blocks + source
    outgoing = jnp.dot(
        placing,
        tile_values[0].reshape(tile_count, tile_edge * tile_edge),
        preferred_element_type=jnp.float32,
    )
    outgoing = outgoing.astype(jnp.bfloat16).reshape(shard_count, capacity, tile_edge, tile_edge)
    packed_slots = jnp.sum(jnp.where(placed, packed[None, :], 0), axis=1).reshape(
        shard_count, capacity
    )
    got_tiles, got_packed = (
        lax.all_to_all(outgoing, "node", split_axis=0, concat_axis=0, tiled=True),
        lax.all_to_all(packed_slots, "node", split_axis=0, concat_axis=0, tiled=True),
    )
    got_packed = got_packed.reshape(slot_count)
    got_target = got_packed // blocks % blocks
    bucket = got_packed // (blocks * blocks) * blocks + got_packed % blocks
    sender = jnp.arange(slot_count) // capacity
    chosen = jnp.take(
        group_rows.reshape(shard_count * blocks, tile_edge, feature),
        sender * blocks + got_target,
        axis=0,
    )
    partial_value = jnp.einsum(
        "sij,sid->sjd",
        got_tiles.reshape(slot_count, tile_edge, tile_edge),
        chosen,
        preferred_element_type=jnp.float32,
    )
    partial_value = partial_value.astype(jnp.bfloat16)
    onehot = (bucket[:, None] == jnp.arange(relations * blocks)[None, :]).astype(jnp.bfloat16)
    summed = jnp.einsum(
        "sk,sx->kx",
        onehot,
        partial_value.reshape(slot_count, tile_edge * feature),
        preferred_element_type=jnp.float32,
    )
    aggregated = summed.reshape(relations, row_count, feature).astype(jnp.bfloat16)
    weight_terms = jnp.einsum(
        "vi,rvj->rij", layer_input[0], aggregated, preferred_element_type=jnp.float32
    )
    rel_weight_grad = lax.psum_scatter(weight_terms, "node", scatter_dimension=1, tiled=True)
    own_rows = lax.psum_scatter(
        jnp.einsum("rvj,rij->vi", aggregated, rel_weights, preferred_element_type=jnp.float32),
        "rel",
        scatter_dimension=0,
        tiled=True,
    )
    self_term = jnp.einsum(
        "vj,ij->vi", out_adjoint[0], self_weight, preferred_element_type=jnp.float32
    )
    d_source = (own_rows + self_term).astype(jnp.bfloat16)[None]
    return (rel_weight_grad, d_source)


def solution(mesh):
    return jax.shard_map(
        on_device,
        mesh=mesh,
        in_specs=(
            P("node", "rel", None),
            P("node", None, None),
            P("rel", None, None),
            P(),
            P("rel", "node", None, None),
            P("rel", "node"),
            P("rel", "node"),
            P("rel", "node"),
            P("rel", "node", None),
        ),
        out_specs=(P("rel", "node", None), P("node", "rel", None)),
        check_vma=False,
    )
```

profile of v0, /device:TPU:0, one launch (start us, length us, event | category | flops | bytes accessed | tf_op | source)
XLA Modules:
  0.0 319.1 jit_solution(7898513398610946683)
XLA Ops:
  8.0 31.3 %all-gather.3.cloned.1.call-done = bf16[1,1024,512]{2,1,0:T(8,128)(2,1)} async-done(((bf16[1,256,512]{2,1,0:T(8,128)(2,1)}), bf16[1,1024,512]{2,1,0:T(8,128)(2,1)}) %all-gather.3.cloned.1.call-update) | async-done | bytes 1048592 | tf_op jit(solution)/shard_map/all_gather | solution.py:27
  39.2 0.9 convert_reduce_fusion
  40.8 0.7 add_bitcast_fusion
  42.3 4.6 %all-to-all-start = ((s32[8,1,8]{2,1,0:T(1,128)}), s32[8,1,8]{2,1,0:T(1,128)S(1)}, u32[]{:S(2)}, u32[]{:S(2)}) async-start(s32[8,1,8]{2,1,0:T(1,128)} %bitcast.2), calls=%async_computation | async-start | bytes 8192 | tf_op jit(solution)/shard_map/all_to_all | solution.py:52
  46.9 3.6 %fusion.7 = bf16[8,8,128,128]{3,1,2,0:T(8,128)(2,1)} fusion(bf16[4,8,128,128]{3,2,1,0:T(8,128)(2,1)} %bitcast.43, s32[32]{0:T(128)S(1)} %multiply_add_fusion), kind=kOutput, calls=%fused_computation.8 | convolution fusion | flops 68159488 | bytes 3145856 | tf_op jit(solution)/shard_map/dot_general | solution.py:41
  50.5 1.9 all-to-all-done
  52.4 3.6 %all-to-all-start.1 = ((bf16[8,8,128,128]{3,1,2,0:T(8,128)(2,1)}), bf16[8,8,128,128]{3,1,2,0:T(8,128)(2,1)S(1)}, u32[]{:S(2)}, u32[]{:S(2)}) async-start(bf16[8,8,128,128]{3,1,2,0:T(8,128)(2,1)} %fusion.7), calls=%async_computation.1 | async-start | bytes 4194304 | tf_op jit(solution)/shard_map/all_to_all | solution.py:51
  57.5 100.3 %all-to-all-done.1 = bf16[8,8,128,128]{3,1,2,0:T(8,128)(2,1)S(1)} async-done(((bf16[8,8,128,128]{3,1,2,0:T(8,128)(2,1)}), bf16[8,8,128,128]{3,1,2,0:T(8,128)(2,1)S(1)}, u32[]{:S(2)}, u32[]{:S(2)}) %all-to-all-start.1) | async-done | bytes 2097184 | tf_op jit(solution)/shard_map/all_to_all | solution.py:51
  157.7 2.8 copy.20
  160.5 6.9 %all-gather.5.cloned.1.call-done = bf16[8,1024,512]{2,1,0:T(8,128)(2,1)} async-done(((bf16[1,1024,512]{2,1,0:T(8,128)(2,1)}), bf16[8,1024,512]{2,1,0:T(8,128)(2,1)}) %all-gather.5.cloned.1.call-update) | async-done | bytes 8388624 | tf_op jit(solution)/shard_map/all_gather | solution.py:39
  167.4 9.1 %gather_fusion = bf16[64,128,512]{2,1,0:T(8,128)(2,1)} fusion(bf16[64,128,512]{2,1,0:T(8,128)(2,1)} %bitcast.41, s32[1024]{0:T(1024)S(1)} %pad_clamp_fusion), kind=kCustom, calls=%fused_computation | custom fusion | bytes 16777472 | tf_op jit(solution)/shard_map/jit(_take)/gather | solution.py:58
  176.5 9.0 %fusion.3 = bf16[64,128,512]{2,1,0:T(8,128)(2,1)} fusion(bf16[64,128,128]{1,2,0:T(8,128)(2,1)S(1)} %bitcast.42, bf16[64,128,512]{2,1,0:T(8,128)(2,1)} %gather_fusion, pred[64]{0:T(512)(128)(4,1)S(1)} %compare_and_fusion), kind=kOutput, calls=%fused_computation.6 | convolution fusion | flops 1082130432 | bytes 18874432 | tf_op jit(solution)/shard_map/sij,sid->sjd/dot_general | solution.py:63
  185.5 11.8 %copy.26 = bf16[8,8,128,512]{3,1,2,0:T(8,128)(2,1)} copy(bf16[8,8,128,512]{3,2,1,0:T(8,128)(2,1)} %bitcast.39) | data formatting | bytes 16777216
  197.3 4.7 %convolution_convert_fusion = bf16[16,65536]{1,0:T(8,128)(2,1)S(1)} fusion(bf16[64,65536]{1,0:T(8,128)(2,1)} %bitcast.40, s32[64]{0:T(128)S(1)} %fusion.17), kind=kOutput, calls=%fused_computation.1 | convolution fusion | flops 135267328 | bytes 10486016 | tf_op jit(solution)/shard_map/sk,sx->kx/dot_general | solution.py:71
  202.0 2.0 convert_element_type.25
  204.0 2.9 convolution_bitcast_fusion.1
  206.8 2.4 copy.22
  209.3 1.5 copy-done.2
  210.9 3.8 %convolution_bitcast_fusion = f32[1024,512]{1,0:T(8,128)} fusion(bf16[2,1024,512]{2,1,0:T(8,128)(2,1)S(1)} %copy-done.2, bf16[2,512,512]{2,1,0:T(8,128)(2,1)} %param.11), kind=kOutput, calls=%fused_computation.9 | convolution fusion | flops 1073741824 | bytes 5242880 | tf_op jit(solution)/shard_map/rvj,rij->vi/dot_general | solution.py:83
  216.6 56.2 %all-reduce.3.cloned.1.call-done = f32[2,512,512]{2,0,1:T(2,128)} async-done(((f32[2,512,512]{2,0,1:T(2,128)}), f32[2,512,512]{2,0,1:T(2,128)}) %all-reduce.3.cloned.1.call-update) | async-done | bytes 2097168
  272.8 1.0 constant_dynamic-slice_fusion
  273.8 0.8 copy.23
  274.5 36.0 %reduce-scatter.2.cloned.1.call-done = f32[256,512]{1,0:T(8,128)} async-done(((f32[1024,512]{1,0:T(8,128)}), f32[256,512]{1,0:T(8,128)}) %reduce-scatter.2.cloned.1.call-update) | async-done | bytes 524304 | tf_op jit(solution)/shard_map/reduce_scatter | solution.py:82
  310.5 2.1 fusion.9
  (31 shorter events, 4.9 us)
Async XLA Ops:
  7.2 196.8 %copy-start = (bf16[1,1024,512]{2,1,0:T(8,128)(2,1)S(1)}, bf16[1,1024,512]{2,1,0:T(8,128)(2,1)}, u32[]{:S(2)}) copy-start(bf16[1,1024,512]{2,1,0:T(8,128)(2,1)} %param.10) | copy-start | bytes 3145732
  7.2 32.0 %all-gather.3.cloned.1.call-start = ((), (), s32[]{:S(2)}) async-start(), calls=%async_computation.3 | async-start | bytes 1310720 | tf_op jit(solution)/shard_map/all_gather | solution.py:27
  7.9 159.5 %all-gather.5.cloned.1.call-start = ((), (), s32[]{:S(2)}) async-start(), calls=%async_computation.4 | async-start | bytes 9437184 | tf_op jit(solution)/shard_map/all_gather | solution.py:39
  42.3 10.1 %all-to-all-start = ((s32[8,1,8]{2,1,0:T(1,128)}), s32[8,1,8]{2,1,0:T(1,128)S(1)}, u32[]{:S(2)}, u32[]{:S(2)}) async-start(s32[8,1,8]{2,1,0:T(1,128)} %bitcast.2), calls=%async_computation | async-start | bytes 8192 | tf_op jit(solution)/shard_map/all_to_all | solution.py:52
  52.4 105.3 %all-to-all-start.1 = ((bf16[8,8,128,128]{3,1,2,0:T(8,128)(2,1)}), bf16[8,8,128,128]{3,1,2,0:T(8,128)(2,1)S(1)}, u32[]{:S(2)}, u32[]{:S(2)}) async-start(bf16[8,8,128,128]{3,1,2,0:T(8,128)(2,1)} %fusion.7), calls=%async_computation.1 | async-start | bytes 4194304 | tf_op jit(solution)/shard_map/all_to_all | solution.py:51
  56.0 216.8 %all-reduce.3.cloned.1.call-start = ((), (), s32[]{:S(2)}) async-start(), calls=%async_computation.6 | async-start | bytes 4194304
  167.4 9.1 %copy-start.1 = (bf16[8,8,128,128]{2,3,1,0:T(8,128)(2,1)S(1)}, bf16[8,8,128,128]{2,3,1,0:T(8,128)(2,1)}, u32[]{:S(2)}) copy-start(bf16[8,8,128,128]{2,3,1,0:T(8,128)(2,1)} %copy.20) | copy-start | bytes 6291460
  209.3 1.6 copy-start.2
  209.3 101.2 %reduce-scatter.2.cloned.1.call-start = ((), (), s32[]{:S(2)}) async-start(), calls=%async_computation.5 | async-start | bytes 2621440 | tf_op jit(solution)/shard_map/reduce_scatter | solution.py:82
  214.7 0.7 copy-start.5
  214.7 95.8 %copy-start.3 = (bf16[1,256,512]{2,1,0:T(8,128)(2,1)S(1)}, bf16[1,256,512]{2,1,0:T(8,128)(2,1)}, u32[]{:S(2)}) copy-start(bf16[1,256,512]{2,1,0:T(8,128)(2,1)} %param.9) | copy-start | bytes 786436
  214.7 95.8 %copy-start.4 = (bf16[512,512]{1,0:T(8,128)(2,1)S(1)}, bf16[512,512]{1,0:T(8,128)(2,1)}, u32[]{:S(2)}) copy-start(bf16[512,512]{1,0:T(8,128)(2,1)} %param.12) | copy-start | bytes 1572868
Sparse Core Ops, SparseCore 0:
  9.9 29.3 all-gather.2
  40.8 126.5 all-gather.4
  209.4 63.3 all-reduce.2
  275.6 34.8 reduce-scatter.1
where the time goes:
time: 320 us; the launch traced here: 319 us
  waiting for transfers between devices  233 us (73%)
  local copies, waits for them, and re-layouts  33.9 us (11%)
  matrix products  26.1 us (8%)
  between operations  14.5 us (5%)
  starting transfers between devices  8.37 us (3%)
    all_to_all x1, waiting for transfers between devices, on_device(): lax.all_to_all(outgoing, 'node', split_axis=0, concat_axis=0, tiled=True)  100 us
    unnamed x5, waiting for transfers between devices  57 us
    reduce_scatter x1, waiting for transfers between devices, on_device(): lax.psum_scatter(jnp.einsum('rvj,rij->vi', aggregated, rel_weights, prefe...  36 us
    all_gather x1, waiting for transfers between devices, on_device(): adjoint = lax.all_gather(out_adjoint, 'rel', axis=1, tiled=True)[0]  31.3 us
    unnamed x16, local copies, waits for them, and re-layouts  16.2 us
    gather x1, local copies, waits for them, and re-layouts, on_device(): jnp.take(group_rows.reshape(shard_count * blocks, tile_edge, feature), se...  9.06 us
    dot_general x1, matrix products, on_device(): jnp.einsum('sij,sid->sjd', got_tiles.reshape(slot_count, tile_edge, tile_...  9.03 us
    all_gather x1, waiting for transfers between devices, on_device(): group_rows = lax.all_gather(adjoint[None], 'node', axis=0, tiled=True)  6.87 us
  transfers between devices with their start and end apart: 6, of which 6 were waited for; matrix products, arithmetic and copies ran while one was open for 5% of the time, Pallas kernels for 0%

commit v1 on v0

v1 whole, which is shorter than its diff:
```python
import functools

import jax
import jax.numpy as jnp
from jax import lax
from jax.experimental import pallas as pl
from jax.experimental.pallas import tpu as pltpu
from jax.sharding import PartitionSpec as P

CAPACITY = 8
CORES = 2


def place_kernel(chips, slots, dest_ref, place_ref, tiles_ref, *refs):
    outs, (order, count, sem) = refs[: chips - 1], refs[chips - 1 :]
    chip = place_ref[0]
    for j in range(chips):
        count[j] = 0
    for s in range(chips * slots):
        order[s] = 0

    def rank(t, carry):
        j = (dest_ref[t] // CORES) ^ chip
        p = count[j]
        order[j * slots + p] = t
        count[j] = p + 1
        return carry

    lax.fori_loop(0, dest_ref.shape[0], rank, 0)
    for j in range(chips - 1, 0, -1):
        for p in range(slots):
            pltpu.make_async_copy(
                tiles_ref.at[order[j * slots + p]], outs[j - 1].at[p], sem.at[j - 1]
            ).start()
    for j in range(chips - 1, 0, -1):
        pltpu.make_async_copy(outs[j - 1], outs[j - 1], sem.at[j - 1]).wait()


def place_tiles(dest, place, tiles, chips, slots):
    edge = tiles.shape[-1]
    return pl.pallas_call(
        functools.partial(place_kernel, chips, slots),
        out_shape=[jax.ShapeDtypeStruct((slots, edge, edge), tiles.dtype)] * (chips - 1),
        in_specs=[
            pl.BlockSpec(memory_space=pltpu.SMEM),
            pl.BlockSpec(memory_space=pltpu.SMEM),
            pl.BlockSpec(memory_space=pl.ANY),
        ],
        out_specs=[pl.BlockSpec(memory_space=pl.ANY)] * (chips - 1),
        scratch_shapes=[
            pltpu.SMEM((chips * slots,), jnp.int32),
            pltpu.SMEM((chips,), jnp.int32),
            pltpu.SemaphoreType.DMA((chips - 1,)),
        ],
        cost_estimate=pl.CostEstimate(
            flops=0, bytes_accessed=4 * (chips - 1) * slots * edge * edge, transcendentals=0
        ),
        name="place_tiles",
    )(dest, place, tiles)


def main_kernel(chips, groups, blocks, relations, *refs):
    meta_ref, count_ref, place_ref, own_ref = refs[:4]
    refs = refs[4:]
    sent, refs = refs[: chips - 1], refs[chips - 1 :]
    pieces, refs = refs[: chips * groups], refs[chips * groups :]
    inputs_ref, weights_ref = refs[:2]
    grad_far, grad_own, rows_far, rows_own = refs[2:6]
    adjoint, own_tiles, sent_tiles, total, sem = refs[6:]
    chip, group, core = place_ref[0], place_ref[1], place_ref[2]
    edge = own_ref.shape[-1]
    feature = adjoint.shape[-1]
    piece = pieces[0].shape[0]
    span = relations * blocks

    def copies(j):
        out = []
        for m in range(groups):
            row = pl.multiple_of((group ^ m) * piece, piece)
            out.append(
                pltpu.make_async_copy(
                    pieces[j * groups + m], adjoint.at[j, pl.ds(row, piece)], sem.at[j, m]
                )
            )
        if j == 0:
            out.append(pltpu.make_async_copy(own_ref, own_tiles, sem.at[j, groups]))
        else:
            out.append(
                pltpu.make_async_copy(sent[j - 1], sent_tiles.at[j - 1], sem.at[j, groups])
            )
        return out

    for j in range(chips):
        for copy in copies(j):
            copy.start()
    total[...] = jnp.zeros_like(total)
    for j in range(chips):
        for copy in copies(j):
            copy.wait()

        def one(p, carry):
            code = meta_ref[j, p]
            bucket = code % (CORES * span)
            rest = code // (CORES * span)
            row = pl.multiple_of((rest % blocks) * edge, edge)
            tile = own_tiles[rest // blocks] if j == 0 else sent_tiles[j - 1, p]
            partial = lax.dot_general(
                tile,
                adjoint[j, pl.ds(row, edge), :],
                (((0,), (0,)), ((), ())),
                preferred_element_type=jnp.float32,
            )
            total[bucket] += partial.astype(jnp.bfloat16).astype(jnp.float32)
            return carry

        lax.fori_loop(0, count_ref[j], one, 0)

    rows = blocks * edge
    share = feature // (chips * CORES)
    for r in range(relations):
        grad = jnp.zeros((feature, feature), jnp.float32)
        for h in range(CORES):
            part = total[pl.ds((h * relations + r) * blocks, blocks)].astype(jnp.bfloat16)
            grad += jnp.dot(
                inputs_ref[h], part.reshape(rows, feature), preferred_element_type=jnp.float32
            )
        for far in range(CORES):
            out = grad_far if far else grad_own
            for c in range(chips):
                for h in range(CORES):
                    piece_of = grad[(c * CORES + h) * share : (c * CORES + h + 1) * share]

                    @pl.when(h == (core ^ far))
                    def _():
                        out[chip ^ c, r] = piece_of.astype(out.dtype)

    for h in range(CORES):
        value = jnp.zeros((rows, feature), jnp.float32)
        for r in range(relations):
            part = total[pl.ds((h * relations + r) * blocks, blocks)].astype(jnp.bfloat16)
            value += lax.dot_general(
                part.reshape(rows, feature),
                weights_ref[r],
                (((1,), (1,)), ((), ())),
                preferred_element_type=jnp.float32,
            )
        for far in range(CORES):
            out = rows_far if far else rows_own

            @pl.when(h == (core ^ far))
            def _():
                for q in range(groups):
                    out[group ^ q] = value[q * piece : (q + 1) * piece].astype(out.dtype)


def main(meta, count, place, own_tiles, sent, pieces, inputs, weights, chips, groups, blocks):
    edge = own_tiles.shape[-1]
    relations, feature = weights.shape[0], weights.shape[-1]
    slots = meta.shape[1]
    piece = pieces[0].shape[0]
    share = feature // (chips * CORES)
    rows = blocks * edge
    smem = pl.BlockSpec(memory_space=pltpu.SMEM)
    hbm = pl.BlockSpec(memory_space=pl.ANY)
    vmem = pl.BlockSpec(memory_space=pltpu.VMEM)
    return pl.pallas_call(
        functools.partial(main_kernel, chips, groups, blocks, relations),
        out_shape=[
            jax.ShapeDtypeStruct((chips, relations, share, feature), jnp.bfloat16),
            jax.ShapeDtypeStruct((chips, relations, share, feature), jnp.float32),
            jax.ShapeDtypeStruct((groups, piece, feature), jnp.bfloat16),
            jax.ShapeDtypeStruct((groups, piece, feature), jnp.float32),
        ],
        in_specs=[smem, smem, smem, hbm] + [hbm] * (len(sent) + len(pieces)) + [vmem, vmem],
        out_specs=[vmem] * 4,
        scratch_shapes=[
            pltpu.VMEM((chips, rows, feature), jnp.bfloat16),
            pltpu.VMEM(own_tiles.shape, jnp.bfloat16),
            pltpu.VMEM((chips - 1, slots, edge, edge), jnp.bfloat16),
            pltpu.VMEM((CORES * relations * blocks, edge, feature), jnp.float32),
            pltpu.SemaphoreType.DMA((chips, groups + 1)),
        ],
        compiler_params=pltpu.CompilerParams(vmem_limit_bytes=44 * 1024 * 1024),
        cost_estimate=pl.CostEstimate(
            flops=8 * rows * feature * feature, bytes_accessed=20_000_000, transcendentals=0
        ),
        name="tiles_and_products",
    )(meta, count, place, own_tiles, *sent, *pieces, inputs, weights)


def on_device(
    out_adjoint,
    layer_input,
    rel_weights,
    self_weight,
    tile_values,
    tile_rel,
    tile_target,
    tile_src,
    tile_dest,
):
    nodes = lax.axis_size("node")
    groups = lax.axis_size("rel")
    chips = nodes // CORES
    node = lax.axis_index("node")
    group = lax.axis_index("rel")
    chip, core = node // CORES, node % CORES
    edge = tile_values.shape[-1]
    rows = layer_input.shape[1]
    feature = layer_input.shape[2]
    blocks = rows // edge
    relations = rel_weights.shape[0]
    tiles = tile_values.shape[1]
    slots = CORES * CAPACITY

    def across(value, axis, size, mask):
        return lax.ppermute(value, axis, [(i, i ^ mask) for i in range(size)])

    def to_chip(value, j):
        return across(value, "node", nodes, CORES * j)

    own = out_adjoint[0]
    place = jnp.stack([chip, group, core]).astype(jnp.int32)
    dest = tile_dest[0, :, 0]

    by_chip = {0: own}
    bit = chips // 2
    while bit:
        for j in list(by_chip):
            by_chip[j ^ bit] = to_chip(by_chip[j], bit)
        bit //= 2
    sent = place_tiles(dest, place, tile_values[0], chips, slots)
    sent = [to_chip(sent[j - 1], j) for j in range(1, chips)]
    pieces = []
    for j in range(chips):
        pieces.append(by_chip[j])
        for m in range(1, groups):
            pieces.append(across(by_chip[j], "rel", groups, m))

    index = jnp.arange(tiles, dtype=jnp.int32)
    code = (index * blocks + tile_target[0]) * (CORES * relations * blocks) + (
        (dest % CORES) * relations + tile_rel[0]
    ) * blocks + tile_src[0]
    gathered = lax.all_gather(jnp.stack([dest // CORES, code]), "node", axis=0)
    gathered = gathered.reshape(chips, CORES, 2, tiles)
    gathered = lax.dynamic_index_in_dim(gathered, core, 1, keepdims=False)
    turned = (jnp.arange(chips)[:, None] ^ chip) == jnp.arange(chips)[None, :]
    gathered = jnp.sum(jnp.where(turned[:, :, None, None], gathered[None], 0), axis=1)
    mine = gathered[:, 0] == chip
    rank = jnp.sum(
        jnp.where(mine[:, None, :] & (index[None, :] < index[:, None])[None], 1, 0), axis=2
    )
    chosen = mine[:, None, :] & (rank[:, None, :] == jnp.arange(slots)[None, :, None])
    meta = jnp.sum(jnp.where(chosen, gathered[:, 1][:, None, :], 0), axis=2).astype(jnp.int32)
    count = jnp.sum(mine, axis=1).astype(jnp.int32)

    near = layer_input[0]
    far = across(near, "node", nodes, 1)
    inputs = jnp.stack([jnp.where(core == 0, near, far), jnp.where(core == 0, far, near)])
    inputs = jnp.swapaxes(inputs, 1, 2)

    grad_far, grad_own, rows_far, rows_own = main(
        meta, count, place, tile_values[0], sent, pieces, inputs, rel_weights, chips, groups, blocks
    )
    grad_far = across(grad_far, "node", nodes, 1)
    rows_far = across(rows_far, "node", nodes, 1)
    grad = grad_own + grad_far.astype(jnp.float32)
    others = [to_chip(grad[j].astype(jnp.bfloat16), j) for j in range(1, chips)]
    rel_weight_grad = grad[0]
    for other in others:
        rel_weight_grad += other.astype(jnp.float32)

    totals = rows_own + rows_far.astype(jnp.float32)
    others = [
        across(totals[m].astype(jnp.bfloat16), "rel", groups, m) for m in range(1, groups)
    ]
    d_source = totals[0] + jnp.einsum(
        "vj,ij->vi", own, self_weight, preferred_element_type=jnp.float32
    )
    for other in others:
        d_source += other.astype(jnp.float32)
    return rel_weight_grad, d_source.astype(jnp.bfloat16)[None]


def solution(mesh):
    return jax.shard_map(
        on_device,
        mesh=mesh,
        in_specs=(
            P("node", "rel", None),
            P("node", None, None),
            P("rel", None, None),
            P(),
            P("rel", "node", None, None),
            P("rel", "node"),
            P("rel", "node"),
            P("rel", "node"),
            P("rel", "node", None),
        ),
        out_specs=(P("rel", "node", None), P("node", "rel", None)),
        check_vma=False,
    )
```

time: 320 us -> 196 us (0.61)
  waiting for transfers between devices: 233 us -> 65.8 us
  Pallas kernels: 0 us -> 65.8 us
  starting transfers between devices: 8.37 us -> 41.3 us
  local copies, waits for them, and re-layouts: 33.9 us -> 3.12 us
  matrix products: 26.1 us -> 0.33 us
  between operations: 14.5 us -> 0.93 us
  blocking collectives: 0 us -> 11.2 us
  other arithmetic: 3.08 us -> 6.75 us
    all_to_all x2 -> x0, waiting for transfers between devices: 102 us -> none  [the longest x1 100 us: on_device(): lax.all_to_all(outgoing, 'node', split_axis=0, concat_axis=0, tiled=True)]
    pallas_call x0 -> x2, Pallas kernels: none -> 65.8 us  [the longest x1 50.1 us: place_tiles(): pl.pallas_call(functools.partial(place_kernel, chips, slots), out_shape=[...]
    ppermute x0 -> x27, waiting for transfers between devices: none -> 65.8 us  [across(): return lax.ppermute(value, axis, [(i, i ^ mask) for i in range(size)])]
    unnamed x5 -> x0, waiting for transfers between devices: 57 us -> none
    ppermute x0 -> x27, starting transfers between devices: none -> 41.3 us  [across(): return lax.ppermute(value, axis, [(i, i ^ mask) for i in range(size)])]
    all_gather x2 -> x0, waiting for transfers between devices: 38.1 us -> none  [the longest x1 31.3 us: on_device(): adjoint = lax.all_gather(out_adjoint, 'rel', axis=1, tiled=True)[0]]
    reduce_scatter x1 -> x0, waiting for transfers between devices: 36 us -> none  [on_device(): lax.psum_scatter(jnp.einsum('rvj,rij->vi', aggregated, rel_weights, prefe...]
    dot_general x6 -> x1, matrix products: 26.1 us -> 0.33 us  [on_device(): jnp.einsum('vj,ij->vi', own, self_weight, preferred_element_type=jnp.floa...]
  transfers between devices with their start and end apart: 6 -> 27, of which waited for: 6 -> 10; matrix products, arithmetic and copies ran while one was open for 5% -> 4% of each run, Pallas kernels for 0% -> 26%
where the time goes in v1:
time: 196 us; the launch traced here: 195 us
  waiting for transfers between devices  65.8 us (34%)
  Pallas kernels  65.8 us (34%)
  starting transfers between devices  41.3 us (21%)
  blocking collectives  11.2 us (6%)
  other arithmetic  6.75 us (3%)
  local copies, waits for them, and re-layouts  3.12 us (2%)
    ppermute x27, waiting for transfers between devices, across(): return lax.ppermute(value, axis, [(i, i ^ mask) for i in range(size)])  65.8 us
    pallas_call x1, Pallas kernels, place_tiles(): pl.pallas_call(functools.partial(place_kernel, chips, slots), out_shape=[...  50.1 us
    ppermute x27, starting transfers between devices, across(): return lax.ppermute(value, axis, [(i, i ^ mask) for i in range(size)])  41.3 us
    pallas_call x1, Pallas kernels, main(): pl.pallas_call(functools.partial(main_kernel, chips, groups, blocks, rela...  15.7 us
    all_gather x1, blocking collectives, on_device(): gathered = lax.all_gather(jnp.stack([dest // CORES, code]), 'node', axis=0)  11.2 us
  transfers between devices with their start and end apart: 27, of which 10 were waited for; matrix products, arithmetic and copies ran while one was open for 4% of the time, Pallas kernels for 26%

profile of v1, /device:TPU:0, one launch (start us, length us, event | category | flops | bytes accessed | tf_op | source)
XLA Modules:
  0.0 195.2 jit_solution(8967331880669704658)
XLA Ops:
  0.7 4.1 %collective-permute-start.10 = (bf16[256,512]{1,0:T(8,128)(2,1)}, bf16[256,512]{1,0:T(8,128)(2,1)S(1)}, u32[]{:S(2)}, u32[]{:S(2)}) collective-permute-start(bf16[256,512]{1,0:T(8,128)(2,1)} %bitcast.82), channel_id=1, source_target_pairs={{0,4},{1,5},{2,6},{3,7},{4,0},{5,1},{6,2},{7,3},{8,12},{9,13},{10,... | collective-permute-start | bytes 786440 | tf_op jit(solution)/shard_map/ppermute | solution.py:217
  4.8 1.6 collective-permute-start.6
  7.9 1.5 collective-permute-start.4
  9.4 2.3 %copy.16 = bf16[1,1024,512]{1,2,0:T(8,128)(2,1)} copy(bf16[1,1024,512]{2,1,0:T(8,128)(2,1)} %param.10) | data formatting | bytes 2097152 | tf_op args[1]
  11.8 11.2 %all-gather.1 = s32[8,2,32]{2,1,0:T(2,128)S(1)} all-gather(s32[1,2,32]{2,1,0:T(2,128)S(1)} %add_bitcast_fusion), channel_id=2, replica_groups=mesh['rel'=4,'node'=8] {'node'}, dimensions={0}, use_global_device_ids=true | all-gather | bytes 2304 | tf_op jit(solution)/shard_map/all_gather | solution.py:244
  22.9 2.5 %collective-permute-start.5 = (bf16[256,512]{1,0:T(8,128)(2,1)S(1)}, bf16[256,512]{1,0:T(8,128)(2,1)}, u32[]{:S(2)}, u32[]{:S(2)}) collective-permute-start(bf16[256,512]{1,0:T(8,128)(2,1)S(1)} %bitcast.86), channel_id=1, source_target_pairs={{0,24},{8,16},{16,8},{24,0},{1,25},{9,17},{17,9},{25,1},{2,26},{10... | collective-permute-start | bytes 786440 | tf_op jit(solution)/shard_map/ppermute | solution.py:217
  26.0 50.1 %place_tiles.1 = (bf16[16,128,128]{2,1,0:T(8,128)(2,1)}, bf16[16,128,128]{2,1,0:T(8,128)(2,1)}, bf16[16,128,128]{2,1,0:T(8,128)(2,1)}) custom-call(s32[32]{0:T(128)} %bitcast.92, s32[3]{0:T(128)} %pad_add_fusion.place_ref.refs_2_, bf16[32,128,128]{2,1,0:T(8,128)(2,1)} %bitcast.80), custom_call_target="tpu_custom_call" | custom-call | bytes 3145728 | tf_op jit(solution)/shard_map/place_tiles/pallas_call | solution.py:41
  77.3 3.3 %collective-permute-start.2 = (bf16[16,128,128]{2,1,0:T(8,128)(2,1)}, bf16[16,128,128]{2,1,0:T(8,128)(2,1)S(1)}, u32[]{:S(2)}, u32[]{:S(2)}) collective-permute-start(bf16[16,128,128]{2,1,0:T(8,128)(2,1)} %get-tuple-element.11), channel_id=1, source_target_pairs={{0,6},{1,7},{2,4},{3,5},{4,2},{5,3},{6,0},{7,1},{8,14},{9,15},{10,... | collective-permute-start | bytes 1572872 | tf_op jit(solution)/shard_map/ppermute | solution.py:217
  81.0 20.5 %collective-permute-done.refs_4_ = bf16[16,128,128]{2,1,0:T(8,128)(2,1)S(1)} collective-permute-done((bf16[16,128,128]{2,1,0:T(8,128)(2,1)}, bf16[16,128,128]{2,1,0:T(8,128)(2,1)S(1)}, u32[]{:S(2)}, u32[]{:S(2)}) %collective-permute-start) | collective-permute-done | bytes 524320 | tf_op jit(solution)/shard_map/ppermute | solution.py:217
  102.0 12.8 %collective-permute-done.1.refs_5_ = bf16[16,128,128]{2,1,0:T(8,128)(2,1)S(1)} collective-permute-done((bf16[16,128,128]{2,1,0:T(8,128)(2,1)}, bf16[16,128,128]{2,1,0:T(8,128)(2,1)S(1)}, u32[]{:S(2)}, u32[]{:S(2)}) %collective-permute-start.1) | collective-permute-done | bytes 524320 | tf_op jit(solution)/shard_map/ppermute | solution.py:217
  116.8 1.6 collective-permute-done.14.refs_19_
  120.5 7.7 %collective-permute-done.12.refs_17_ = bf16[256,512]{1,0:T(8,128)(2,1)} collective-permute-done((bf16[256,512]{1,0:T(8,128)(2,1)S(1)}, bf16[256,512]{1,0:T(8,128)(2,1)}, u32[]{:S(2)}, u32[]{:S(2)}) %collective-permute-start.12) | collective-permute-done | bytes 262176 | tf_op jit(solution)/shard_map/ppermute | solution.py:217
  129.8 2.4 %collective-permute-start.15 = (bf16[256,512]{1,0:T(8,128)(2,1)}, bf16[256,512]{1,0:T(8,128)(2,1)S(1)}, u32[]{:S(2)}, u32[]{:S(2)}) collective-permute-start(bf16[256,512]{1,0:T(8,128)(2,1)} %copy-done.3), channel_id=1, source_target_pairs={{0,8},{8,0},{16,24},{24,16},{1,9},{9,1},{17,25},{25,17},{2,10},{10... | collective-permute-start | bytes 786440 | tf_op jit(solution)/shard_map/ppermute | solution.py:217
  132.1 1.5 collective-permute-start.17
  133.7 1.7 select_bitcast_fusion.1
  135.4 1.5 maximum_bitcast_fusion.refs_23_
  136.9 4.7 %collective-permute-done.8.refs_13_ = bf16[256,512]{1,0:T(8,128)(2,1)S(1)} collective-permute-done((bf16[256,512]{1,0:T(8,128)(2,1)S(1)}, bf16[256,512]{1,0:T(8,128)(2,1)S(1)}, u32[]{:S(2)}, u32[]{:S(2)}) %collective-permute-start.8) | collective-permute-done | bytes 262176 | tf_op jit(solution)/shard_map/ppermute | solution.py:217
  142.4 7.0 %collective-permute-done.16.refs_21_ = bf16[256,512]{1,0:T(8,128)(2,1)S(1)} collective-permute-done((bf16[256,512]{1,0:T(8,128)(2,1)}, bf16[256,512]{1,0:T(8,128)(2,1)S(1)}, u32[]{:S(2)}, u32[]{:S(2)}) %collective-permute-start.16) | collective-permute-done | bytes 262176 | tf_op jit(solution)/shard_map/ppermute | solution.py:217
  149.4 15.7 %tiles_and_products.1 = (bf16[4,2,64,512]{3,2,1,0:T(8,128)(2,1)S(1)}, f32[4,2,64,512]{3,2,1,0:T(8,128)S(1)}, bf16[4,256,512]{2,1,0:T(8,128)(2,1)S(1)}, f32[4,256,512]{2,1,0:T(8,128)}) custom-call(s32[4,16]{1,0:T(4,128)S(1)} %select_reduce_fusion.1.refs_0_, s32[4]{0:T(128)S(1)} %get-tuple-element.20.refs_1_, s32[3]{0:T(128)S(1)} %copy-done.5, ...), custom_call_target="tpu_custom_call" | custom-call | flops 2147483648 | bytes 20000000 | tf_op jit(solution)/shard_map/tiles_and_products/pallas_call | solution.py:166
  167.4 10.1 %collective-permute-start.20 = (bf16[2,64,512]{2,1,0:T(8,128)(2,1)S(1)}, bf16[2,64,512]{2,1,0:T(8,128)(2,1)S(1)}, u32[]{:S(2)}, u32[]{:S(2)}) collective-permute-start(bf16[2,64,512]{2,1,0:T(8,128)(2,1)S(1)} %get-tuple-element.27), channel_id=1, source_target_pairs={{0,2},{1,3},{2,0},{3,1},{4,6},{5,7},{6,4},{7,5},{8,10},{9,11},{10,... | collective-permute-start | bytes 393224 | tf_op jit(solution)/shard_map/ppermute | solution.py:217
  177.4 2.4 %collective-permute-start.22 = (bf16[2,64,512]{2,1,0:T(8,128)(2,1)S(1)}, bf16[2,64,512]{2,1,0:T(8,128)(2,1)S(1)}, u32[]{:S(2)}, u32[]{:S(2)}) collective-permute-start(bf16[2,64,512]{2,1,0:T(8,128)(2,1)S(1)} %get-tuple-element.28), channel_id=1, source_target_pairs={{0,6},{1,7},{2,4},{3,5},{4,2},{5,3},{6,0},{7,1},{8,14},{9,15},{10,... | collective-permute-start | bytes 393224 | tf_op jit(solution)/shard_map/ppermute | solution.py:217
  181.9 2.1 %collective-permute-start.26 = (bf16[256,512]{1,0:T(8,128)(2,1)S(1)}, bf16[256,512]{1,0:T(8,128)(2,1)S(1)}, u32[]{:S(2)}, u32[]{:S(2)}) collective-permute-start(bf16[256,512]{1,0:T(8,128)(2,1)S(1)} %get-tuple-element.25), channel_id=1, source_target_pairs={{0,24},{8,16},{16,8},{24,0},{1,25},{9,17},{17,9},{25,1},{2,26},{10... | collective-permute-start | bytes 786440 | tf_op jit(solution)/shard_map/ppermute | solution.py:217
  184.3 4.8 %collective-permute-done.21 = bf16[2,64,512]{2,1,0:T(8,128)(2,1)S(1)} collective-permute-done((bf16[2,64,512]{2,1,0:T(8,128)(2,1)S(1)}, bf16[2,64,512]{2,1,0:T(8,128)(2,1)S(1)}, u32[]{:S(2)}, u32[]{:S(2)}) %collective-permute-start.21) | collective-permute-done | bytes 131104 | tf_op jit(solution)/shard_map/ppermute | solution.py:217
  189.9 4.5 %collective-permute-done.25 = bf16[256,512]{1,0:T(8,128)(2,1)S(1)} collective-permute-done((bf16[256,512]{1,0:T(8,128)(2,1)S(1)}, bf16[256,512]{1,0:T(8,128)(2,1)S(1)}, u32[]{:S(2)}, u32[]{:S(2)}) %collective-permute-start.25) | collective-permute-done | bytes 262176 | tf_op jit(solution)/shard_map/ppermute | solution.py:217
  (78 shorter events, 16.7 us)
Async XLA Ops:
  0.7 22.2 %collective-permute-start.10 = (bf16[256,512]{1,0:T(8,128)(2,1)}, bf16[256,512]{1,0:T(8,128)(2,1)S(1)}, u32[]{:S(2)}, u32[]{:S(2)}) collective-permute-start(bf16[256,512]{1,0:T(8,128)(2,1)} %bitcast.82), channel_id=1, source_target_pairs={{0,4},{1,5},{2,6},{3,7},{4,0},{5,1},{6,2},{7,3},{8,12},{9,13},{10,... | collective-permute-start | bytes 786440 | tf_op jit(solution)/shard_map/ppermute | solution.py:217
  4.8 71.3 %collective-permute-start.6 = (bf16[256,512]{1,0:T(8,128)(2,1)}, bf16[256,512]{1,0:T(8,128)(2,1)S(1)}, u32[]{:S(2)}, u32[]{:S(2)}) collective-permute-start(bf16[256,512]{1,0:T(8,128)(2,1)} %bitcast.83), channel_id=1, source_target_pairs={{0,2},{1,3},{2,0},{3,1},{4,6},{5,7},{6,4},{7,5},{8,10},{9,11},{10,... | collective-permute-start | bytes 786440 | tf_op jit(solution)/shard_map/ppermute | solution.py:217
  6.4 69.9 %collective-permute-start.3 = (bf16[256,512]{1,0:T(8,128)(2,1)}, bf16[256,512]{1,0:T(8,128)(2,1)S(1)}, u32[]{:S(2)}, u32[]{:S(2)}) collective-permute-start(bf16[256,512]{1,0:T(8,128)(2,1)} %bitcast.84), channel_id=1, source_target_pairs={{0,8},{8,0},{16,24},{24,16},{1,9},{9,1},{17,25},{25,17},{2,10},{10... | collective-permute-start | bytes 786440 | tf_op jit(solution)/shard_map/ppermute | solution.py:217
  7.9 69.4 %collective-permute-start.4 = (bf16[256,512]{1,0:T(8,128)(2,1)}, bf16[256,512]{1,0:T(8,128)(2,1)S(1)}, u32[]{:S(2)}, u32[]{:S(2)}) collective-permute-start(bf16[256,512]{1,0:T(8,128)(2,1)} %bitcast.85), channel_id=1, source_target_pairs={{0,16},{8,24},{16,0},{24,8},{1,17},{9,25},{17,1},{25,9},{2,18},{10... | collective-permute-start | bytes 786440 | tf_op jit(solution)/shard_map/ppermute | solution.py:217
  11.7 120.5 %collective-permute-start.18 = (bf16[1024,512]{0,1:T(8,128)(2,1)}, bf16[1024,512]{0,1:T(8,128)(2,1)}, u32[]{:S(2)}, u32[]{:S(2)}) collective-permute-start(bf16[1024,512]{0,1:T(8,128)(2,1)} %bitcast.11), channel_id=1, source_target_pairs={{0,1},{1,0},{2,3},{3,2},{4,5},{5,4},{6,7},{7,6},{8,9},{9,8},{10,11... | collective-permute-start | bytes 3145736 | tf_op jit(solution)/shard_map/ppermute | solution.py:217
  22.9 57.8 %collective-permute-start.5 = (bf16[256,512]{1,0:T(8,128)(2,1)S(1)}, bf16[256,512]{1,0:T(8,128)(2,1)}, u32[]{:S(2)}, u32[]{:S(2)}) collective-permute-start(bf16[256,512]{1,0:T(8,128)(2,1)S(1)} %bitcast.86), channel_id=1, source_target_pairs={{0,24},{8,16},{16,8},{24,0},{1,25},{9,17},{17,9},{25,1},{2,26},{10... | collective-permute-start | bytes 786440 | tf_op jit(solution)/shard_map/ppermute | solution.py:217
  76.2 25.3 %collective-permute-start = (bf16[16,128,128]{2,1,0:T(8,128)(2,1)}, bf16[16,128,128]{2,1,0:T(8,128)(2,1)S(1)}, u32[]{:S(2)}, u32[]{:S(2)}) collective-permute-start(bf16[16,128,128]{2,1,0:T(8,128)(2,1)} %get-tuple-element.9), channel_id=1, source_target_pairs={{0,2},{1,3},{2,0},{3,1},{4,6},{5,7},{6,4},{7,5},{8,10},{9,11},{10,... | collective-permute-start | bytes 1572872 | tf_op jit(solution)/shard_map/ppermute | solution.py:217
  76.2 38.5 %collective-permute-start.1 = (bf16[16,128,128]{2,1,0:T(8,128)(2,1)}, bf16[16,128,128]{2,1,0:T(8,128)(2,1)S(1)}, u32[]{:S(2)}, u32[]{:S(2)}) collective-permute-start(bf16[16,128,128]{2,1,0:T(8,128)(2,1)} %get-tuple-element.10), channel_id=1, source_target_pairs={{0,4},{1,5},{2,6},{3,7},{4,0},{5,1},{6,2},{7,3},{8,12},{9,13},{10,... | collective-permute-start | bytes 1572872 | tf_op jit(solution)/shard_map/ppermute | solution.py:217
  77.3 38.0 %collective-permute-start.2 = (bf16[16,128,128]{2,1,0:T(8,128)(2,1)}, bf16[16,128,128]{2,1,0:T(8,128)(2,1)S(1)}, u32[]{:S(2)}, u32[]{:S(2)}) collective-permute-start(bf16[16,128,128]{2,1,0:T(8,128)(2,1)} %get-tuple-element.11), channel_id=1, source_target_pairs={{0,6},{1,7},{2,4},{3,5},{4,2},{5,3},{6,0},{7,1},{8,14},{9,15},{10,... | collective-permute-start | bytes 1572872 | tf_op jit(solution)/shard_map/ppermute | solution.py:217
  80.7 37.7 %collective-permute-start.14 = (bf16[256,512]{1,0:T(8,128)(2,1)S(1)}, bf16[256,512]{1,0:T(8,128)(2,1)S(1)}, u32[]{:S(2)}, u32[]{:S(2)}) collective-permute-start(bf16[256,512]{1,0:T(8,128)(2,1)S(1)} %collective-permute-done.10.refs_15_), channel_id=1, source_target_pairs={{0,2},{1,3},{2,0},{3,1},{4,6},{5,7},{6,4},{7,5},{8,10},{9,11},{10,... | collective-permute-start | bytes 786440 | tf_op jit(solution)/shard_map/ppermute | solution.py:217
  101.5 18.5 %collective-permute-start.11 = (bf16[256,512]{1,0:T(8,128)(2,1)S(1)}, bf16[256,512]{1,0:T(8,128)(2,1)}, u32[]{:S(2)}, u32[]{:S(2)}) collective-permute-start(bf16[256,512]{1,0:T(8,128)(2,1)S(1)} %collective-permute-done.10.refs_15_), channel_id=1, source_target_pairs={{0,8},{8,0},{16,24},{24,16},{1,9},{9,1},{17,25},{25,17},{2,10},{10... | collective-permute-start | bytes 786440 | tf_op jit(solution)/shard_map/ppermute | solution.py:217
  114.8 13.5 %collective-permute-start.12 = (bf16[256,512]{1,0:T(8,128)(2,1)S(1)}, bf16[256,512]{1,0:T(8,128)(2,1)}, u32[]{:S(2)}, u32[]{:S(2)}) collective-permute-start(bf16[256,512]{1,0:T(8,128)(2,1)S(1)} %collective-permute-done.10.refs_15_), channel_id=1, source_target_pairs={{0,16},{8,24},{16,0},{24,8},{1,17},{9,25},{17,1},{25,9},{2,18},{10... | collective-permute-start | bytes 786440 | tf_op jit(solution)/shard_map/ppermute | solution.py:217
  115.3 14.5 %collective-permute-start.13 = (bf16[256,512]{1,0:T(8,128)(2,1)S(1)}, bf16[256,512]{1,0:T(8,128)(2,1)}, u32[]{:S(2)}, u32[]{:S(2)}) collective-permute-start(bf16[256,512]{1,0:T(8,128)(2,1)S(1)} %collective-permute-done.10.refs_15_), channel_id=1, source_target_pairs={{0,24},{8,16},{16,8},{24,0},{1,25},{9,17},{17,9},{25,1},{2,26},{10... | collective-permute-start | bytes 786440 | tf_op jit(solution)/shard_map/ppermute | solution.py:217
  119.1 13.0 %collective-permute-start.7 = (bf16[256,512]{1,0:T(8,128)(2,1)S(1)}, bf16[256,512]{1,0:T(8,128)(2,1)}, u32[]{:S(2)}, u32[]{:S(2)}) collective-permute-start(bf16[256,512]{1,0:T(8,128)(2,1)S(1)} %collective-permute-done.6.refs_11_), channel_id=1, source_target_pairs={{0,8},{8,0},{16,24},{24,16},{1,9},{9,1},{17,25},{25,17},{2,10},{10... | collective-permute-start | bytes 786440 | tf_op jit(solution)/shard_map/ppermute | solution.py:217
  120.0 21.7 %collective-permute-start.8 = (bf16[256,512]{1,0:T(8,128)(2,1)S(1)}, bf16[256,512]{1,0:T(8,128)(2,1)S(1)}, u32[]{:S(2)}, u32[]{:S(2)}) collective-permute-start(bf16[256,512]{1,0:T(8,128)(2,1)S(1)} %collective-permute-done.6.refs_11_), channel_id=1, source_target_pairs={{0,16},{8,24},{16,0},{24,8},{1,17},{9,25},{17,1},{25,9},{2,18},{10... | collective-permute-start | bytes 786440 | tf_op jit(solution)/shard_map/ppermute | solution.py:217
  128.3 13.4 %collective-permute-start.9 = (bf16[256,512]{1,0:T(8,128)(2,1)S(1)}, bf16[256,512]{1,0:T(8,128)(2,1)S(1)}, u32[]{:S(2)}, u32[]{:S(2)}) collective-permute-start(bf16[256,512]{1,0:T(8,128)(2,1)S(1)} %collective-permute-done.6.refs_11_), channel_id=1, source_target_pairs={{0,24},{8,16},{16,8},{24,0},{1,25},{9,17},{17,9},{25,1},{2,26},{10... | collective-permute-start | bytes 786440 | tf_op jit(solution)/shard_map/ppermute | solution.py:217
  129.8 12.6 %collective-permute-start.15 = (bf16[256,512]{1,0:T(8,128)(2,1)}, bf16[256,512]{1,0:T(8,128)(2,1)S(1)}, u32[]{:S(2)}, u32[]{:S(2)}) collective-permute-start(bf16[256,512]{1,0:T(8,128)(2,1)} %copy-done.3), channel_id=1, source_target_pairs={{0,8},{8,0},{16,24},{24,16},{1,9},{9,1},{17,25},{25,17},{2,10},{10... | collective-permute-start | bytes 786440 | tf_op jit(solution)/shard_map/ppermute | solution.py:217
  132.1 17.2 %collective-permute-start.16 = (bf16[256,512]{1,0:T(8,128)(2,1)}, bf16[256,512]{1,0:T(8,128)(2,1)S(1)}, u32[]{:S(2)}, u32[]{:S(2)}) collective-permute-start(bf16[256,512]{1,0:T(8,128)(2,1)} %copy-done.3), channel_id=1, source_target_pairs={{0,16},{8,24},{16,0},{24,8},{1,17},{9,25},{17,1},{25,9},{2,18},{10... | collective-permute-start | bytes 786440 | tf_op jit(solution)/shard_map/ppermute | solution.py:217
  132.1 17.2 %collective-permute-start.17 = (bf16[256,512]{1,0:T(8,128)(2,1)}, bf16[256,512]{1,0:T(8,128)(2,1)S(1)}, u32[]{:S(2)}, u32[]{:S(2)}) collective-permute-start(bf16[256,512]{1,0:T(8,128)(2,1)} %copy-done.3), channel_id=1, source_target_pairs={{0,24},{8,16},{16,8},{24,0},{1,25},{9,17},{17,9},{25,1},{2,26},{10... | collective-permute-start | bytes 786440 | tf_op jit(solution)/shard_map/ppermute | solution.py:217
  165.2 14.7 %collective-permute-start.23 = (bf16[4,256,512]{2,1,0:T(8,128)(2,1)S(1)}, bf16[4,256,512]{2,1,0:T(8,128)(2,1)S(1)}, u32[]{:S(2)}, u32[]{:S(2)}) collective-permute-start(bf16[4,256,512]{2,1,0:T(8,128)(2,1)S(1)} %get-tuple-element.15), channel_id=1, source_target_pairs={{0,1},{1,0},{2,3},{3,2},{4,5},{5,4},{6,7},{7,6},{8,9},{9,8},{10,11... | collective-permute-start | bytes 3145736 | tf_op jit(solution)/shard_map/ppermute | solution.py:217
  167.4 14.5 %collective-permute-start.20 = (bf16[2,64,512]{2,1,0:T(8,128)(2,1)S(1)}, bf16[2,64,512]{2,1,0:T(8,128)(2,1)S(1)}, u32[]{:S(2)}, u32[]{:S(2)}) collective-permute-start(bf16[2,64,512]{2,1,0:T(8,128)(2,1)S(1)} %get-tuple-element.27), channel_id=1, source_target_pairs={{0,2},{1,3},{2,0},{3,1},{4,6},{5,7},{6,4},{7,5},{8,10},{9,11},{10,... | collective-permute-start | bytes 393224 | tf_op jit(solution)/shard_map/ppermute | solution.py:217
  177.4 11.7 %collective-permute-start.21 = (bf16[2,64,512]{2,1,0:T(8,128)(2,1)S(1)}, bf16[2,64,512]{2,1,0:T(8,128)(2,1)S(1)}, u32[]{:S(2)}, u32[]{:S(2)}) collective-permute-start(bf16[2,64,512]{2,1,0:T(8,128)(2,1)S(1)} %get-tuple-element.29), channel_id=1, source_target_pairs={{0,4},{1,5},{2,6},{3,7},{4,0},{5,1},{6,2},{7,3},{8,12},{9,13},{10,... | collective-permute-start | bytes 393224 | tf_op jit(solution)/shard_map/ppermute | solution.py:217
  181.2 13.1 %collective-permute-start.25 = (bf16[256,512]{1,0:T(8,128)(2,1)S(1)}, bf16[256,512]{1,0:T(8,128)(2,1)S(1)}, u32[]{:S(2)}, u32[]{:S(2)}) collective-permute-start(bf16[256,512]{1,0:T(8,128)(2,1)S(1)} %get-tuple-element.26), channel_id=1, source_target_pairs={{0,16},{8,24},{16,0},{24,8},{1,17},{9,25},{17,1},{25,9},{2,18},{10... | collective-permute-start | bytes 786440 | tf_op jit(solution)/shard_map/ppermute | solution.py:217
  181.9 12.4 %collective-permute-start.26 = (bf16[256,512]{1,0:T(8,128)(2,1)S(1)}, bf16[256,512]{1,0:T(8,128)(2,1)S(1)}, u32[]{:S(2)}, u32[]{:S(2)}) collective-permute-start(bf16[256,512]{1,0:T(8,128)(2,1)S(1)} %get-tuple-element.25), channel_id=1, source_target_pairs={{0,24},{8,16},{16,8},{24,0},{1,25},{9,17},{17,9},{25,1},{2,26},{10... | collective-permute-start | bytes 786440 | tf_op jit(solution)/shard_map/ppermute | solution.py:217
  (14 other events, 330.1 us)

commit v2 on v0

v2 whole, which is shorter than its diff:
```python
import functools

import jax
import jax.numpy as jnp
from jax import lax
from jax.experimental import pallas as pl
from jax.experimental.pallas import tpu as pltpu
from jax.sharding import PartitionSpec as P

CAPACITY = 8
CORES = 2
SLOTS = CORES * CAPACITY
LIMIT = 32 * 1024 * 1024
HEAD = 5
SMEM = pl.BlockSpec(memory_space=pltpu.SMEM)
VMEM = pl.BlockSpec(memory_space=pltpu.VMEM)
ANY = pl.BlockSpec(memory_space=pl.ANY)


def payload_rows(edge, first, size):
    return size * edge + (SLOTS if first == 0 else 0)


def place_kernel(parts, chips, blocks, relations, *refs):
    given, place_ref, outs = refs[:2], refs[2], refs[3 : 3 + len(parts)]
    details, tiles_ref, order, count, sem = refs[3 + len(parts) :]
    copies = [
        pltpu.make_async_copy(given[0], details, sem.at[0]),
        pltpu.make_async_copy(given[1], tiles_ref, sem.at[1]),
    ]
    for copy in copies:
        copy.start()
    chip = place_ref[0]
    edge = tiles_ref.shape[-1]
    for j in range(chips):
        count[j] = 0
    for s in range(chips * SLOTS):
        order[s] = 0
    copies[0].wait()

    def rank(t, carry):
        j = (details[0, t] // CORES) ^ chip
        p = count[j]
        order[j * SLOTS + p] = t
        count[j] = p + 1
        return carry

    lax.fori_loop(0, details.shape[1], rank, 0)
    copies[1].wait()
    lane = lax.broadcasted_iota(jnp.int32, (SLOTS, edge), 1)
    row = lax.broadcasted_iota(jnp.int32, (SLOTS, edge), 0)
    for out, (j, first, size) in zip(outs, parts, strict=True):
        for p in range(size):
            tile = tiles_ref[order[j * SLOTS + first + p]]
            full = first + p < count[j]
            out[p * edge : (p + 1) * edge, :] = jnp.where(full, tile, jnp.zeros_like(tile))
        if first == 0:
            codes = jnp.zeros((SLOTS, edge), jnp.int32)
            for p in range(SLOTS):
                t = order[j * SLOTS + p]
                bucket = (details[0, t] % CORES) * relations + details[1, t]
                code = jnp.where(lane == 0, bucket * blocks + details[3, t], details[2, t])
                codes = jnp.where(row == p, code, codes)
            out[size * edge :, :] = codes.astype(jnp.float32).astype(jnp.bfloat16)


def place_tiles(parts, chips, blocks, relations, details, tiles, place):
    edge = tiles.shape[-1]
    shapes = [
        jax.ShapeDtypeStruct((payload_rows(edge, first, size), edge), tiles.dtype)
        for _, first, size in parts
    ]
    return pl.pallas_call(
        functools.partial(place_kernel, parts, chips, blocks, relations),
        out_shape=shapes,
        in_specs=[ANY] * 2 + [SMEM],
        out_specs=[VMEM] * len(shapes),
        scratch_shapes=[
            pltpu.SMEM(details.shape, jnp.int32),
            pltpu.VMEM(tiles.shape, tiles.dtype),
            pltpu.SMEM((chips * SLOTS,), jnp.int32),
            pltpu.SMEM((chips,), jnp.int32),
            pltpu.SemaphoreType.DMA((2,)),
        ],
        compiler_params=pltpu.CompilerParams(vmem_limit_bytes=LIMIT),
        cost_estimate=pl.CostEstimate(flops=0, bytes_accessed=4_000_000, transcendentals=0),
        name="place_tiles",
    )(details, tiles, place)


def tiles_kernel(parts, segments, chips, groups, blocks, relations, *refs):
    place_ref, refs = refs[0], refs[1:]
    buffers, refs = refs[: len(segments)], refs[len(segments) :]
    payloads, refs = refs[: len(parts)], refs[len(parts) :]
    near_ref, far_ref, grad_far, grad_own, summed = refs[:5]
    adjoint, total, vector, codes, sem, landed = refs[5:]
    chip, group, core = place_ref[0], place_ref[1], place_ref[2]
    piece = adjoint.shape[1] // groups
    moves = {j: [] for j in range(chips)}
    for buffer, (level, origins) in zip(buffers, segments, strict=True):
        for q, origin in enumerate(origins):
            start = jnp.where(core == 0, origin[0], origin[1]) ^ group
            start = pl.multiple_of(start * piece, piece)
            for n, j in enumerate(level):
                moves[j].append(
                    pltpu.make_async_copy(
                        buffer.at[pl.ds((q * len(level) + n) * piece, piece)],
                        adjoint.at[j, pl.ds(start, piece)],
                        landed.at[j, len(moves[j])],
                    )
                )
    for j in range(chips):
        for move in moves[j]:
            move.start()
    edge = payloads[0].shape[-1]
    copies = {}
    for payload, (j, first, size) in zip(payloads, parts, strict=True):
        if first == 0:
            vector[j] = payload[size * edge :, :].astype(jnp.float32).astype(jnp.int32)
            copies[j] = pltpu.make_async_copy(vector.at[j], codes.at[j], sem.at[j])
            copies[j].start()
    total[...] = jnp.zeros_like(total)

    def add(j, payload, slot, p):
        row = pl.multiple_of(codes[j, slot + p, 1] * edge, edge)
        partial = lax.dot_general(
            payload[pl.ds(pl.multiple_of(p * edge, edge), edge), :],
            adjoint[j, pl.ds(row, edge), :],
            (((0,), (0,)), ((), ())),
            preferred_element_type=jnp.float32,
        )
        total[codes[j, slot + p, 0]] += partial.astype(jnp.bfloat16).astype(jnp.float32)

    for payload, (j, first, size) in zip(payloads, parts, strict=True):
        if first == 0:
            copies[j].wait()
            for move in moves[j]:
                move.wait()
        unroll = next(u for u in range(min(size, 8), 0, -1) if size % u == 0)
        if unroll == 1:
            unroll = size

        def some(i, carry):
            for u in range(unroll):
                add(j, payload, first, i * unroll + u)
            return carry

        lax.fori_loop(0, size // unroll, some, 0)

    rows = blocks * edge
    share = near_ref.shape[0] // (chips * CORES)
    for r in range(relations):
        for h in range(CORES):
            part = total[pl.ds((h * relations + r) * blocks, blocks)].astype(jnp.bfloat16)
            summed[h, r] = part.reshape(rows, part.shape[-1])
        grad = jnp.dot(near_ref[...], summed[core, r], preferred_element_type=jnp.float32)
        grad += jnp.dot(far_ref[...], summed[1 - core, r], preferred_element_type=jnp.float32)
        for far in range(CORES):
            out = grad_far if far else grad_own
            for c in range(chips):
                for h in range(CORES):
                    slab = grad[(c * CORES + h) * share : (c * CORES + h + 1) * share]

                    @pl.when(h == (core ^ far))
                    def _():
                        out[chip ^ c, r] = slab.astype(out.dtype)


def tiles_and_grad(parts, segments, place, buffers, payloads, near, far, sizes):
    chips, groups, blocks, relations = sizes
    feature, rows = near.shape
    edge = rows // blocks
    shape = (chips, relations, feature // (chips * CORES), feature)
    return pl.pallas_call(
        functools.partial(tiles_kernel, parts, segments, chips, groups, blocks, relations),
        out_shape=[
            jax.ShapeDtypeStruct(shape, jnp.bfloat16),
            jax.ShapeDtypeStruct(shape, jnp.float32),
            jax.ShapeDtypeStruct((CORES, relations, rows, feature), jnp.bfloat16),
        ],
        in_specs=[SMEM] + [ANY] * len(buffers) + [VMEM] * (2 + len(payloads)),
        out_specs=[VMEM] * 3,
        scratch_shapes=[
            pltpu.VMEM((chips, rows, feature), jnp.bfloat16),
            pltpu.VMEM((CORES * relations * blocks, edge, feature), jnp.float32),
            pltpu.VMEM((chips, SLOTS, edge), jnp.int32),
            pltpu.SMEM((chips, SLOTS, edge), jnp.int32),
            pltpu.SemaphoreType.DMA((chips,)),
            pltpu.SemaphoreType.DMA((chips, groups)),
        ],
        compiler_params=pltpu.CompilerParams(vmem_limit_bytes=LIMIT),
        cost_estimate=pl.CostEstimate(flops=0, bytes_accessed=1_000_000, transcendentals=0),
        name="tiles_and_grad",
    )(place, *buffers, *payloads, near, far)


def rows_kernel(groups, relations, far, place_ref, summed, weights_ref, out):
    group, core = place_ref[1], place_ref[2]
    piece = summed.shape[2] // groups
    value = None
    for r in range(relations):
        term = lax.dot_general(
            summed[core ^ far, r],
            weights_ref[r],
            (((1,), (1,)), ((), ())),
            preferred_element_type=jnp.float32,
        )
        value = term if value is None else value + term
    for q in range(groups):
        out[group ^ q] = value[q * piece : (q + 1) * piece].astype(out.dtype)


def row_terms(place, summed, weights, groups, far, dtype):
    _, relations, rows, feature = summed.shape
    return pl.pallas_call(
        functools.partial(rows_kernel, groups, relations, far),
        out_shape=jax.ShapeDtypeStruct((groups, rows // groups, feature), dtype),
        in_specs=[SMEM, VMEM, VMEM],
        out_specs=VMEM,
        compiler_params=pltpu.CompilerParams(vmem_limit_bytes=LIMIT),
        cost_estimate=pl.CostEstimate(
            flops=4 * rows * feature * feature, bytes_accessed=4_000_000, transcendentals=0
        ),
        name="row_terms",
    )(place, summed, weights)


def plane_masks(groups, core):
    masks = [1 << i for i in range(groups.bit_length() - 1)]
    return masks[::-1] if core % CORES else masks


def after(value, *others):
    return lax.optimization_barrier((value, *others))[0]


def on_device(
    out_adjoint,
    layer_input,
    rel_weights,
    self_weight,
    tile_values,
    tile_rel,
    tile_target,
    tile_src,
    tile_dest,
):
    nodes = lax.axis_size("node")
    groups = lax.axis_size("rel")
    chips = nodes // CORES
    node = lax.axis_index("node")
    group = lax.axis_index("rel")
    chip, core = node // CORES, node % CORES
    edge = tile_values.shape[-1]
    rows = layer_input.shape[1]
    blocks = rows // edge
    relations = rel_weights.shape[0]

    def across(value, axis, size, mask):
        return lax.ppermute(value, axis, [(i, i ^ mask) for i in range(size)])

    def to_chip(value, j):
        return across(value, "node", nodes, CORES * j)

    def in_plane(value, step):
        pairs = []
        for g in range(groups):
            for n in range(nodes):
                mask = plane_masks(groups, n)[step]
                pairs.append((g * nodes + n, (g ^ mask) * nodes + n))
        return lax.ppermute(value, ("rel", "node"), pairs)

    own = out_adjoint[0]
    place = jnp.stack([chip, group, core]).astype(jnp.int32)
    details = jnp.stack([tile_dest[0, :, 0], tile_rel[0], tile_target[0], tile_src[0]])

    levels = [
        [j for j in range(chips) if j.bit_count() == count]
        for count in range(chips.bit_length())
    ]
    levels[:2] = [levels[0] + levels[1]]
    steps = groups.bit_length() - 1
    near = layer_input[0].T
    far = across(near, "node", nodes, 1)
    mid = chips // 2
    parts = [(0, 0, SLOTS), (mid, 0, HEAD), (mid, HEAD, SLOTS - HEAD)]
    parts = tuple(parts + [(j, 0, SLOTS) for j in range(chips - 1, 0, -1) if j != mid])
    placed = place_tiles(parts, chips, blocks, relations, details, tile_values[0], place)

    by_chip = {0: own}
    for j in levels[0][1:]:
        by_chip[j] = to_chip(own, j)
    head = to_chip(placed[1], mid)
    first = [head, far] + [by_chip[j] for j in levels[0][1:]]
    body = to_chip(after(placed[2], *first), mid)
    payloads = [placed[0], head, body]
    for value, (j, _, _) in list(zip(placed, parts, strict=True))[3:]:
        payloads.append(to_chip(after(value, *first, *([body] if j == 1 else [])), j))
    for level in levels[1:]:
        for j in level:
            bit = j & -j
            by_chip[j] = to_chip(after(by_chip[j ^ bit], *first), bit)

    buffers, segments = [], []
    for n, level in enumerate(levels):
        held = [by_chip[j] for j in level]
        held = held[0] if len(held) == 1 else jnp.concatenate(held)
        if n == 0:
            held = after(held, *first)
        held = [(held, ((0, 0),))]
        for step in range(steps):
            if n:
                merged = jnp.concatenate([value for value, _ in held]) if step else held[0][0]
                held = [(merged, sum((origins for _, origins in held), ()))]
            masks = [plane_masks(groups, c)[step] for c in range(CORES)]
            held = held + [
                (in_plane(value, step), tuple((a ^ masks[0], b ^ masks[1]) for a, b in origins))
                for value, origins in held
            ]
        for value, origins in held:
            buffers.append(value)
            segments.append((level, origins))
    sizes = (chips, groups, blocks, relations)
    grad_far, grad_own, summed = tiles_and_grad(
        parts, segments, place, buffers, payloads, near, far, sizes
    )
    grad_far = across(grad_far, "node", nodes, 1)
    rows_far = row_terms(place, summed, rel_weights, groups, 1, jnp.bfloat16)
    rows_far = across(rows_far, "node", nodes, 1)
    rows_own = row_terms(place, summed, rel_weights, groups, 0, jnp.float32)
    grad = grad_own + grad_far.astype(jnp.float32)
    others = [to_chip(grad[j].astype(jnp.bfloat16), j) for j in range(1, chips)]
    rel_weight_grad = grad[0]
    for other in others:
        rel_weight_grad += other.astype(jnp.float32)

    totals = rows_own + rows_far.astype(jnp.float32)
    others = [
        across(totals[m].astype(jnp.bfloat16), "rel", groups, m) for m in range(1, groups)
    ]
    d_source = totals[0] + jnp.einsum(
        "vj,ij->vi", own, self_weight, preferred_element_type=jnp.float32
    )
    for other in others:
        d_source += other.astype(jnp.float32)
    return rel_weight_grad, d_source.astype(jnp.bfloat16)[None]


def solution(mesh):
    return jax.shard_map(
        on_device,
        mesh=mesh,
        in_specs=(
            P("node", "rel", None),
            P("node", None, None),
            P("rel", None, None),
            P(),
            P("rel", "node", None, None),
            P("rel", "node"),
            P("rel", "node"),
            P("rel", "node"),
            P("rel", "node", None),
        ),
        out_specs=(P("rel", "node", None), P("node", "rel", None)),
        check_vma=False,
    )
```

time: 320 us -> 104 us (0.33)
  waiting for transfers between devices: 233 us -> 54.6 us
  local copies, waits for them, and re-layouts: 33.9 us -> 2.92 us
  matrix products: 26.1 us -> 0.32 us
  starting transfers between devices: 8.37 us -> 27.8 us
  Pallas kernels: 0 us -> 14.8 us
  between operations: 14.5 us -> 0.84 us
    all_to_all x2 -> x0, waiting for transfers between devices: 102 us -> none  [the longest x1 100 us: on_device(): lax.all_to_all(outgoing, 'node', split_axis=0, concat_axis=0, tiled=True)]
    unnamed x5 -> x0, waiting for transfers between devices: 57 us -> none
    ppermute x0 -> x21, waiting for transfers between devices: none -> 54.6 us  [the longest x16 54.6 us: across(): return lax.ppermute(value, axis, [(i, i ^ mask) for i in range(size)])]
    all_gather x2 -> x0, waiting for transfers between devices: 38.1 us -> none  [the longest x1 31.3 us: on_device(): adjoint = lax.all_gather(out_adjoint, 'rel', axis=1, tiled=True)[0]]
    reduce_scatter x1 -> x0, waiting for transfers between devices: 36 us -> none  [on_device(): lax.psum_scatter(jnp.einsum('rvj,rij->vi', aggregated, rel_weights, prefe...]
    ppermute x0 -> x21, starting transfers between devices: none -> 27.8 us  [the longest x16 20.9 us: across(): return lax.ppermute(value, axis, [(i, i ^ mask) for i in range(size)])]
    dot_general x6 -> x1, matrix products: 26.1 us -> 0.32 us  [on_device(): jnp.einsum('vj,ij->vi', own, self_weight, preferred_element_type=jnp.floa...]
    pallas_call x0 -> x4, Pallas kernels: none -> 14.8 us  [the longest x1 8.4 us: tiles_and_grad(): pl.pallas_call(functools.partial(tiles_kernel, parts, segments, chips, gr...]
  transfers between devices with their start and end apart: 6 -> 21, of which waited for: 6 -> 11; matrix products, arithmetic and copies ran while one was open for 5% -> 2% of each run, Pallas kernels for 0% -> 6%
where the time goes in v2:
time: 104 us
  waiting for transfers between devices  54.6 us (52%)
  starting transfers between devices  27.8 us (27%)
  Pallas kernels  14.8 us (14%)
  local copies, waits for them, and re-layouts  2.92 us (3%)
  other arithmetic  2.52 us (2%)
    ppermute x16, waiting for transfers between devices, across(): return lax.ppermute(value, axis, [(i, i ^ mask) for i in range(size)])  54.6 us
    ppermute x16, starting transfers between devices, across(): return lax.ppermute(value, axis, [(i, i ^ mask) for i in range(size)])  20.9 us
    pallas_call x1, Pallas kernels, tiles_and_grad(): pl.pallas_call(functools.partial(tiles_kernel, parts, segments, chips, gr...  8.4 us
    ppermute x5, starting transfers between devices, in_plane(): return lax.ppermute(value, ('rel', 'node'), pairs)  6.96 us
    pallas_call x2, Pallas kernels, row_terms(): pl.pallas_call(functools.partial(rows_kernel, groups, relations, far), ou...  3.63 us
    unnamed x18, local copies, waits for them, and re-layouts  2.82 us
    pallas_call x1, Pallas kernels, place_tiles(): pl.pallas_call(functools.partial(place_kernel, parts, chips, blocks, rela...  2.73 us
  transfers between devices with their start and end apart: 21, of which 11 were waited for; matrix products, arithmetic and copies ran while one was open for 2% of the time, Pallas kernels for 6%

profile of v2, /device:TPU:0, one launch (start us, length us, event | category | flops | bytes accessed | tf_op | source)
XLA Modules:
  0.0 103.8 jit_solution(8631550873377625411)
XLA Ops:
  0.7 1.5 %copy.11 = bf16[1,1024,512]{1,2,0:T(8,128)(2,1)S(1)} copy(bf16[1,1024,512]{2,1,0:T(8,128)(2,1)} %param.10) | data formatting | bytes 2097152 | tf_op args[1]
  2.8 2.7 %collective-permute-start = (bf16[256,512]{1,0:T(8,128)(2,1)S(1)}, bf16[256,512]{1,0:T(8,128)(2,1)S(1)}, u32[]{:S(2)}, u32[]{:S(2)}) collective-permute-start(bf16[256,512]{1,0:T(8,128)(2,1)S(1)} %bitcast.51), channel_id=1, source_target_pairs={{0,2},{1,3},{2,0},{3,1},{4,6},{5,7},{6,4},{7,5},{8,10},{9,11},{10,... | collective-permute-start | bytes 786440 | tf_op jit(solution)/shard_map/ppermute | solution.py:260
  5.4 2.6 %collective-permute-start.1 = (bf16[256,512]{1,0:T(8,128)(2,1)S(1)}, bf16[256,512]{1,0:T(8,128)(2,1)S(1)}, u32[]{:S(2)}, u32[]{:S(2)}) collective-permute-start(bf16[256,512]{1,0:T(8,128)(2,1)S(1)} %bitcast.52), channel_id=1, source_target_pairs={{0,4},{1,5},{2,6},{3,7},{4,0},{5,1},{6,2},{7,3},{8,12},{9,13},{10,... | collective-permute-start | bytes 786440 | tf_op jit(solution)/shard_map/ppermute | solution.py:260
  9.4 2.7 %place_tiles.1 = (bf16[2064,128]{1,0:T(8,128)(2,1)S(1)}, bf16[656,128]{1,0:T(8,128)(2,1)S(1)}, bf16[1408,128]{1,0:T(8,128)(2,1)S(1)}, bf16[2064,128]{1,0:T(8,128)(2,1)S(1)}, bf16[2064,128]{1,0:T(8,128)(2,1)S(1)}) custom-call(s32[4,32]{1,0:T(4,128)S(1)} %pad_add_fusion.refs_0_, bf16[32,128,128]{2,1,0:T(8,128)(2,1)S(1)} %bitcast.50, ...), custom_call_target="tpu_custom_call" | custom-call | bytes 4000000 | tf_op jit(solution)/shard_map/place_tiles/pallas_call | solution.py:73
  12.5 5.3 %collective-permute-done = bf16[256,512]{1,0:T(8,128)(2,1)S(1)} collective-permute-done((bf16[256,512]{1,0:T(8,128)(2,1)S(1)}, bf16[256,512]{1,0:T(8,128)(2,1)S(1)}, u32[]{:S(2)}, u32[]{:S(2)}) %collective-permute-start) | collective-permute-done | bytes 262176 | tf_op jit(solution)/shard_map/ppermute | solution.py:260
  17.8 6.2 %collective-permute-done.1 = bf16[256,512]{1,0:T(8,128)(2,1)S(1)} collective-permute-done((bf16[256,512]{1,0:T(8,128)(2,1)S(1)}, bf16[256,512]{1,0:T(8,128)(2,1)S(1)}, u32[]{:S(2)}, u32[]{:S(2)}) %collective-permute-start.1) | collective-permute-done | bytes 262176 | tf_op jit(solution)/shard_map/ppermute | solution.py:260
  24.1 3.5 %collective-permute-done.2.refs_8_ = bf16[656,128]{1,0:T(8,128)(2,1)S(1)} collective-permute-done((bf16[656,128]{1,0:T(8,128)(2,1)S(1)}, bf16[656,128]{1,0:T(8,128)(2,1)S(1)}, u32[]{:S(2)}, u32[]{:S(2)}) %collective-permute-start.2) | collective-permute-done | bytes 167968 | tf_op jit(solution)/shard_map/ppermute | solution.py:260
  27.6 1.5 %collective-permute-start.4 = (bf16[768,512]{1,0:T(8,128)(2,1)S(1)}, bf16[768,512]{1,0:T(8,128)(2,1)S(1)}, u32[]{:S(2)}, u32[]{:S(2)}) collective-permute-start(bf16[768,512]{1,0:T(8,128)(2,1)S(1)} %pad_maximum_fusion.refs_1_), channel_id=1, source_target_pairs={{0,8},{1,17},{2,10},{3,19},{4,12},{5,21},{6,14},{7,23},{8,0},{9,25... | collective-permute-start | bytes 2359304 | tf_op jit(solution)/shard_map/ppermute | solution.py:271
  29.1 3.0 %collective-permute-start.10 = (bf16[1408,128]{1,0:T(8,128)(2,1)S(1)}, bf16[1408,128]{1,0:T(8,128)(2,1)S(1)}, u32[]{:S(2)}, u32[]{:S(2)}) collective-permute-start(bf16[1408,128]{1,0:T(8,128)(2,1)S(1)} %get-tuple-element.20), channel_id=1, source_target_pairs={{0,4},{1,5},{2,6},{3,7},{4,0},{5,1},{6,2},{7,3},{8,12},{9,13},{10,... | collective-permute-start | bytes 1081352 | tf_op jit(solution)/shard_map/ppermute | solution.py:260
  32.1 9.8 %collective-permute-done.7 = bf16[256,512]{1,0:T(8,128)(2,1)S(1)} collective-permute-done((bf16[256,512]{1,0:T(8,128)(2,1)S(1)}, bf16[256,512]{1,0:T(8,128)(2,1)S(1)}, u32[]{:S(2)}, u32[]{:S(2)}) %collective-permute-start.7) | collective-permute-done | bytes 262176 | tf_op jit(solution)/shard_map/ppermute | solution.py:260
  43.8 1.5 %collective-permute-start.6 = (bf16[768,512]{1,0:T(8,128)(2,1)S(1)}, bf16[768,512]{1,0:T(8,128)(2,1)S(1)}, u32[]{:S(2)}, u32[]{:S(2)}) collective-permute-start(bf16[768,512]{1,0:T(8,128)(2,1)S(1)} %collective-permute-done.4.refs_2_), channel_id=1, source_target_pairs={{0,16},{1,9},{2,18},{3,11},{4,20},{5,13},{6,22},{7,15},{8,24},{9,1... | collective-permute-start | bytes 2359304 | tf_op jit(solution)/shard_map/ppermute | solution.py:271
  45.4 2.0 %collective-permute-start.11 = (bf16[2064,128]{1,0:T(8,128)(2,1)S(1)}, bf16[2064,128]{1,0:T(8,128)(2,1)S(1)}, u32[]{:S(2)}, u32[]{:S(2)}) collective-permute-start(bf16[2064,128]{1,0:T(8,128)(2,1)S(1)} %get-tuple-element.22), channel_id=1, source_target_pairs={{0,6},{1,7},{2,4},{3,5},{4,2},{5,3},{6,0},{7,1},{8,14},{9,15},{10,... | collective-permute-start | bytes 1585160 | tf_op jit(solution)/shard_map/ppermute | solution.py:260
  47.4 11.4 %collective-permute-done.10.refs_9_ = bf16[1408,128]{1,0:T(8,128)(2,1)S(1)} collective-permute-done((bf16[1408,128]{1,0:T(8,128)(2,1)S(1)}, bf16[1408,128]{1,0:T(8,128)(2,1)S(1)}, u32[]{:S(2)}, u32[]{:S(2)}) %collective-permute-start.10) | collective-permute-done | bytes 360480 | tf_op jit(solution)/shard_map/ppermute | solution.py:260
  58.8 2.0 %collective-permute-start.9 = (bf16[512,512]{1,0:T(8,128)(2,1)S(1)}, bf16[512,512]{1,0:T(8,128)(2,1)S(1)}, u32[]{:S(2)}, u32[]{:S(2)}) collective-permute-start(bf16[512,512]{1,0:T(8,128)(2,1)S(1)} %constant_dynamic-update-slice_fusion.refs_5_), channel_id=1, source_target_pairs={{0,16},{1,9},{2,18},{3,11},{4,20},{5,13},{6,22},{7,15},{8,24},{9,1... | collective-permute-start | bytes 1572872 | tf_op jit(solution)/shard_map/ppermute | solution.py:271
  62.2 8.8 %collective-permute-done.12.refs_11_ = bf16[2064,128]{1,0:T(8,128)(2,1)S(1)} collective-permute-done((bf16[2064,128]{1,0:T(8,128)(2,1)S(1)}, bf16[2064,128]{1,0:T(8,128)(2,1)S(1)}, u32[]{:S(2)}, u32[]{:S(2)}) %collective-permute-start.12) | collective-permute-done | bytes 528416 | tf_op jit(solution)/shard_map/ppermute | solution.py:260
  71.0 8.4 %tiles_and_grad.1 = (bf16[4,2,64,512]{3,2,1,0:T(8,128)(2,1)S(1)}, f32[4,2,64,512]{3,2,1,0:T(8,128)S(1)}, bf16[2,2,1024,512]{3,2,1,0:T(8,128)(2,1)S(1)}) custom-call(s32[3]{0:T(128)S(1)} %pad_add_fusion.1.refs_2_.refs_0_.place_ref, bf16[768,512]{1,0:T(8,128)(2,1)S(1)} %pad_maximum_fusion.refs_1_, bf16[768,512]{1,0:T(8,128)(2,1)S(1)} %collective-permute-done.4.refs_2_, ...), custom_call_target="tpu_custom_call" | custom-call | bytes 1000000 | tf_op jit(solution)/shard_map/tiles_and_grad/pallas_call | solution.py:174
  79.5 1.8 %row_terms.3 = bf16[4,256,512]{2,1,0:T(8,128)(2,1)S(1)} custom-call(s32[3]{0:T(128)S(1)} %pad_add_fusion.1.refs_2_.refs_0_.place_ref, bf16[2,2,1024,512]{3,2,1,0:T(8,128)(2,1)S(1)} %get-tuple-element.27.summed, bf16[2,512,512]{2,1,0:T(8,128)(2,1)S(1)} %copy-done.1), custom_call_target="tpu_custom_call" | custom-call | flops 1073741824 | bytes 4000000 | tf_op jit(solution)/shard_map/row_terms/pallas_call | solution.py:215
  81.9 1.8 %row_terms.2 = f32[4,256,512]{2,1,0:T(8,128)S(1)} custom-call(s32[3]{0:T(128)S(1)} %pad_add_fusion.1.refs_2_.refs_0_.place_ref, bf16[2,2,1024,512]{3,2,1,0:T(8,128)(2,1)S(1)} %get-tuple-element.27.summed, bf16[2,512,512]{2,1,0:T(8,128)(2,1)S(1)} %copy-done.1), custom_call_target="tpu_custom_call" | custom-call | flops 1073741824 | bytes 4000000 | tf_op jit(solution)/shard_map/row_terms/pallas_call | solution.py:215
  84.2 2.4 %collective-permute-start.15 = (bf16[2,64,512]{2,1,0:T(8,128)(2,1)S(1)}, bf16[2,64,512]{2,1,0:T(8,128)(2,1)S(1)}, u32[]{:S(2)}, u32[]{:S(2)}) collective-permute-start(bf16[2,64,512]{2,1,0:T(8,128)(2,1)S(1)} %get-tuple-element.37), channel_id=1, source_target_pairs={{0,4},{1,5},{2,6},{3,7},{4,0},{5,1},{6,2},{7,3},{8,12},{9,13},{10,... | collective-permute-start | bytes 393224 | tf_op jit(solution)/shard_map/ppermute | solution.py:260
  86.6 1.8 %collective-permute-start.16 = (bf16[2,64,512]{2,1,0:T(8,128)(2,1)S(1)}, bf16[2,64,512]{2,1,0:T(8,128)(2,1)S(1)}, u32[]{:S(2)}, u32[]{:S(2)}) collective-permute-start(bf16[2,64,512]{2,1,0:T(8,128)(2,1)S(1)} %get-tuple-element.36), channel_id=1, source_target_pairs={{0,6},{1,7},{2,4},{3,5},{4,2},{5,3},{6,0},{7,1},{8,14},{9,15},{10,... | collective-permute-start | bytes 393224 | tf_op jit(solution)/shard_map/ppermute | solution.py:260
  90.2 1.6 %collective-permute-start.19 = (bf16[256,512]{1,0:T(8,128)(2,1)S(1)}, bf16[256,512]{1,0:T(8,128)(2,1)S(1)}, u32[]{:S(2)}, u32[]{:S(2)}) collective-permute-start(bf16[256,512]{1,0:T(8,128)(2,1)S(1)} %get-tuple-element.34), channel_id=1, source_target_pairs={{0,16},{8,24},{16,0},{24,8},{1,17},{9,25},{17,1},{25,9},{2,18},{10... | collective-permute-start | bytes 786440 | tf_op jit(solution)/shard_map/ppermute | solution.py:260
  91.8 1.8 %collective-permute-start.20 = (bf16[256,512]{1,0:T(8,128)(2,1)S(1)}, bf16[256,512]{1,0:T(8,128)(2,1)S(1)}, u32[]{:S(2)}, u32[]{:S(2)}) collective-permute-start(bf16[256,512]{1,0:T(8,128)(2,1)S(1)} %get-tuple-element.33), channel_id=1, source_target_pairs={{0,24},{8,16},{16,8},{24,0},{1,25},{9,17},{17,9},{25,1},{2,26},{10... | collective-permute-start | bytes 786440 | tf_op jit(solution)/shard_map/ppermute | solution.py:260
  93.9 3.2 %collective-permute-done.15 = bf16[2,64,512]{2,1,0:T(8,128)(2,1)S(1)} collective-permute-done((bf16[2,64,512]{2,1,0:T(8,128)(2,1)S(1)}, bf16[2,64,512]{2,1,0:T(8,128)(2,1)S(1)}, u32[]{:S(2)}, u32[]{:S(2)}) %collective-permute-start.15) | collective-permute-done | bytes 131104 | tf_op jit(solution)/shard_map/ppermute | solution.py:260
  98.3 3.7 %collective-permute-done.19 = bf16[256,512]{1,0:T(8,128)(2,1)S(1)} collective-permute-done((bf16[256,512]{1,0:T(8,128)(2,1)S(1)}, bf16[256,512]{1,0:T(8,128)(2,1)S(1)}, u32[]{:S(2)}, u32[]{:S(2)}) %collective-permute-start.19) | collective-permute-done | bytes 262176 | tf_op jit(solution)/shard_map/ppermute | solution.py:260
  (51 shorter events, 11.8 us)
Async XLA Ops:
  0.6 92.9 %copy-start = (bf16[512,512]{1,0:T(8,128)(2,1)S(1)}, bf16[512,512]{1,0:T(8,128)(2,1)}, u32[]{:S(2)}) copy-start(bf16[512,512]{1,0:T(8,128)(2,1)} %param.12) | copy-start | bytes 1572868
  0.7 7.4 %copy-start.7 = (s32[1,32,1]{1,2,0:T(1,128)S(1)}, s32[1,32,1]{1,2,0:T(1,128)}, u32[]{:S(2)}) copy-start(s32[1,32,1]{1,2,0:T(1,128)} %param.17) | copy-start | bytes 388
  2.3 25.3 %collective-permute-start.3 = (bf16[512,1024]{1,0:T(8,128)(2,1)S(1)}, bf16[512,1024]{1,0:T(8,128)(2,1)S(1)}, u32[]{:S(2)}, u32[]{:S(2)}) collective-permute-start(bf16[512,1024]{1,0:T(8,128)(2,1)S(1)} %bitcast.48), channel_id=1, source_target_pairs={{0,1},{1,0},{2,3},{3,2},{4,5},{5,4},{6,7},{7,6},{8,9},{9,8},{10,11... | collective-permute-start | bytes 3145736 | tf_op jit(solution)/shard_map/ppermute | solution.py:260
  2.8 15.1 %collective-permute-start = (bf16[256,512]{1,0:T(8,128)(2,1)S(1)}, bf16[256,512]{1,0:T(8,128)(2,1)S(1)}, u32[]{:S(2)}, u32[]{:S(2)}) collective-permute-start(bf16[256,512]{1,0:T(8,128)(2,1)S(1)} %bitcast.51), channel_id=1, source_target_pairs={{0,2},{1,3},{2,0},{3,1},{4,6},{5,7},{6,4},{7,5},{8,10},{9,11},{10,... | collective-permute-start | bytes 786440 | tf_op jit(solution)/shard_map/ppermute | solution.py:260
  5.4 18.6 %collective-permute-start.1 = (bf16[256,512]{1,0:T(8,128)(2,1)S(1)}, bf16[256,512]{1,0:T(8,128)(2,1)S(1)}, u32[]{:S(2)}, u32[]{:S(2)}) collective-permute-start(bf16[256,512]{1,0:T(8,128)(2,1)S(1)} %bitcast.52), channel_id=1, source_target_pairs={{0,4},{1,5},{2,6},{3,7},{4,0},{5,1},{6,2},{7,3},{8,12},{9,13},{10,... | collective-permute-start | bytes 786440 | tf_op jit(solution)/shard_map/ppermute | solution.py:260
  12.1 15.5 %collective-permute-start.2 = (bf16[656,128]{1,0:T(8,128)(2,1)S(1)}, bf16[656,128]{1,0:T(8,128)(2,1)S(1)}, u32[]{:S(2)}, u32[]{:S(2)}) collective-permute-start(bf16[656,128]{1,0:T(8,128)(2,1)S(1)} %get-tuple-element.15), channel_id=1, source_target_pairs={{0,4},{1,5},{2,6},{3,7},{4,0},{5,1},{6,2},{7,3},{8,12},{9,13},{10,... | collective-permute-start | bytes 503816 | tf_op jit(solution)/shard_map/ppermute | solution.py:260
  27.6 16.3 %collective-permute-start.4 = (bf16[768,512]{1,0:T(8,128)(2,1)S(1)}, bf16[768,512]{1,0:T(8,128)(2,1)S(1)}, u32[]{:S(2)}, u32[]{:S(2)}) collective-permute-start(bf16[768,512]{1,0:T(8,128)(2,1)S(1)} %pad_maximum_fusion.refs_1_), channel_id=1, source_target_pairs={{0,8},{1,17},{2,10},{3,19},{4,12},{5,21},{6,14},{7,23},{8,0},{9,25... | collective-permute-start | bytes 2359304 | tf_op jit(solution)/shard_map/ppermute | solution.py:271
  29.1 12.8 %collective-permute-start.7 = (bf16[256,512]{1,0:T(8,128)(2,1)S(1)}, bf16[256,512]{1,0:T(8,128)(2,1)S(1)}, u32[]{:S(2)}, u32[]{:S(2)}) collective-permute-start(bf16[256,512]{1,0:T(8,128)(2,1)S(1)} %collective-permute-done.1), channel_id=1, source_target_pairs={{0,2},{1,3},{2,0},{3,1},{4,6},{5,7},{6,4},{7,5},{8,10},{9,11},{10,... | collective-permute-start | bytes 786440 | tf_op jit(solution)/shard_map/ppermute | solution.py:260
  29.1 29.7 %collective-permute-start.10 = (bf16[1408,128]{1,0:T(8,128)(2,1)S(1)}, bf16[1408,128]{1,0:T(8,128)(2,1)S(1)}, u32[]{:S(2)}, u32[]{:S(2)}) collective-permute-start(bf16[1408,128]{1,0:T(8,128)(2,1)S(1)} %get-tuple-element.20), channel_id=1, source_target_pairs={{0,4},{1,5},{2,6},{3,7},{4,0},{5,1},{6,2},{7,3},{8,12},{9,13},{10,... | collective-permute-start | bytes 1081352 | tf_op jit(solution)/shard_map/ppermute | solution.py:260
  41.8 17.0 %collective-permute-start.8 = (bf16[256,512]{1,0:T(8,128)(2,1)S(1)}, bf16[256,512]{1,0:T(8,128)(2,1)S(1)}, u32[]{:S(2)}, u32[]{:S(2)}) collective-permute-start(bf16[256,512]{1,0:T(8,128)(2,1)S(1)} %collective-permute-done.7), channel_id=1, source_target_pairs={{0,8},{1,17},{2,10},{3,19},{4,12},{5,21},{6,14},{7,23},{8,0},{9,25... | collective-permute-start | bytes 786440 | tf_op jit(solution)/shard_map/ppermute | solution.py:271
  43.3 18.8 %collective-permute-start.5 = (bf16[768,512]{1,0:T(8,128)(2,1)S(1)}, bf16[768,512]{1,0:T(8,128)(2,1)S(1)}, u32[]{:S(2)}, u32[]{:S(2)}) collective-permute-start(bf16[768,512]{1,0:T(8,128)(2,1)S(1)} %pad_maximum_fusion.refs_1_), channel_id=1, source_target_pairs={{0,16},{1,9},{2,18},{3,11},{4,20},{5,13},{6,22},{7,15},{8,24},{9,1... | collective-permute-start | bytes 2359304 | tf_op jit(solution)/shard_map/ppermute | solution.py:271
  43.8 27.1 %collective-permute-start.6 = (bf16[768,512]{1,0:T(8,128)(2,1)S(1)}, bf16[768,512]{1,0:T(8,128)(2,1)S(1)}, u32[]{:S(2)}, u32[]{:S(2)}) collective-permute-start(bf16[768,512]{1,0:T(8,128)(2,1)S(1)} %collective-permute-done.4.refs_2_), channel_id=1, source_target_pairs={{0,16},{1,9},{2,18},{3,11},{4,20},{5,13},{6,22},{7,15},{8,24},{9,1... | collective-permute-start | bytes 2359304 | tf_op jit(solution)/shard_map/ppermute | solution.py:271
  45.4 16.8 %collective-permute-start.11 = (bf16[2064,128]{1,0:T(8,128)(2,1)S(1)}, bf16[2064,128]{1,0:T(8,128)(2,1)S(1)}, u32[]{:S(2)}, u32[]{:S(2)}) collective-permute-start(bf16[2064,128]{1,0:T(8,128)(2,1)S(1)} %get-tuple-element.22), channel_id=1, source_target_pairs={{0,6},{1,7},{2,4},{3,5},{4,2},{5,3},{6,0},{7,1},{8,14},{9,15},{10,... | collective-permute-start | bytes 1585160 | tf_op jit(solution)/shard_map/ppermute | solution.py:260
  58.8 12.2 %collective-permute-start.12 = (bf16[2064,128]{1,0:T(8,128)(2,1)S(1)}, bf16[2064,128]{1,0:T(8,128)(2,1)S(1)}, u32[]{:S(2)}, u32[]{:S(2)}) collective-permute-start(bf16[2064,128]{1,0:T(8,128)(2,1)S(1)} %get-tuple-element.24), channel_id=1, source_target_pairs={{0,2},{1,3},{2,0},{3,1},{4,6},{5,7},{6,4},{7,5},{8,10},{9,11},{10,... | collective-permute-start | bytes 1585160 | tf_op jit(solution)/shard_map/ppermute | solution.py:260
  58.8 12.1 %collective-permute-start.9 = (bf16[512,512]{1,0:T(8,128)(2,1)S(1)}, bf16[512,512]{1,0:T(8,128)(2,1)S(1)}, u32[]{:S(2)}, u32[]{:S(2)}) collective-permute-start(bf16[512,512]{1,0:T(8,128)(2,1)S(1)} %constant_dynamic-update-slice_fusion.refs_5_), channel_id=1, source_target_pairs={{0,16},{1,9},{2,18},{3,11},{4,20},{5,13},{6,22},{7,15},{8,24},{9,1... | collective-permute-start | bytes 1572872 | tf_op jit(solution)/shard_map/ppermute | solution.py:271
  71.0 8.5 %copy-start.1 = (bf16[2,512,512]{2,1,0:T(8,128)(2,1)S(1)}, bf16[2,512,512]{2,1,0:T(8,128)(2,1)}, u32[]{:S(2)}) copy-start(bf16[2,512,512]{2,1,0:T(8,128)(2,1)} %weights_ref.3) | copy-start | bytes 3145732
  79.4 4.3 %collective-permute-start.13 = (bf16[4,2,64,512]{3,2,1,0:T(8,128)(2,1)S(1)}, bf16[4,2,64,512]{3,2,1,0:T(8,128)(2,1)S(1)}, u32[]{:S(2)}, u32[]{:S(2)}) collective-permute-start(bf16[4,2,64,512]{3,2,1,0:T(8,128)(2,1)S(1)} %get-tuple-element.26), channel_id=1, source_target_pairs={{0,1},{1,0},{2,3},{3,2},{4,5},{5,4},{6,7},{7,6},{8,9},{9,8},{10,11... | collective-permute-start | bytes 1572872 | tf_op jit(solution)/shard_map/ppermute | solution.py:260
  81.3 7.1 %collective-permute-start.17 = (bf16[4,256,512]{2,1,0:T(8,128)(2,1)S(1)}, bf16[4,256,512]{2,1,0:T(8,128)(2,1)S(1)}, u32[]{:S(2)}, u32[]{:S(2)}) collective-permute-start(bf16[4,256,512]{2,1,0:T(8,128)(2,1)S(1)} %row_terms.3), channel_id=1, source_target_pairs={{0,1},{1,0},{2,3},{3,2},{4,5},{5,4},{6,7},{7,6},{8,9},{9,8},{10,11... | collective-permute-start | bytes 3145736 | tf_op jit(solution)/shard_map/ppermute | solution.py:260
  84.0 7.8 %collective-permute-start.14 = (bf16[2,64,512]{2,1,0:T(8,128)(2,1)S(1)}, bf16[2,64,512]{2,1,0:T(8,128)(2,1)S(1)}, u32[]{:S(2)}, u32[]{:S(2)}) collective-permute-start(bf16[2,64,512]{2,1,0:T(8,128)(2,1)S(1)} %get-tuple-element.35), channel_id=1, source_target_pairs={{0,2},{1,3},{2,0},{3,1},{4,6},{5,7},{6,4},{7,5},{8,10},{9,11},{10,... | collective-permute-start | bytes 393224 | tf_op jit(solution)/shard_map/ppermute | solution.py:260
  84.2 12.9 %collective-permute-start.15 = (bf16[2,64,512]{2,1,0:T(8,128)(2,1)S(1)}, bf16[2,64,512]{2,1,0:T(8,128)(2,1)S(1)}, u32[]{:S(2)}, u32[]{:S(2)}) collective-permute-start(bf16[2,64,512]{2,1,0:T(8,128)(2,1)S(1)} %get-tuple-element.37), channel_id=1, source_target_pairs={{0,4},{1,5},{2,6},{3,7},{4,0},{5,1},{6,2},{7,3},{8,12},{9,13},{10,... | collective-permute-start | bytes 393224 | tf_op jit(solution)/shard_map/ppermute | solution.py:260
  86.6 10.5 %collective-permute-start.16 = (bf16[2,64,512]{2,1,0:T(8,128)(2,1)S(1)}, bf16[2,64,512]{2,1,0:T(8,128)(2,1)S(1)}, u32[]{:S(2)}, u32[]{:S(2)}) collective-permute-start(bf16[2,64,512]{2,1,0:T(8,128)(2,1)S(1)} %get-tuple-element.36), channel_id=1, source_target_pairs={{0,6},{1,7},{2,4},{3,5},{4,2},{5,3},{6,0},{7,1},{8,14},{9,15},{10,... | collective-permute-start | bytes 393224 | tf_op jit(solution)/shard_map/ppermute | solution.py:260
  89.0 9.3 %collective-permute-start.18 = (bf16[256,512]{1,0:T(8,128)(2,1)S(1)}, bf16[256,512]{1,0:T(8,128)(2,1)S(1)}, u32[]{:S(2)}, u32[]{:S(2)}) collective-permute-start(bf16[256,512]{1,0:T(8,128)(2,1)S(1)} %get-tuple-element.32), channel_id=1, source_target_pairs={{0,8},{8,0},{16,24},{24,16},{1,9},{9,1},{17,25},{25,17},{2,10},{10... | collective-permute-start | bytes 786440 | tf_op jit(solution)/shard_map/ppermute | solution.py:260
  90.2 11.9 %collective-permute-start.19 = (bf16[256,512]{1,0:T(8,128)(2,1)S(1)}, bf16[256,512]{1,0:T(8,128)(2,1)S(1)}, u32[]{:S(2)}, u32[]{:S(2)}) collective-permute-start(bf16[256,512]{1,0:T(8,128)(2,1)S(1)} %get-tuple-element.34), channel_id=1, source_target_pairs={{0,16},{8,24},{16,0},{24,8},{1,17},{9,25},{17,1},{25,9},{2,18},{10... | collective-permute-start | bytes 786440 | tf_op jit(solution)/shard_map/ppermute | solution.py:260
  91.8 11.1 %collective-permute-start.20 = (bf16[256,512]{1,0:T(8,128)(2,1)S(1)}, bf16[256,512]{1,0:T(8,128)(2,1)S(1)}, u32[]{:S(2)}, u32[]{:S(2)}) collective-permute-start(bf16[256,512]{1,0:T(8,128)(2,1)S(1)} %get-tuple-element.33), channel_id=1, source_target_pairs={{0,24},{8,16},{16,8},{24,0},{1,25},{9,17},{17,9},{25,1},{2,26},{10... | collective-permute-start | bytes 786440 | tf_op jit(solution)/shard_map/ppermute | solution.py:260
  (5 other events, 25.6 us)

commit v3 on v2

--- a/solution.py
+++ b/solution.py
@@ -10,7 +10,7 @@
 CAPACITY = 8
 CORES = 2
 SLOTS = CORES * CAPACITY
-LIMIT = 32 * 1024 * 1024
+LIMIT = 24 * 1024 * 1024
 HEAD = 5
 SMEM = pl.BlockSpec(memory_space=pltpu.SMEM)
 VMEM = pl.BlockSpec(memory_space=pltpu.VMEM)
@@ -88,15 +88,22 @@
     )(details, tiles, place)
 
 
-def tiles_kernel(parts, segments, chips, groups, blocks, relations, *refs):
-    place_ref, refs = refs[0], refs[1:]
-    buffers, refs = refs[: len(segments)], refs[len(segments) :]
-    payloads, refs = refs[: len(parts)], refs[len(parts) :]
-    near_ref, far_ref, grad_far, grad_own, summed = refs[:5]
-    adjoint, total, vector, codes, sem, landed = refs[5:]
-    chip, group, core = place_ref[0], place_ref[1], place_ref[2]
+def read_codes(parts, payloads, vector, codes, sem):
+    copies = {}
+    for payload, (j, first, size) in zip(payloads, parts, strict=True):
+        if first == 0:
+            last = payload[payload.shape[0] - SLOTS :, :]
+            vector[j] = last.astype(jnp.float32).astype(jnp.int32)
+            copies[j] = pltpu.make_async_copy(vector.at[j], codes.at[j], sem.at[j])
+            copies[j].start()
+    return copies
+
+
+def gather_moves(buffers, segments, place_ref, groups, adjoint, landed):
+    group, core = place_ref[1], place_ref[2]
     piece = adjoint.shape[1] // groups
-    moves = {j: [] for j in range(chips)}
+    where = sorted({j for level, _ in segments for j in level})
+    moves = {j: [] for j in where}
     for buffer, (level, origins) in zip(buffers, segments, strict=True):
         for q, origin in enumerate(origins):
             start = jnp.where(core == 0, origin[0], origin[1]) ^ group
@@ -105,47 +112,93 @@
                 moves[j].append(
                     pltpu.make_async_copy(
                         buffer.at[pl.ds((q * len(level) + n) * piece, piece)],
-                        adjoint.at[j, pl.ds(start, piece)],
-                        landed.at[j, len(moves[j])],
+                        adjoint.at[where.index(j), pl.ds(start, piece)],
+                        landed.at[where.index(j), len(moves[j])],
                     )
                 )
-    for j in range(chips):
+                moves[j][-1].start()
+    return where, moves
+
+
+def add_tiles(payload, j, first, size, adjoint, total, codes):
+    edge = payload.shape[-1]
+    unroll = next(u for u in range(min(size, 8), 0, -1) if size % u == 0)
+    if unroll == 1:
+        unroll = size
+
+    def some(i, carry):
+        for u in range(unroll):
+            p = i * unroll + u
+            row = pl.multiple_of(codes[j, first + p, 1] * edge, edge)
+            partial = lax.dot_general(
+                payload[pl.ds(pl.multiple_of(p * edge, edge), edge), :],
+                adjoint[pl.ds(row, edge), :],
+                (((0,), (0,)), ((), ())),
+                preferred_element_type=jnp.float32,
+            )
+            total[codes[j, first + p, 0]] += partial.astype(jnp.bfloat16).astype(jnp.float32)
+        return carry
+
+    lax.fori_loop(0, size // unroll, some, 0)
+
+
+def early_kernel(parts, segments, groups, place_ref, *refs):
+    buffers, refs = refs[: len(segments)], refs[len(segments) :]
+    payloads, refs = refs[: len(parts)], refs[len(parts) :]
+    adjoint, total, vector, codes, sem, landed = refs
+    where, moves = gather_moves(buffers, segments, place_ref, groups, adjoint, landed)
+    copies = read_codes(parts, payloads, vector, codes, sem)
+    total[...] = jnp.zeros_like(total)
+    for j in where:
         for move in moves[j]:
-            move.start()
-    edge = payloads[0].shape[-1]
-    copies = {}
-    for payload, (j, first, size) in zip(payloads, parts, strict=True):
-        if first == 0:
-            vector[j] = payload[size * edge :, :].astype(jnp.float32).astype(jnp.int32)
-            copies[j] = pltpu.make_async_copy(vector.at[j], codes.at[j], sem.at[j])
-            copies[j].start()
-    total[...] = jnp.zeros_like(total)
-
-    def add(j, payload, slot, p):
-        row = pl.multiple_of(codes[j, slot + p, 1] * edge, edge)
-        partial = lax.dot_general(
-            payload[pl.ds(pl.multiple_of(p * edge, edge), edge), :],
-            adjoint[j, pl.ds(row, edge), :],
-            (((0,), (0,)), ((), ())),
-            preferred_element_type=jnp.float32,
-        )
-        total[codes[j, slot + p, 0]] += partial.astype(jnp.bfloat16).astype(jnp.float32)
-
+            move.wait()
     for payload, (j, first, size) in zip(payloads, parts, strict=True):
         if first == 0:
             copies[j].wait()
-            for move in moves[j]:
+        add_tiles(payload, j, first, size, adjoint.at[where.index(j)], total, codes)
+
+
+def early_tiles(parts, segments, place, buffers, payloads, sizes):
+    chips, groups, blocks, relations = sizes
+    edge, feature = payloads[0].shape[-1], buffers[0].shape[-1]
+    held = len({j for level, _ in segments for j in level})
+    return pl.pallas_call(
+        functools.partial(early_kernel, parts, segments, groups),
+        out_shape=[
+            jax.ShapeDtypeStruct((held, blocks * edge, feature), jnp.bfloat16),
+            jax.ShapeDtypeStruct((CORES * relations * blocks, edge, feature), jnp.float32),
+        ],
+        in_specs=[SMEM] + [ANY] * len(buffers) + [VMEM] * len(payloads),
+        out_specs=[VMEM] * 2,
+        scratch_shapes=[
+            pltpu.VMEM((chips, SLOTS, edge), jnp.int32),
+            pltpu.SMEM((chips, SLOTS, edge), jnp.int32),
+            pltpu.SemaphoreType.DMA((chips,)),
+            pltpu.SemaphoreType.DMA((held, groups)),
+        ],
+        compiler_params=pltpu.CompilerParams(vmem_limit_bytes=LIMIT),
+        cost_estimate=pl.CostEstimate(flops=0, bytes_accessed=1_000_000, transcendentals=0),
+        name="early_tiles",
+    )(place, *buffers, *payloads)
+
+
+def late_kernel(parts, held, segments, sizes, place_ref, adjoint, before, *refs):
+    chips, groups, blocks, relations = sizes
+    buffers, refs = refs[: len(segments)], refs[len(segments) :]
+    payloads, refs = refs[: len(parts)], refs[len(parts) :]
+    near_ref, far_ref, grad_far, grad_own, summed, total = refs[:6]
+    late, vector, codes, sem, landed = refs[6:]
+    chip, core = place_ref[0], place_ref[2]
+    edge = payloads[0].shape[-1]
+    where, moves = gather_moves(buffers, segments, place_ref, groups, late, landed)
+    copies = read_codes(parts, payloads, vector, codes, sem)
+    for payload, (j, first, size) in zip(payloads, parts, strict=True):
+        if first == 0:
+            copies[j].wait()
+            for move in moves.get(j, []):
                 move.wait()
-        unroll = next(u for u in range(min(size, 8), 0, -1) if size % u == 0)
-        if unroll == 1:
-            unroll = size
-
-        def some(i, carry):
-            for u in range(unroll):
-                add(j, payload, first, i * unroll + u)
-            return carry
-
-        lax.fori_loop(0, size // unroll, some, 0)
+        shard = late.at[where.index(j)] if j in where else adjoint.at[held.index(j)]
+        add_tiles(payload, j, first, size, shard, total, codes)
 
     rows = blocks * edge
     share = near_ref.shape[0] // (chips * CORES)
@@ -166,32 +219,52 @@
                         out[chip ^ c, r] = slab.astype(out.dtype)
 
 
-def tiles_and_grad(parts, segments, place, buffers, payloads, near, far, sizes):
+def late_tiles_and_grad(parts, held, segments, place, adjoint, total, buffers, payloads, inputs, sizes):
     chips, groups, blocks, relations = sizes
-    feature, rows = near.shape
+    feature, rows = inputs[0].shape
     edge = rows // blocks
     shape = (chips, relations, feature // (chips * CORES), feature)
+    behind = len({j for level, _ in segments for j in level})
     return pl.pallas_call(
-        functools.partial(tiles_kernel, parts, segments, chips, groups, blocks, relations),
+        functools.partial(late_kernel, parts, held, segments, sizes),
         out_shape=[
             jax.ShapeDtypeStruct(shape, jnp.bfloat16),
             jax.ShapeDtypeStruct(shape, jnp.float32),
             jax.ShapeDtypeStruct((CORES, relations, rows, feature), jnp.bfloat16),
+            jax.ShapeDtypeStruct(total.shape, total.dtype),
         ],
-        in_specs=[SMEM] + [ANY] * len(buffers) + [VMEM] * (2 + len(payloads)),
-        out_specs=[VMEM] * 3,
+        in_specs=[SMEM] + [VMEM] * 2 + [ANY] * len(buffers) + [VMEM] * (2 + len(payloads)),
+        out_specs=[VMEM] * 4,
         scratch_shapes=[
-            pltpu.VMEM((chips, rows, feature), jnp.bfloat16),
-            pltpu.VMEM((CORES * relations * blocks, edge, feature), jnp.float32),
+            pltpu.VMEM((behind, rows, feature), jnp.bfloat16),
             pltpu.VMEM((chips, SLOTS, edge), jnp.int32),
             pltpu.SMEM((chips, SLOTS, edge), jnp.int32),
             pltpu.SemaphoreType.DMA((chips,)),
-            pltpu.SemaphoreType.DMA((chips, groups)),
+            pltpu.SemaphoreType.DMA((behind, groups)),
         ],
+        input_output_aliases={2: 3},
         compiler_params=pltpu.CompilerParams(vmem_limit_bytes=LIMIT),
         cost_estimate=pl.CostEstimate(flops=0, bytes_accessed=1_000_000, transcendentals=0),
-        name="tiles_and_grad",
-    )(place, *buffers, *payloads, near, far)
+        name="late_tiles_and_grad",
+    )(place, adjoint, total, *buffers, *payloads, *inputs)
+
+
+def turn_kernel(*refs):
+    half = len(refs) // 2
+    for source, target in zip(refs[:half], refs[half:], strict=True):
+        target[...] = source[...].T
+
+
+def turned(*arrays):
+    return pl.pallas_call(
+        turn_kernel,
+        out_shape=[jax.ShapeDtypeStruct(a.shape[::-1], a.dtype) for a in arrays],
+        in_specs=[VMEM] * len(arrays),
+        out_specs=[VMEM] * len(arrays),
+        compiler_params=pltpu.CompilerParams(vmem_limit_bytes=LIMIT),
+        cost_estimate=pl.CostEstimate(flops=0, bytes_accessed=1_000_000, transcendentals=0),
+        name="turn_inputs",
+    )(*arrays)
 
 
 def rows_kernel(groups, relations, far, place_ref, summed, weights_ref, out):
@@ -280,7 +353,7 @@
     ]
     levels[:2] = [levels[0] + levels[1]]
     steps = groups.bit_length() - 1
-    near = layer_input[0].T
+    near = layer_input[0]
     far = across(near, "node", nodes, 1)
     mid = chips // 2
     parts = [(0, 0, SLOTS), (mid, 0, HEAD), (mid, HEAD, SLOTS - HEAD)]
@@ -320,9 +393,30 @@
         for value, origins in held:
             buffers.append(value)
             segments.append((level, origins))
+    near, far = turned(near, far)
     sizes = (chips, groups, blocks, relations)
-    grad_far, grad_own, summed = tiles_and_grad(
-        parts, segments, place, buffers, payloads, near, far, sizes
+    early = [i for i, (j, _, _) in enumerate(parts) if j in (0, mid)]
+    late = [i for i in range(len(parts)) if i not in early][::-1]
+    split = sum(level == levels[0] for level, _ in segments)
+    adjoint, total = early_tiles(
+        tuple(parts[i] for i in early),
+        segments[:split],
+        place,
+        buffers[:split],
+        [payloads[i] for i in early],
+        sizes,
+    )
+    grad_far, grad_own, summed, _ = late_tiles_and_grad(
+        tuple(parts[i] for i in late),
+        sorted(levels[0]),
+        segments[split:],
+        place,
+        adjoint,
+        total,
+        buffers[split:],
+        [payloads[i] for i in late],
+        [near, far],
+        sizes,
     )
     grad_far = across(grad_far, "node", nodes, 1)
     rows_far = row_terms(place, summed, rel_weights, groups, 1, jnp.bfloat16)

time: 104 us -> 100 us (0.962)
  waiting for transfers between devices: 54.6 us -> 48.7 us
  Pallas kernels: 14.8 us -> 17.1 us
  other arithmetic: 2.52 us -> 4.14 us
  local copies, waits for them, and re-layouts: 2.92 us -> 1.36 us
    ppermute x16, waiting for transfers between devices: 54.6 us -> 46.4 us  [across(): return lax.ppermute(value, axis, [(i, i ^ mask) for i in range(size)])]
    pallas_call x1 -> x3, Pallas kernels: 8.4 us -> 10.8 us  [the longest x1 6.35 us: late_tiles_and_grad(): pl.pallas_call(functools.partial(late_kernel, parts, held, segments, size...]
    ppermute x5, waiting for transfers between devices: 0.01 us -> 2.31 us  [in_plane(): return lax.ppermute(value, ('rel', 'node'), pairs)]
    unnamed x18 -> x11, local copies, waits for them, and re-layouts: 2.82 us -> 1.26 us
  transfers between devices with their start and end apart: 21 -> 21, of which waited for: 11 -> 11; matrix products, arithmetic and copies ran while one was open for 2% -> 4% of each run, Pallas kernels for 6% -> 11%
where the time goes in v3:
time: 100 us
  waiting for transfers between devices  48.7 us (49%)
  starting transfers between devices  27.8 us (28%)
  Pallas kernels  17.1 us (17%)
  other arithmetic  4.14 us (4%)
  local copies, waits for them, and re-layouts  1.36 us (1%)
    ppermute x16, waiting for transfers between devices, across(): return lax.ppermute(value, axis, [(i, i ^ mask) for i in range(size)])  46.4 us
    ppermute x16, starting transfers between devices, across(): return lax.ppermute(value, axis, [(i, i ^ mask) for i in range(size)])  20.9 us
    ppermute x5, starting transfers between devices, in_plane(): return lax.ppermute(value, ('rel', 'node'), pairs)  6.99 us
    pallas_call x1, Pallas kernels, late_tiles_and_grad(): pl.pallas_call(functools.partial(late_kernel, parts, held, segments, size...  6.35 us
    pallas_call x1, Pallas kernels, early_tiles(): pl.pallas_call(functools.partial(early_kernel, parts, segments, groups),...  3.8 us
    pallas_call x2, Pallas kernels, row_terms(): pl.pallas_call(functools.partial(rows_kernel, groups, relations, far), ou...  3.63 us
    pallas_call x1, Pallas kernels, place_tiles(): pl.pallas_call(functools.partial(place_kernel, parts, chips, blocks, rela...  2.73 us
    ppermute x5, waiting for transfers between devices, in_plane(): return lax.ppermute(value, ('rel', 'node'), pairs)  2.31 us
  transfers between devices with their start and end apart: 21, of which 11 were waited for; matrix products, arithmetic and copies ran while one was open for 4% of the time, Pallas kernels for 11%

profile of v3, /device:TPU:0, one launch (start us, length us, event | category | flops | bytes accessed | tf_op | source)
XLA Modules:
  0.0 100.3 jit_solution(2298193185739347643)
XLA Ops:
  1.2 2.7 %collective-permute-start = (bf16[256,512]{1,0:T(8,128)(2,1)}, bf16[256,512]{1,0:T(8,128)(2,1)S(1)}, u32[]{:S(2)}, u32[]{:S(2)}) collective-permute-start(bf16[256,512]{1,0:T(8,128)(2,1)} %bitcast.49), channel_id=1, source_target_pairs={{0,2},{1,3},{2,0},{3,1},{4,6},{5,7},{6,4},{7,5},{8,10},{9,11},{10,... | collective-permute-start | bytes 786440 | tf_op jit(solution)/shard_map/ppermute | solution.py:333
  3.8 2.6 %collective-permute-start.1 = (bf16[256,512]{1,0:T(8,128)(2,1)}, bf16[256,512]{1,0:T(8,128)(2,1)S(1)}, u32[]{:S(2)}, u32[]{:S(2)}) collective-permute-start(bf16[256,512]{1,0:T(8,128)(2,1)} %bitcast.50), channel_id=1, source_target_pairs={{0,4},{1,5},{2,6},{3,7},{4,0},{5,1},{6,2},{7,3},{8,12},{9,13},{10,... | collective-permute-start | bytes 786440 | tf_op jit(solution)/shard_map/ppermute | solution.py:333
  8.4 2.7 %place_tiles.1 = (bf16[2064,128]{1,0:T(8,128)(2,1)S(1)}, bf16[656,128]{1,0:T(8,128)(2,1)S(1)}, bf16[1408,128]{1,0:T(8,128)(2,1)S(1)}, bf16[2064,128]{1,0:T(8,128)(2,1)S(1)}, bf16[2064,128]{1,0:T(8,128)(2,1)S(1)}) custom-call(s32[4,32]{1,0:T(4,128)S(1)} %pad_add_fusion.refs_0_, bf16[32,128,128]{2,1,0:T(8,128)(2,1)S(1)} %bitcast.46, ...), custom_call_target="tpu_custom_call" | custom-call | bytes 4000000 | tf_op jit(solution)/shard_map/place_tiles/pallas_call | solution.py:73
  11.6 4.8 %collective-permute-done = bf16[256,512]{1,0:T(8,128)(2,1)S(1)} collective-permute-done((bf16[256,512]{1,0:T(8,128)(2,1)}, bf16[256,512]{1,0:T(8,128)(2,1)S(1)}, u32[]{:S(2)}, u32[]{:S(2)}) %collective-permute-start) | collective-permute-done | bytes 262176 | tf_op jit(solution)/shard_map/ppermute | solution.py:333
  16.4 6.2 %collective-permute-done.1 = bf16[256,512]{1,0:T(8,128)(2,1)S(1)} collective-permute-done((bf16[256,512]{1,0:T(8,128)(2,1)}, bf16[256,512]{1,0:T(8,128)(2,1)S(1)}, u32[]{:S(2)}, u32[]{:S(2)}) %collective-permute-start.1) | collective-permute-done | bytes 262176 | tf_op jit(solution)/shard_map/ppermute | solution.py:333
  23.6 2.5 %collective-permute-done.2.refs_5_ = bf16[656,128]{1,0:T(8,128)(2,1)S(1)} collective-permute-done((bf16[656,128]{1,0:T(8,128)(2,1)S(1)}, bf16[656,128]{1,0:T(8,128)(2,1)S(1)}, u32[]{:S(2)}, u32[]{:S(2)}) %collective-permute-start.2) | collective-permute-done | bytes 167968 | tf_op jit(solution)/shard_map/ppermute | solution.py:333
  27.7 3.0 %collective-permute-start.7 = (bf16[1408,128]{1,0:T(8,128)(2,1)S(1)}, bf16[1408,128]{1,0:T(8,128)(2,1)S(1)}, u32[]{:S(2)}, u32[]{:S(2)}) collective-permute-start(bf16[1408,128]{1,0:T(8,128)(2,1)S(1)} %get-tuple-element.23), channel_id=1, source_target_pairs={{0,4},{1,5},{2,6},{3,7},{4,0},{5,1},{6,2},{7,3},{8,12},{9,13},{10,... | collective-permute-start | bytes 1081352 | tf_op jit(solution)/shard_map/ppermute | solution.py:333
  30.7 9.8 %collective-permute-done.8 = bf16[256,512]{1,0:T(8,128)(2,1)S(1)} collective-permute-done((bf16[256,512]{1,0:T(8,128)(2,1)S(1)}, bf16[256,512]{1,0:T(8,128)(2,1)S(1)}, u32[]{:S(2)}, u32[]{:S(2)}) %collective-permute-start.8) | collective-permute-done | bytes 262176 | tf_op jit(solution)/shard_map/ppermute | solution.py:333
  42.5 1.5 %collective-permute-start.6 = (bf16[768,512]{1,0:T(8,128)(2,1)S(1)}, bf16[768,512]{1,0:T(8,128)(2,1)S(1)}, u32[]{:S(2)}, u32[]{:S(2)}) collective-permute-start(bf16[768,512]{1,0:T(8,128)(2,1)S(1)} %collective-permute-done.4.refs_1_), channel_id=1, source_target_pairs={{0,16},{1,9},{2,18},{3,11},{4,20},{5,13},{6,22},{7,15},{8,24},{9,1... | collective-permute-start | bytes 2359304 | tf_op jit(solution)/shard_map/ppermute | solution.py:344
  44.0 2.0 %collective-permute-start.12 = (bf16[2064,128]{1,0:T(8,128)(2,1)S(1)}, bf16[2064,128]{1,0:T(8,128)(2,1)S(1)}, u32[]{:S(2)}, u32[]{:S(2)}) collective-permute-start(bf16[2064,128]{1,0:T(8,128)(2,1)S(1)} %get-tuple-element.30), channel_id=1, source_target_pairs={{0,6},{1,7},{2,4},{3,5},{4,2},{5,3},{6,0},{7,1},{8,14},{9,15},{10,... | collective-permute-start | bytes 1585160 | tf_op jit(solution)/shard_map/ppermute | solution.py:333
  46.0 11.4 %collective-permute-done.7.refs_6_ = bf16[1408,128]{1,0:T(8,128)(2,1)S(1)} collective-permute-done((bf16[1408,128]{1,0:T(8,128)(2,1)S(1)}, bf16[1408,128]{1,0:T(8,128)(2,1)S(1)}, u32[]{:S(2)}, u32[]{:S(2)}) %collective-permute-start.7) | collective-permute-done | bytes 360480 | tf_op jit(solution)/shard_map/ppermute | solution.py:333
  57.4 2.0 %collective-permute-start.10 = (bf16[512,512]{1,0:T(8,128)(2,1)S(1)}, bf16[512,512]{1,0:T(8,128)(2,1)S(1)}, u32[]{:S(2)}, u32[]{:S(2)}) collective-permute-start(bf16[512,512]{1,0:T(8,128)(2,1)S(1)} %constant_dynamic-update-slice_fusion.refs_0_), channel_id=1, source_target_pairs={{0,16},{1,9},{2,18},{3,11},{4,20},{5,13},{6,22},{7,15},{8,24},{9,1... | collective-permute-start | bytes 1572872 | tf_op jit(solution)/shard_map/ppermute | solution.py:344
  60.1 2.3 %collective-permute-done.6.refs_3_ = bf16[768,512]{1,0:T(8,128)(2,1)S(1)} collective-permute-done((bf16[768,512]{1,0:T(8,128)(2,1)S(1)}, bf16[768,512]{1,0:T(8,128)(2,1)S(1)}, u32[]{:S(2)}, u32[]{:S(2)}) %collective-permute-start.6) | collective-permute-done | bytes 786464 | tf_op jit(solution)/shard_map/ppermute | solution.py:344
  62.4 3.8 %early_tiles.1 = (bf16[3,1024,512]{2,1,0:T(8,128)(2,1)S(1)}, f32[32,128,512]{2,1,0:T(8,128)S(1)}) custom-call(s32[3]{0:T(128)S(1)} %pad_add_fusion.1.refs_2_.place_ref, bf16[768,512]{1,0:T(8,128)(2,1)S(1)} %pad_maximum_fusion.refs_0_, bf16[768,512]{1,0:T(8,128)(2,1)S(1)} %collective-permute-done.4.refs_1_, ...), custom_call_target="tpu_custom_call" | custom-call | bytes 1000000 | tf_op jit(solution)/shard_map/early_tiles/pallas_call | solution.py:165
  66.2 3.4 %collective-permute-done.11.refs_2_ = bf16[2064,128]{1,0:T(8,128)(2,1)S(1)} collective-permute-done((bf16[2064,128]{1,0:T(8,128)(2,1)S(1)}, bf16[2064,128]{1,0:T(8,128)(2,1)S(1)}, u32[]{:S(2)}, u32[]{:S(2)}) %collective-permute-start.11) | collective-permute-done | bytes 528416 | tf_op jit(solution)/shard_map/ppermute | solution.py:333
  69.6 6.4 %late_tiles_and_grad.1 = (bf16[4,2,64,512]{3,2,1,0:T(8,128)(2,1)S(1)}, f32[4,2,64,512]{3,2,1,0:T(8,128)S(1)}, bf16[2,2,1024,512]{3,2,1,0:T(8,128)(2,1)S(1)}, f32[32,128,512]{2,1,0:T(8,128)S(1)}) custom-call(s32[3]{0:T(128)S(1)} %pad_add_fusion.1.refs_2_.place_ref, ...), custom_call_target="tpu_custom_call", output_to_operand_aliasing={{3}: (2, {})} | custom-call | bytes 1000000 | tf_op jit(solution)/shard_map/late_tiles_and_grad/pallas_call | solution.py:228
  76.0 1.8 %row_terms.3 = bf16[4,256,512]{2,1,0:T(8,128)(2,1)S(1)} custom-call(s32[3]{0:T(128)S(1)} %pad_add_fusion.1.refs_2_.place_ref, bf16[2,2,1024,512]{3,2,1,0:T(8,128)(2,1)S(1)} %get-tuple-element.35.summed, bf16[2,512,512]{2,1,0:T(8,128)(2,1)S(1)} %copy-done.1), custom_call_target="tpu_custom_call" | custom-call | flops 1073741824 | bytes 4000000 | tf_op jit(solution)/shard_map/row_terms/pallas_call | solution.py:288
  78.4 1.8 %row_terms.2 = f32[4,256,512]{2,1,0:T(8,128)S(1)} custom-call(s32[3]{0:T(128)S(1)} %pad_add_fusion.1.refs_2_.place_ref, bf16[2,2,1024,512]{3,2,1,0:T(8,128)(2,1)S(1)} %get-tuple-element.35.summed, bf16[2,512,512]{2,1,0:T(8,128)(2,1)S(1)} %copy-done.1), custom_call_target="tpu_custom_call" | custom-call | flops 1073741824 | bytes 4000000 | tf_op jit(solution)/shard_map/row_terms/pallas_call | solution.py:288
  80.7 2.4 %collective-permute-start.15 = (bf16[2,64,512]{2,1,0:T(8,128)(2,1)S(1)}, bf16[2,64,512]{2,1,0:T(8,128)(2,1)S(1)}, u32[]{:S(2)}, u32[]{:S(2)}) collective-permute-start(bf16[2,64,512]{2,1,0:T(8,128)(2,1)S(1)} %get-tuple-element.45), channel_id=1, source_target_pairs={{0,4},{1,5},{2,6},{3,7},{4,0},{5,1},{6,2},{7,3},{8,12},{9,13},{10,... | collective-permute-start | bytes 393224 | tf_op jit(solution)/shard_map/ppermute | solution.py:333
  83.1 1.8 %collective-permute-start.16 = (bf16[2,64,512]{2,1,0:T(8,128)(2,1)S(1)}, bf16[2,64,512]{2,1,0:T(8,128)(2,1)S(1)}, u32[]{:S(2)}, u32[]{:S(2)}) collective-permute-start(bf16[2,64,512]{2,1,0:T(8,128)(2,1)S(1)} %get-tuple-element.44), channel_id=1, source_target_pairs={{0,6},{1,7},{2,4},{3,5},{4,2},{5,3},{6,0},{7,1},{8,14},{9,15},{10,... | collective-permute-start | bytes 393224 | tf_op jit(solution)/shard_map/ppermute | solution.py:333
  86.7 1.6 %collective-permute-start.19 = (bf16[256,512]{1,0:T(8,128)(2,1)S(1)}, bf16[256,512]{1,0:T(8,128)(2,1)S(1)}, u32[]{:S(2)}, u32[]{:S(2)}) collective-permute-start(bf16[256,512]{1,0:T(8,128)(2,1)S(1)} %get-tuple-element.42), channel_id=1, source_target_pairs={{0,16},{8,24},{16,0},{24,8},{1,17},{9,25},{17,1},{25,9},{2,18},{10... | collective-permute-start | bytes 786440 | tf_op jit(solution)/shard_map/ppermute | solution.py:333
  88.3 1.8 %collective-permute-start.20 = (bf16[256,512]{1,0:T(8,128)(2,1)S(1)}, bf16[256,512]{1,0:T(8,128)(2,1)S(1)}, u32[]{:S(2)}, u32[]{:S(2)}) collective-permute-start(bf16[256,512]{1,0:T(8,128)(2,1)S(1)} %get-tuple-element.41), channel_id=1, source_target_pairs={{0,24},{8,16},{16,8},{24,0},{1,25},{9,17},{17,9},{25,1},{2,26},{10... | collective-permute-start | bytes 786440 | tf_op jit(solution)/shard_map/ppermute | solution.py:333
  90.4 3.2 %collective-permute-done.15 = bf16[2,64,512]{2,1,0:T(8,128)(2,1)S(1)} collective-permute-done((bf16[2,64,512]{2,1,0:T(8,128)(2,1)S(1)}, bf16[2,64,512]{2,1,0:T(8,128)(2,1)S(1)}, u32[]{:S(2)}, u32[]{:S(2)}) %collective-permute-start.15) | collective-permute-done | bytes 131104 | tf_op jit(solution)/shard_map/ppermute | solution.py:333
  94.8 3.7 %collective-permute-done.19 = bf16[256,512]{1,0:T(8,128)(2,1)S(1)} collective-permute-done((bf16[256,512]{1,0:T(8,128)(2,1)S(1)}, bf16[256,512]{1,0:T(8,128)(2,1)S(1)}, u32[]{:S(2)}, u32[]{:S(2)}) %collective-permute-start.19) | collective-permute-done | bytes 262176 | tf_op jit(solution)/shard_map/ppermute | solution.py:333
  (46 shorter events, 14.2 us)
Async XLA Ops:
  0.6 89.5 %copy-start = (bf16[512,512]{1,0:T(8,128)(2,1)S(1)}, bf16[512,512]{1,0:T(8,128)(2,1)}, u32[]{:S(2)}) copy-start(bf16[512,512]{1,0:T(8,128)(2,1)} %param.12) | copy-start | bytes 1572868
  0.6 25.5 %collective-permute-start.3 = (bf16[1024,512]{1,0:T(8,128)(2,1)}, bf16[1024,512]{1,0:T(8,128)(2,1)S(1)}, u32[]{:S(2)}, u32[]{:S(2)}) collective-permute-start(bf16[1024,512]{1,0:T(8,128)(2,1)} %bitcast.47), channel_id=1, source_target_pairs={{0,1},{1,0},{2,3},{3,2},{4,5},{5,4},{6,7},{7,6},{8,9},{9,8},{10,11... | collective-permute-start | bytes 3145736 | tf_op jit(solution)/shard_map/ppermute | solution.py:333
  1.2 15.2 %collective-permute-start = (bf16[256,512]{1,0:T(8,128)(2,1)}, bf16[256,512]{1,0:T(8,128)(2,1)S(1)}, u32[]{:S(2)}, u32[]{:S(2)}) collective-permute-start(bf16[256,512]{1,0:T(8,128)(2,1)} %bitcast.49), channel_id=1, source_target_pairs={{0,2},{1,3},{2,0},{3,1},{4,6},{5,7},{6,4},{7,5},{8,10},{9,11},{10,... | collective-permute-start | bytes 786440 | tf_op jit(solution)/shard_map/ppermute | solution.py:333
  3.8 18.8 %collective-permute-start.1 = (bf16[256,512]{1,0:T(8,128)(2,1)}, bf16[256,512]{1,0:T(8,128)(2,1)S(1)}, u32[]{:S(2)}, u32[]{:S(2)}) collective-permute-start(bf16[256,512]{1,0:T(8,128)(2,1)} %bitcast.50), channel_id=1, source_target_pairs={{0,4},{1,5},{2,6},{3,7},{4,0},{5,1},{6,2},{7,3},{8,12},{9,13},{10,... | collective-permute-start | bytes 786440 | tf_op jit(solution)/shard_map/ppermute | solution.py:333
  8.4 51.0 %copy-start.3 = (bf16[1,1024,512]{2,1,0:T(8,128)(2,1)S(1)}, bf16[1,1024,512]{2,1,0:T(8,128)(2,1)}, u32[]{:S(2)}) copy-start(bf16[1,1024,512]{2,1,0:T(8,128)(2,1)} %param.10) | copy-start | bytes 3145732
  11.2 15.0 %collective-permute-start.2 = (bf16[656,128]{1,0:T(8,128)(2,1)S(1)}, bf16[656,128]{1,0:T(8,128)(2,1)S(1)}, u32[]{:S(2)}, u32[]{:S(2)}) collective-permute-start(bf16[656,128]{1,0:T(8,128)(2,1)S(1)} %get-tuple-element.19), channel_id=1, source_target_pairs={{0,4},{1,5},{2,6},{3,7},{4,0},{5,1},{6,2},{7,3},{8,12},{9,13},{10,... | collective-permute-start | bytes 503816 | tf_op jit(solution)/shard_map/ppermute | solution.py:333
  26.2 16.3 %collective-permute-start.4 = (bf16[768,512]{1,0:T(8,128)(2,1)S(1)}, bf16[768,512]{1,0:T(8,128)(2,1)S(1)}, u32[]{:S(2)}, u32[]{:S(2)}) collective-permute-start(bf16[768,512]{1,0:T(8,128)(2,1)S(1)} %pad_maximum_fusion.refs_0_), channel_id=1, source_target_pairs={{0,8},{1,17},{2,10},{3,19},{4,12},{5,21},{6,14},{7,23},{8,0},{9,25... | collective-permute-start | bytes 2359304 | tf_op jit(solution)/shard_map/ppermute | solution.py:344
  27.7 12.8 %collective-permute-start.8 = (bf16[256,512]{1,0:T(8,128)(2,1)S(1)}, bf16[256,512]{1,0:T(8,128)(2,1)S(1)}, u32[]{:S(2)}, u32[]{:S(2)}) collective-permute-start(bf16[256,512]{1,0:T(8,128)(2,1)S(1)} %collective-permute-done.1), channel_id=1, source_target_pairs={{0,2},{1,3},{2,0},{3,1},{4,6},{5,7},{6,4},{7,5},{8,10},{9,11},{10,... | collective-permute-start | bytes 786440 | tf_op jit(solution)/shard_map/ppermute | solution.py:333
  27.7 29.7 %collective-permute-start.7 = (bf16[1408,128]{1,0:T(8,128)(2,1)S(1)}, bf16[1408,128]{1,0:T(8,128)(2,1)S(1)}, u32[]{:S(2)}, u32[]{:S(2)}) collective-permute-start(bf16[1408,128]{1,0:T(8,128)(2,1)S(1)} %get-tuple-element.23), channel_id=1, source_target_pairs={{0,4},{1,5},{2,6},{3,7},{4,0},{5,1},{6,2},{7,3},{8,12},{9,13},{10,... | collective-permute-start | bytes 1081352 | tf_op jit(solution)/shard_map/ppermute | solution.py:333
  40.5 17.0 %collective-permute-start.9 = (bf16[256,512]{1,0:T(8,128)(2,1)S(1)}, bf16[256,512]{1,0:T(8,128)(2,1)S(1)}, u32[]{:S(2)}, u32[]{:S(2)}) collective-permute-start(bf16[256,512]{1,0:T(8,128)(2,1)S(1)} %collective-permute-done.8), channel_id=1, source_target_pairs={{0,8},{1,17},{2,10},{3,19},{4,12},{5,21},{6,14},{7,23},{8,0},{9,25... | collective-permute-start | bytes 786440 | tf_op jit(solution)/shard_map/ppermute | solution.py:344
  41.9 18.1 %collective-permute-start.5 = (bf16[768,512]{1,0:T(8,128)(2,1)S(1)}, bf16[768,512]{1,0:T(8,128)(2,1)S(1)}, u32[]{:S(2)}, u32[]{:S(2)}) collective-permute-start(bf16[768,512]{1,0:T(8,128)(2,1)S(1)} %pad_maximum_fusion.refs_0_), channel_id=1, source_target_pairs={{0,16},{1,9},{2,18},{3,11},{4,20},{5,13},{6,22},{7,15},{8,24},{9,1... | collective-permute-start | bytes 2359304 | tf_op jit(solution)/shard_map/ppermute | solution.py:344
  42.5 19.9 %collective-permute-start.6 = (bf16[768,512]{1,0:T(8,128)(2,1)S(1)}, bf16[768,512]{1,0:T(8,128)(2,1)S(1)}, u32[]{:S(2)}, u32[]{:S(2)}) collective-permute-start(bf16[768,512]{1,0:T(8,128)(2,1)S(1)} %collective-permute-done.4.refs_1_), channel_id=1, source_target_pairs={{0,16},{1,9},{2,18},{3,11},{4,20},{5,13},{6,22},{7,15},{8,24},{9,1... | collective-permute-start | bytes 2359304 | tf_op jit(solution)/shard_map/ppermute | solution.py:344
  44.0 22.2 %collective-permute-start.12 = (bf16[2064,128]{1,0:T(8,128)(2,1)S(1)}, bf16[2064,128]{1,0:T(8,128)(2,1)S(1)}, u32[]{:S(2)}, u32[]{:S(2)}) collective-permute-start(bf16[2064,128]{1,0:T(8,128)(2,1)S(1)} %get-tuple-element.30), channel_id=1, source_target_pairs={{0,6},{1,7},{2,4},{3,5},{4,2},{5,3},{6,0},{7,1},{8,14},{9,15},{10,... | collective-permute-start | bytes 1585160 | tf_op jit(solution)/shard_map/ppermute | solution.py:333
  57.4 12.2 %collective-permute-start.11 = (bf16[2064,128]{1,0:T(8,128)(2,1)S(1)}, bf16[2064,128]{1,0:T(8,128)(2,1)S(1)}, u32[]{:S(2)}, u32[]{:S(2)}) collective-permute-start(bf16[2064,128]{1,0:T(8,128)(2,1)S(1)} %get-tuple-element.28), channel_id=1, source_target_pairs={{0,2},{1,3},{2,0},{3,1},{4,6},{5,7},{6,4},{7,5},{8,10},{9,11},{10,... | collective-permute-start | bytes 1585160 | tf_op jit(solution)/shard_map/ppermute | solution.py:333
  57.4 12.1 %collective-permute-start.10 = (bf16[512,512]{1,0:T(8,128)(2,1)S(1)}, bf16[512,512]{1,0:T(8,128)(2,1)S(1)}, u32[]{:S(2)}, u32[]{:S(2)}) collective-permute-start(bf16[512,512]{1,0:T(8,128)(2,1)S(1)} %constant_dynamic-update-slice_fusion.refs_0_), channel_id=1, source_target_pairs={{0,16},{1,9},{2,18},{3,11},{4,20},{5,13},{6,22},{7,15},{8,24},{9,1... | collective-permute-start | bytes 1572872 | tf_op jit(solution)/shard_map/ppermute | solution.py:344
  75.9 4.3 %collective-permute-start.13 = (bf16[4,2,64,512]{3,2,1,0:T(8,128)(2,1)S(1)}, bf16[4,2,64,512]{3,2,1,0:T(8,128)(2,1)S(1)}, u32[]{:S(2)}, u32[]{:S(2)}) collective-permute-start(bf16[4,2,64,512]{3,2,1,0:T(8,128)(2,1)S(1)} %get-tuple-element.34), channel_id=1, source_target_pairs={{0,1},{1,0},{2,3},{3,2},{4,5},{5,4},{6,7},{7,6},{8,9},{9,8},{10,11... | collective-permute-start | bytes 1572872 | tf_op jit(solution)/shard_map/ppermute | solution.py:333
  77.8 7.1 %collective-permute-start.17 = (bf16[4,256,512]{2,1,0:T(8,128)(2,1)S(1)}, bf16[4,256,512]{2,1,0:T(8,128)(2,1)S(1)}, u32[]{:S(2)}, u32[]{:S(2)}) collective-permute-start(bf16[4,256,512]{2,1,0:T(8,128)(2,1)S(1)} %row_terms.3), channel_id=1, source_target_pairs={{0,1},{1,0},{2,3},{3,2},{4,5},{5,4},{6,7},{7,6},{8,9},{9,8},{10,11... | collective-permute-start | bytes 3145736 | tf_op jit(solution)/shard_map/ppermute | solution.py:333
  80.5 7.8 %collective-permute-start.14 = (bf16[2,64,512]{2,1,0:T(8,128)(2,1)S(1)}, bf16[2,64,512]{2,1,0:T(8,128)(2,1)S(1)}, u32[]{:S(2)}, u32[]{:S(2)}) collective-permute-start(bf16[2,64,512]{2,1,0:T(8,128)(2,1)S(1)} %get-tuple-element.43), channel_id=1, source_target_pairs={{0,2},{1,3},{2,0},{3,1},{4,6},{5,7},{6,4},{7,5},{8,10},{9,11},{10,... | collective-permute-start | bytes 393224 | tf_op jit(solution)/shard_map/ppermute | solution.py:333
  80.7 12.9 %collective-permute-start.15 = (bf16[2,64,512]{2,1,0:T(8,128)(2,1)S(1)}, bf16[2,64,512]{2,1,0:T(8,128)(2,1)S(1)}, u32[]{:S(2)}, u32[]{:S(2)}) collective-permute-start(bf16[2,64,512]{2,1,0:T(8,128)(2,1)S(1)} %get-tuple-element.45), channel_id=1, source_target_pairs={{0,4},{1,5},{2,6},{3,7},{4,0},{5,1},{6,2},{7,3},{8,12},{9,13},{10,... | collective-permute-start | bytes 393224 | tf_op jit(solution)/shard_map/ppermute | solution.py:333
  83.1 7.0 %copy-start.4 = (bf16[1,256,512]{2,1,0:T(8,128)(2,1)S(1)}, bf16[1,256,512]{2,1,0:T(8,128)(2,1)}, u32[]{:S(2)}) copy-start(bf16[1,256,512]{2,1,0:T(8,128)(2,1)} %param.9) | copy-start | bytes 786436
  83.1 10.5 %collective-permute-start.16 = (bf16[2,64,512]{2,1,0:T(8,128)(2,1)S(1)}, bf16[2,64,512]{2,1,0:T(8,128)(2,1)S(1)}, u32[]{:S(2)}, u32[]{:S(2)}) collective-permute-start(bf16[2,64,512]{2,1,0:T(8,128)(2,1)S(1)} %get-tuple-element.44), channel_id=1, source_target_pairs={{0,6},{1,7},{2,4},{3,5},{4,2},{5,3},{6,0},{7,1},{8,14},{9,15},{10,... | collective-permute-start | bytes 393224 | tf_op jit(solution)/shard_map/ppermute | solution.py:333
  85.5 9.3 %collective-permute-start.18 = (bf16[256,512]{1,0:T(8,128)(2,1)S(1)}, bf16[256,512]{1,0:T(8,128)(2,1)S(1)}, u32[]{:S(2)}, u32[]{:S(2)}) collective-permute-start(bf16[256,512]{1,0:T(8,128)(2,1)S(1)} %get-tuple-element.40), channel_id=1, source_target_pairs={{0,8},{8,0},{16,24},{24,16},{1,9},{9,1},{17,25},{25,17},{2,10},{10... | collective-permute-start | bytes 786440 | tf_op jit(solution)/shard_map/ppermute | solution.py:333
  86.7 11.9 %collective-permute-start.19 = (bf16[256,512]{1,0:T(8,128)(2,1)S(1)}, bf16[256,512]{1,0:T(8,128)(2,1)S(1)}, u32[]{:S(2)}, u32[]{:S(2)}) collective-permute-start(bf16[256,512]{1,0:T(8,128)(2,1)S(1)} %get-tuple-element.42), channel_id=1, source_target_pairs={{0,16},{8,24},{16,0},{24,8},{1,17},{9,25},{17,1},{25,9},{2,18},{10... | collective-permute-start | bytes 786440 | tf_op jit(solution)/shard_map/ppermute | solution.py:333
  88.3 11.1 %collective-permute-start.20 = (bf16[256,512]{1,0:T(8,128)(2,1)S(1)}, bf16[256,512]{1,0:T(8,128)(2,1)S(1)}, u32[]{:S(2)}, u32[]{:S(2)}) collective-permute-start(bf16[256,512]{1,0:T(8,128)(2,1)S(1)} %get-tuple-element.41), channel_id=1, source_target_pairs={{0,24},{8,16},{16,8},{24,0},{1,25},{9,17},{17,9},{25,1},{2,26},{10... | collective-permute-start | bytes 786440 | tf_op jit(solution)/shard_map/ppermute | solution.py:333
  (2 other events, 7.7 us)

commit v4 on v3

--- a/solution.py
+++ b/solution.py
@@ -11,7 +11,7 @@
 CORES = 2
 SLOTS = CORES * CAPACITY
 LIMIT = 24 * 1024 * 1024
-HEAD = 5
+HEAD = 3
 SMEM = pl.BlockSpec(memory_space=pltpu.SMEM)
 VMEM = pl.BlockSpec(memory_space=pltpu.VMEM)
 ANY = pl.BlockSpec(memory_space=pl.ANY)
@@ -186,9 +186,7 @@
     chips, groups, blocks, relations = sizes
     buffers, refs = refs[: len(segments)], refs[len(segments) :]
     payloads, refs = refs[: len(parts)], refs[len(parts) :]
-    near_ref, far_ref, grad_far, grad_own, summed, total = refs[:6]
-    late, vector, codes, sem, landed = refs[6:]
-    chip, core = place_ref[0], place_ref[2]
+    weights_ref, rows_far, summed, total, late, vector, codes, sem, landed = refs
     edge = payloads[0].shape[-1]
     where, moves = gather_moves(buffers, segments, place_ref, groups, late, landed)
     copies = read_codes(parts, payloads, vector, codes, sem)
@@ -200,41 +198,54 @@
         shard = late.at[where.index(j)] if j in where else adjoint.at[held.index(j)]
         add_tiles(payload, j, first, size, shard, total, codes)
 
+    for h in range(CORES):
+        for r in range(relations):
+            part = total[pl.ds((h * relations + r) * blocks, blocks)].astype(jnp.bfloat16)
+            summed[h, r] = part.reshape(blocks * edge, part.shape[-1])
+    for spot, value in multiply_rows(place_ref, summed, weights_ref, groups, 1):
+        rows_far[spot] = value.astype(rows_far.dtype)
+
+
+def multiply_rows(place_ref, summed, weights_ref, groups, far):
+    group, core = place_ref[1], place_ref[2]
+    piece = summed.shape[2] // groups
+    steps = groups.bit_length() - 1
+    value = None
+    for r in range(summed.shape[1]):
+        term = lax.dot_general(
+            summed[core ^ far, r],
+            weights_ref[r],
+            (((1,), (1,)), ((), ())),
+            preferred_element_type=jnp.float32,
+        )
+        value = term if value is None else value + term
+    pieces = []
+    for q in range(groups):
+        mask = group ^ q
+        spot = [0, 0]
+        for step in range(steps):
+            for c in range(CORES):
+                bit = plane_masks(groups, c)[step].bit_length() - 1
+                spot[c] = spot[c] + (((mask >> bit) & 1) << (steps - 1 - step))
+        spot = jnp.where((core ^ far) == 0, spot[0], spot[1])
+        pieces.append((spot, value[q * piece : (q + 1) * piece]))
+    return pieces
+
+
+def late_tiles_and_rows(parts, held, segments, place, adjoint, total, buffers, payloads, weights, sizes):
+    chips, groups, blocks, relations = sizes
+    edge, feature = total.shape[1:]
     rows = blocks * edge
-    share = near_ref.shape[0] // (chips * CORES)
-    for r in range(relations):
-        for h in range(CORES):
-            part = total[pl.ds((h * relations + r) * blocks, blocks)].astype(jnp.bfloat16)
-            summed[h, r] = part.reshape(rows, part.shape[-1])
-        grad = jnp.dot(near_ref[...], summed[core, r], preferred_element_type=jnp.float32)
-        grad += jnp.dot(far_ref[...], summed[1 - core, r], preferred_element_type=jnp.float32)
-        for far in range(CORES):
-            out = grad_far if far else grad_own
-            for c in range(chips):
-                for h in range(CORES):
-                    slab = grad[(c * CORES + h) * share : (c * CORES + h + 1) * share]
-
-                    @pl.when(h == (core ^ far))
-                    def _():
-                        out[chip ^ c, r] = slab.astype(out.dtype)
-
-
-def late_tiles_and_grad(parts, held, segments, place, adjoint, total, buffers, payloads, inputs, sizes):
-    chips, groups, blocks, relations = sizes
-    feature, rows = inputs[0].shape
-    edge = rows // blocks
-    shape = (chips, relations, feature // (chips * CORES), feature)
     behind = len({j for level, _ in segments for j in level})
     return pl.pallas_call(
         functools.partial(late_kernel, parts, held, segments, sizes),
         out_shape=[
-            jax.ShapeDtypeStruct(shape, jnp.bfloat16),
-            jax.ShapeDtypeStruct(shape, jnp.float32),
+            jax.ShapeDtypeStruct((groups, rows // groups, feature), jnp.bfloat16),
             jax.ShapeDtypeStruct((CORES, relations, rows, feature), jnp.bfloat16),
             jax.ShapeDtypeStruct(total.shape, total.dtype),
         ],
-        in_specs=[SMEM] + [VMEM] * 2 + [ANY] * len(buffers) + [VMEM] * (2 + len(payloads)),
-        out_specs=[VMEM] * 4,
+        in_specs=[SMEM] + [VMEM] * 2 + [ANY] * len(buffers) + [VMEM] * (1 + len(payloads)),
+        out_specs=[VMEM] * 3,
         scratch_shapes=[
             pltpu.VMEM((behind, rows, feature), jnp.bfloat16),
             pltpu.VMEM((chips, SLOTS, edge), jnp.int32),
@@ -242,11 +253,11 @@
             pltpu.SemaphoreType.DMA((chips,)),
             pltpu.SemaphoreType.DMA((behind, groups)),
         ],
-        input_output_aliases={2: 3},
+        input_output_aliases={2: 2},
         compiler_params=pltpu.CompilerParams(vmem_limit_bytes=LIMIT),
         cost_estimate=pl.CostEstimate(flops=0, bytes_accessed=1_000_000, transcendentals=0),
-        name="late_tiles_and_grad",
-    )(place, adjoint, total, *buffers, *payloads, *inputs)
+        name="late_tiles_and_rows",
+    )(place, adjoint, total, *buffers, *payloads, weights)
 
 
 def turn_kernel(*refs):
@@ -267,35 +278,72 @@
     )(*arrays)
 
 
-def rows_kernel(groups, relations, far, place_ref, summed, weights_ref, out):
-    group, core = place_ref[1], place_ref[2]
-    piece = summed.shape[2] // groups
-    value = None
-    for r in range(relations):
-        term = lax.dot_general(
-            summed[core ^ far, r],
-            weights_ref[r],
-            (((1,), (1,)), ((), ())),
-            preferred_element_type=jnp.float32,
-        )
-        value = term if value is None else value + term
-    for q in range(groups):
-        out[group ^ q] = value[q * piece : (q + 1) * piece].astype(out.dtype)
-
-
-def row_terms(place, summed, weights, groups, far, dtype):
-    _, relations, rows, feature = summed.shape
+def rows_kernel(groups, place_ref, summed, weights_ref, far_ref, kept, sent):
+    half = groups // 2
+    for spot, value in multiply_rows(place_ref, summed, weights_ref, groups, 0):
+        value += far_ref[spot].astype(jnp.float32)
+
+        @pl.when(spot < half)
+        def _():
+            kept[spot] = value
+
+        @pl.when(spot >= half)
+        def _():
+            sent[spot - half] = value.astype(sent.dtype)
+
+
+def row_terms(place, summed, weights, far):
+    groups, piece, feature = far.shape
+    shape = (groups // 2, piece, feature)
     return pl.pallas_call(
-        functools.partial(rows_kernel, groups, relations, far),
-        out_shape=jax.ShapeDtypeStruct((groups, rows // groups, feature), dtype),
-        in_specs=[SMEM, VMEM, VMEM],
-        out_specs=VMEM,
+        functools.partial(rows_kernel, groups),
+        out_shape=[
+            jax.ShapeDtypeStruct(shape, jnp.float32),
+            jax.ShapeDtypeStruct(shape, jnp.bfloat16),
+        ],
+        in_specs=[SMEM, VMEM, VMEM, VMEM],
+        out_specs=[VMEM] * 2,
         compiler_params=pltpu.CompilerParams(vmem_limit_bytes=LIMIT),
         cost_estimate=pl.CostEstimate(
-            flops=4 * rows * feature * feature, bytes_accessed=4_000_000, transcendentals=0
+            flops=2 * summed.size * feature, bytes_accessed=4_000_000, transcendentals=0
         ),
         name="row_terms",
-    )(place, summed, weights)
+    )(place, summed, weights, far)
+
+
+def grad_kernel(chips, place_ref, summed, near_ref, far_ref, grad_far, grad_own):
+    chip, core = place_ref[0], place_ref[2]
+    _, relations, _, feature = summed.shape
+    share = feature // (chips * CORES)
+    for r in range(relations):
+        grad = jnp.dot(near_ref[...], summed[core, r], preferred_element_type=jnp.float32)
+        grad += jnp.dot(far_ref[...], summed[1 - core, r], preferred_element_type=jnp.float32)
+        for far in range(CORES):
+            out = grad_far if far else grad_own
+            for c in range(chips):
+                for h in range(CORES):
+                    slab = grad[(c * CORES + h) * share : (c * CORES + h + 1) * share]
+
+                    @pl.when(h == (core ^ far))
+                    def _():
+                        out[chip ^ c, r] = slab.astype(out.dtype)
+
+
+def grad_terms(place, summed, near, far, chips):
+    _, relations, rows, feature = summed.shape
+    shape = (chips, relations, feature // (chips * CORES), feature)
+    return pl.pallas_call(
+        functools.partial(grad_kernel, chips),
+        out_shape=[
+            jax.ShapeDtypeStruct(shape, jnp.bfloat16),
+            jax.ShapeDtypeStruct(shape, jnp.float32),
+        ],
+        in_specs=[SMEM, VMEM, VMEM, VMEM],
+        out_specs=[VMEM] * 2,
+        compiler_params=pltpu.CompilerParams(vmem_limit_bytes=LIMIT),
+        cost_estimate=pl.CostEstimate(flops=0, bytes_accessed=1_000_000, transcendentals=0),
+        name="grad_terms",
+    )(place, summed, near, far)
 
 
 def plane_masks(groups, core):
@@ -367,8 +415,8 @@
     first = [head, far] + [by_chip[j] for j in levels[0][1:]]
     body = to_chip(after(placed[2], *first), mid)
     payloads = [placed[0], head, body]
-    for value, (j, _, _) in list(zip(placed, parts, strict=True))[3:]:
-        payloads.append(to_chip(after(value, *first, *([body] if j == 1 else [])), j))
+    for value, (j, _, _) in list(zip(placed, parts, strict=True))[3:-1]:
+        payloads.append(to_chip(after(value, *first), j))
     for level in levels[1:]:
         for j in level:
             bit = j & -j
@@ -384,6 +432,9 @@
         for step in range(steps):
             if n:
                 merged = jnp.concatenate([value for value, _ in held]) if step else held[0][0]
+                if n == 1 and step == steps - 1:
+                    payloads.append(to_chip(after(placed[-1], merged), 1))
+                    merged = after(merged, body)
                 held = [(merged, sum((origins for _, origins in held), ()))]
             masks = [plane_masks(groups, c)[step] for c in range(CORES)]
             held = held + [
@@ -393,20 +444,20 @@
         for value, origins in held:
             buffers.append(value)
             segments.append((level, origins))
-    near, far = turned(near, far)
     sizes = (chips, groups, blocks, relations)
     early = [i for i, (j, _, _) in enumerate(parts) if j in (0, mid)]
     late = [i for i in range(len(parts)) if i not in early][::-1]
     split = sum(level == levels[0] for level, _ in segments)
+    near, far = turned(near, far)
     adjoint, total = early_tiles(
         tuple(parts[i] for i in early),
         segments[:split],
-        place,
+        after(place, near, far),
         buffers[:split],
         [payloads[i] for i in early],
         sizes,
     )
-    grad_far, grad_own, summed, _ = late_tiles_and_grad(
+    rows_far, summed, _ = late_tiles_and_rows(
         tuple(parts[i] for i in late),
         sorted(levels[0]),
         segments[split:],
@@ -415,28 +466,27 @@
         total,
         buffers[split:],
         [payloads[i] for i in late],
-        [near, far],
+        rel_weights,
         sizes,
     )
+    rows_far = across(rows_far, "node", nodes, 1)
+    sums, passed = row_terms(place, summed, rel_weights, rows_far)
+    for step in range(steps):
+        if step:
+            half = sums.shape[0] // 2
+            sums, passed = sums[:half], sums[half:].astype(jnp.bfloat16)
+        sums = sums + in_plane(passed, step).astype(jnp.float32)
+    d_source = sums[0] + jnp.einsum(
+        "vj,ij->vi", own, self_weight, preferred_element_type=jnp.float32
+    )
+
+    grad_far, grad_own = grad_terms(place, summed, near, far, chips)
     grad_far = across(grad_far, "node", nodes, 1)
-    rows_far = row_terms(place, summed, rel_weights, groups, 1, jnp.bfloat16)
-    rows_far = across(rows_far, "node", nodes, 1)
-    rows_own = row_terms(place, summed, rel_weights, groups, 0, jnp.float32)
     grad = grad_own + grad_far.astype(jnp.float32)
     others = [to_chip(grad[j].astype(jnp.bfloat16), j) for j in range(1, chips)]
     rel_weight_grad = grad[0]
     for other in others:
         rel_weight_grad += other.astype(jnp.float32)
-
-    totals = rows_own + rows_far.astype(jnp.float32)
-    others = [
-        across(totals[m].astype(jnp.bfloat16), "rel", groups, m) for m in range(1, groups)
-    ]
-    d_source = totals[0] + jnp.einsum(
-        "vj,ij->vi", own, self_weight, preferred_element_type=jnp.float32
-    )
-    for other in others:
-        d_source += other.astype(jnp.float32)
     return rel_weight_grad, d_source.astype(jnp.bfloat16)[None]
 
 

time: 100 us -> 96.9 us (0.969)
  starting transfers between devices: 27.8 us -> 25.1 us
    ppermute x16 -> x13, waiting for transfers between devices: 46.4 us -> 37.3 us  [across(): return lax.ppermute(value, axis, [(i, i ^ mask) for i in range(size)])]
    ppermute x5 -> x7, waiting for transfers between devices: 2.31 us -> 10.6 us  [in_plane(): return lax.ppermute(value, ('rel', 'node'), pairs)]
    ppermute x16 -> x13, starting transfers between devices: 20.9 us -> 16.4 us  [across(): return lax.ppermute(value, axis, [(i, i ^ mask) for i in range(size)])]
    ppermute x5 -> x7, starting transfers between devices: 6.99 us -> 8.69 us  [in_plane(): return lax.ppermute(value, ('rel', 'node'), pairs)]
  transfers between devices with their start and end apart: 21 -> 20, of which waited for: 11 -> 11; matrix products, arithmetic and copies ran while one was open for 4% -> 3% of each run, Pallas kernels for 11% -> 13%
where the time goes in v4:
time: 96.9 us; the launch traced here: 96.7 us
  waiting for transfers between devices  48 us (50%)
  starting transfers between devices  25.1 us (26%)
  Pallas kernels  17.4 us (18%)
  other arithmetic  3.78 us (4%)
  local copies, waits for them, and re-layouts  1.39 us (1%)
    ppermute x13, waiting for transfers between devices, across(): return lax.ppermute(value, axis, [(i, i ^ mask) for i in range(size)])  37.3 us
    ppermute x13, starting transfers between devices, across(): return lax.ppermute(value, axis, [(i, i ^ mask) for i in range(size)])  16.4 us
    ppermute x7, waiting for transfers between devices, in_plane(): return lax.ppermute(value, ('rel', 'node'), pairs)  10.6 us
    ppermute x7, starting transfers between devices, in_plane(): return lax.ppermute(value, ('rel', 'node'), pairs)  8.69 us
    pallas_call x1, Pallas kernels, late_tiles_and_rows(): pl.pallas_call(functools.partial(late_kernel, parts, held, segments, size...  4.91 us
    pallas_call x1, Pallas kernels, early_tiles(): pl.pallas_call(functools.partial(early_kernel, parts, segments, groups),...  3.8 us
    pallas_call x1, Pallas kernels, grad_terms(): pl.pallas_call(functools.partial(grad_kernel, chips), out_shape=[jax.Shap...  3.2 us
    pallas_call x1, Pallas kernels, place_tiles(): pl.pallas_call(functools.partial(place_kernel, parts, chips, blocks, rela...  2.74 us
  transfers between devices with their start and end apart: 20, of which 11 were waited for; matrix products, arithmetic and copies ran while one was open for 3% of the time, Pallas kernels for 13%

profile of v4, /device:TPU:0, one launch (start us, length us, event | category | flops | bytes accessed | tf_op | source)
XLA Modules:
  0.0 96.7 jit_solution(3209999491421760624)
XLA Ops:
  1.2 2.7 %collective-permute-start.1 = (bf16[256,512]{1,0:T(8,128)(2,1)}, bf16[256,512]{1,0:T(8,128)(2,1)S(1)}, u32[]{:S(2)}, u32[]{:S(2)}) collective-permute-start(bf16[256,512]{1,0:T(8,128)(2,1)} %bitcast.37), channel_id=1, source_target_pairs={{0,2},{1,3},{2,0},{3,1},{4,6},{5,7},{6,4},{7,5},{8,10},{9,11},{10,... | collective-permute-start | bytes 786440 | tf_op jit(solution)/shard_map/ppermute | solution.py:381
  3.8 2.6 %collective-permute-start.2 = (bf16[256,512]{1,0:T(8,128)(2,1)}, bf16[256,512]{1,0:T(8,128)(2,1)S(1)}, u32[]{:S(2)}, u32[]{:S(2)}) collective-permute-start(bf16[256,512]{1,0:T(8,128)(2,1)} %bitcast.38), channel_id=1, source_target_pairs={{0,4},{1,5},{2,6},{3,7},{4,0},{5,1},{6,2},{7,3},{8,12},{9,13},{10,... | collective-permute-start | bytes 786440 | tf_op jit(solution)/shard_map/ppermute | solution.py:381
  8.4 2.7 %place_tiles.1 = (bf16[2064,128]{1,0:T(8,128)(2,1)S(1)}, bf16[400,128]{1,0:T(8,128)(2,1)S(1)}, bf16[1664,128]{1,0:T(8,128)(2,1)S(1)}, bf16[2064,128]{1,0:T(8,128)(2,1)S(1)}, bf16[2064,128]{1,0:T(8,128)(2,1)S(1)}) custom-call(s32[4,32]{1,0:T(4,128)S(1)} %pad_add_fusion.refs_0_, bf16[32,128,128]{2,1,0:T(8,128)(2,1)S(1)} %bitcast.34, ...), custom_call_target="tpu_custom_call" | custom-call | bytes 4000000 | tf_op jit(solution)/shard_map/place_tiles/pallas_call | solution.py:73
  11.6 4.8 %collective-permute-done.1 = bf16[256,512]{1,0:T(8,128)(2,1)S(1)} collective-permute-done((bf16[256,512]{1,0:T(8,128)(2,1)}, bf16[256,512]{1,0:T(8,128)(2,1)S(1)}, u32[]{:S(2)}, u32[]{:S(2)}) %collective-permute-start.1) | collective-permute-done | bytes 262176 | tf_op jit(solution)/shard_map/ppermute | solution.py:381
  16.4 4.8 %collective-permute-done.2 = bf16[256,512]{1,0:T(8,128)(2,1)S(1)} collective-permute-done((bf16[256,512]{1,0:T(8,128)(2,1)}, bf16[256,512]{1,0:T(8,128)(2,1)S(1)}, u32[]{:S(2)}, u32[]{:S(2)}) %collective-permute-start.2) | collective-permute-done | bytes 262176 | tf_op jit(solution)/shard_map/ppermute | solution.py:381
  23.4 1.5 %collective-permute-start.4 = (bf16[768,512]{1,0:T(8,128)(2,1)S(1)}, bf16[768,512]{1,0:T(8,128)(2,1)S(1)}, u32[]{:S(2)}, u32[]{:S(2)}) collective-permute-start(bf16[768,512]{1,0:T(8,128)(2,1)S(1)} %pad_maximum_fusion.refs_0_), channel_id=1, source_target_pairs={{0,8},{1,17},{2,10},{3,19},{4,12},{5,21},{6,14},{7,23},{8,0},{9,25... | collective-permute-start | bytes 2359304 | tf_op jit(solution)/shard_map/ppermute | solution.py:392
  24.9 3.0 %collective-permute-start.7 = (bf16[1664,128]{1,0:T(8,128)(2,1)S(1)}, bf16[1664,128]{1,0:T(8,128)(2,1)S(1)}, u32[]{:S(2)}, u32[]{:S(2)}) collective-permute-start(bf16[1664,128]{1,0:T(8,128)(2,1)S(1)} %get-tuple-element.31), channel_id=1, source_target_pairs={{0,4},{1,5},{2,6},{3,7},{4,0},{5,1},{6,2},{7,3},{8,12},{9,13},{10,... | collective-permute-start | bytes 1277960 | tf_op jit(solution)/shard_map/ppermute | solution.py:381
  27.9 9.8 %collective-permute-done.8 = bf16[256,512]{1,0:T(8,128)(2,1)S(1)} collective-permute-done((bf16[256,512]{1,0:T(8,128)(2,1)S(1)}, bf16[256,512]{1,0:T(8,128)(2,1)S(1)}, u32[]{:S(2)}, u32[]{:S(2)}) %collective-permute-start.8) | collective-permute-done | bytes 262176 | tf_op jit(solution)/shard_map/ppermute | solution.py:381
  37.6 1.5 %collective-permute-start.9 = (bf16[256,512]{1,0:T(8,128)(2,1)S(1)}, bf16[256,512]{1,0:T(8,128)(2,1)S(1)}, u32[]{:S(2)}, u32[]{:S(2)}) collective-permute-start(bf16[256,512]{1,0:T(8,128)(2,1)S(1)} %collective-permute-done.8), channel_id=1, source_target_pairs={{0,8},{1,17},{2,10},{3,19},{4,12},{5,21},{6,14},{7,23},{8,0},{9,25... | collective-permute-start | bytes 786440 | tf_op jit(solution)/shard_map/ppermute | solution.py:392
  39.6 1.5 %collective-permute-start.6 = (bf16[768,512]{1,0:T(8,128)(2,1)S(1)}, bf16[768,512]{1,0:T(8,128)(2,1)S(1)}, u32[]{:S(2)}, u32[]{:S(2)}) collective-permute-start(bf16[768,512]{1,0:T(8,128)(2,1)S(1)} %collective-permute-done.4.refs_1_), channel_id=1, source_target_pairs={{0,16},{1,9},{2,18},{3,11},{4,20},{5,13},{6,22},{7,15},{8,24},{9,1... | collective-permute-start | bytes 2359304 | tf_op jit(solution)/shard_map/ppermute | solution.py:392
  41.2 2.0 %collective-permute-start.12 = (bf16[2064,128]{1,0:T(8,128)(2,1)S(1)}, bf16[2064,128]{1,0:T(8,128)(2,1)S(1)}, u32[]{:S(2)}, u32[]{:S(2)}) collective-permute-start(bf16[2064,128]{1,0:T(8,128)(2,1)S(1)} %get-tuple-element.39), channel_id=1, source_target_pairs={{0,6},{1,7},{2,4},{3,5},{4,2},{5,3},{6,0},{7,1},{8,14},{9,15},{10,... | collective-permute-start | bytes 1585160 | tf_op jit(solution)/shard_map/ppermute | solution.py:381
  43.2 3.7 %collective-permute-done.9 = bf16[256,512]{1,0:T(8,128)(2,1)S(1)} collective-permute-done((bf16[256,512]{1,0:T(8,128)(2,1)S(1)}, bf16[256,512]{1,0:T(8,128)(2,1)S(1)}, u32[]{:S(2)}, u32[]{:S(2)}) %collective-permute-start.9) | collective-permute-done | bytes 262176 | tf_op jit(solution)/shard_map/ppermute | solution.py:392
  47.0 12.1 %collective-permute-done.7.refs_6_ = bf16[1664,128]{1,0:T(8,128)(2,1)S(1)} collective-permute-done((bf16[1664,128]{1,0:T(8,128)(2,1)S(1)}, bf16[1664,128]{1,0:T(8,128)(2,1)S(1)}, u32[]{:S(2)}, u32[]{:S(2)}) %collective-permute-start.7) | collective-permute-done | bytes 426016 | tf_op jit(solution)/shard_map/ppermute | solution.py:381
  59.1 1.4 %collective-permute-start.10 = (bf16[512,512]{1,0:T(8,128)(2,1)S(1)}, bf16[512,512]{1,0:T(8,128)(2,1)S(1)}, u32[]{:S(2)}, u32[]{:S(2)}) collective-permute-start(bf16[512,512]{1,0:T(8,128)(2,1)S(1)} %constant_dynamic-update-slice_fusion.refs_0_), channel_id=1, source_target_pairs={{0,16},{1,9},{2,18},{3,11},{4,20},{5,13},{6,22},{7,15},{8,24},{9,1... | collective-permute-start | bytes 1572872 | tf_op jit(solution)/shard_map/ppermute | solution.py:392
  61.2 3.8 %early_tiles.1 = (bf16[3,1024,512]{2,1,0:T(8,128)(2,1)S(1)}, f32[32,128,512]{2,1,0:T(8,128)S(1)}) custom-call(s32[3]{0:T(128)S(1)} %pad_add_fusion.1.refs_2_.place_ref, bf16[768,512]{1,0:T(8,128)(2,1)S(1)} %pad_maximum_fusion.refs_0_, bf16[768,512]{1,0:T(8,128)(2,1)S(1)} %collective-permute-done.4.refs_1_, ...), custom_call_target="tpu_custom_call" | custom-call | bytes 1000000 | tf_op jit(solution)/shard_map/early_tiles/pallas_call | solution.py:165
  65.0 3.3 %collective-permute-done.10.refs_1_ = bf16[512,512]{1,0:T(8,128)(2,1)S(1)} collective-permute-done((bf16[512,512]{1,0:T(8,128)(2,1)S(1)}, bf16[512,512]{1,0:T(8,128)(2,1)S(1)}, u32[]{:S(2)}, u32[]{:S(2)}) %collective-permute-start.10) | collective-permute-done | bytes 524320 | tf_op jit(solution)/shard_map/ppermute | solution.py:392
  69.1 4.9 %late_tiles_and_rows.1 = (bf16[4,256,512]{2,1,0:T(8,128)(2,1)S(1)}, bf16[2,2,1024,512]{3,2,1,0:T(8,128)(2,1)S(1)}, f32[32,128,512]{2,1,0:T(8,128)S(1)}) custom-call(s32[3]{0:T(128)S(1)} %pad_add_fusion.1.refs_2_.place_ref, bf16[3,1024,512]{2,1,0:T(8,128)(2,1)S(1)} %get-tuple-element.32.adjoint, ...), custom_call_target="tpu_custom_call", output_to_operand_aliasing={{2}: (2, {})} | custom-call | bytes 1000000 | tf_op jit(solution)/shard_map/late_tiles_and_rows/pallas_call | solution.py:240
  74.1 3.2 %grad_terms.1 = (bf16[4,2,64,512]{3,2,1,0:T(8,128)(2,1)S(1)}, f32[4,2,64,512]{3,2,1,0:T(8,128)S(1)}) custom-call(s32[3]{0:T(128)S(1)} %pad_add_fusion.1.refs_2_.place_ref, bf16[2,2,1024,512]{3,2,1,0:T(8,128)(2,1)S(1)} %get-tuple-element.40.summed, bf16[512,1024]{1,0:T(8,128)(2,1)S(1)} %get-tuple-element.24.near_ref, ...), custom_call_target="tpu_custom_call" | custom-call | bytes 1000000 | tf_op jit(solution)/shard_map/grad_terms/pallas_call | solution.py:335
  77.9 2.1 %row_terms.1 = (f32[2,256,512]{2,1,0:T(8,128)S(1)}, bf16[2,256,512]{2,1,0:T(8,128)(2,1)S(1)}) custom-call(s32[3]{0:T(128)S(1)} %pad_add_fusion.1.refs_2_.place_ref, bf16[2,2,1024,512]{3,2,1,0:T(8,128)(2,1)S(1)} %get-tuple-element.40.summed, bf16[2,512,512]{2,1,0:T(8,128)(2,1)S(1)} %copy-done.3, bf16[4,256,512]{2,1,0:T(8,128)(2,1)S(1)} %collective-permute-done.17.far_ref), custom_call_target="tpu_custom_call" | custom-call | flops 2147483648 | bytes 4000000 | tf_op jit(solution)/shard_map/row_terms/pallas_call | solution.py:298
  80.0 1.6 %collective-permute-start.18 = (bf16[2,256,512]{2,1,0:T(8,128)(2,1)S(1)}, bf16[2,256,512]{2,1,0:T(8,128)(2,1)S(1)}, u32[]{:S(2)}, u32[]{:S(2)}) collective-permute-start(bf16[2,256,512]{2,1,0:T(8,128)(2,1)S(1)} %get-tuple-element.45), channel_id=1, source_target_pairs={{0,8},{1,17},{2,10},{3,19},{4,12},{5,21},{6,14},{7,23},{8,0},{9,25... | collective-permute-start | bytes 1572872 | tf_op jit(solution)/shard_map/ppermute | solution.py:392
  82.5 1.7 %collective-permute-start.15 = (bf16[2,64,512]{2,1,0:T(8,128)(2,1)S(1)}, bf16[2,64,512]{2,1,0:T(8,128)(2,1)S(1)}, u32[]{:S(2)}, u32[]{:S(2)}) collective-permute-start(bf16[2,64,512]{2,1,0:T(8,128)(2,1)S(1)} %get-tuple-element.50), channel_id=1, source_target_pairs={{0,4},{1,5},{2,6},{3,7},{4,0},{5,1},{6,2},{7,3},{8,12},{9,13},{10,... | collective-permute-start | bytes 393224 | tf_op jit(solution)/shard_map/ppermute | solution.py:381
  84.2 2.1 %collective-permute-start.16 = (bf16[2,64,512]{2,1,0:T(8,128)(2,1)S(1)}, bf16[2,64,512]{2,1,0:T(8,128)(2,1)S(1)}, u32[]{:S(2)}, u32[]{:S(2)}) collective-permute-start(bf16[2,64,512]{2,1,0:T(8,128)(2,1)S(1)} %get-tuple-element.49), channel_id=1, source_target_pairs={{0,6},{1,7},{2,4},{3,5},{4,2},{5,3},{6,0},{7,1},{8,14},{9,15},{10,... | collective-permute-start | bytes 393224 | tf_op jit(solution)/shard_map/ppermute | solution.py:381
  86.3 2.9 %collective-permute-done.18 = bf16[2,256,512]{2,1,0:T(8,128)(2,1)S(1)} collective-permute-done((bf16[2,256,512]{2,1,0:T(8,128)(2,1)S(1)}, bf16[2,256,512]{2,1,0:T(8,128)(2,1)S(1)}, u32[]{:S(2)}, u32[]{:S(2)}) %collective-permute-start.18) | collective-permute-done | bytes 524320 | tf_op jit(solution)/shard_map/ppermute | solution.py:392
  90.5 3.8 %collective-permute-done.15 = bf16[2,64,512]{2,1,0:T(8,128)(2,1)S(1)} collective-permute-done((bf16[2,64,512]{2,1,0:T(8,128)(2,1)S(1)}, bf16[2,64,512]{2,1,0:T(8,128)(2,1)S(1)}, u32[]{:S(2)}, u32[]{:S(2)}) %collective-permute-start.15) | collective-permute-done | bytes 131104 | tf_op jit(solution)/shard_map/ppermute | solution.py:381
  (44 shorter events, 12.4 us)
Async XLA Ops:
  0.6 89.5 %copy-start = (bf16[512,512]{1,0:T(8,128)(2,1)S(1)}, bf16[512,512]{1,0:T(8,128)(2,1)}, u32[]{:S(2)}) copy-start(bf16[512,512]{1,0:T(8,128)(2,1)} %param.12) | copy-start | bytes 1572868
  0.6 22.7 %collective-permute-start = (bf16[1024,512]{1,0:T(8,128)(2,1)}, bf16[1024,512]{1,0:T(8,128)(2,1)S(1)}, u32[]{:S(2)}, u32[]{:S(2)}) collective-permute-start(bf16[1024,512]{1,0:T(8,128)(2,1)} %bitcast.35), channel_id=1, source_target_pairs={{0,1},{1,0},{2,3},{3,2},{4,5},{5,4},{6,7},{7,6},{8,9},{9,8},{10,11... | collective-permute-start | bytes 3145736 | tf_op jit(solution)/shard_map/ppermute | solution.py:381
  1.2 15.2 %collective-permute-start.1 = (bf16[256,512]{1,0:T(8,128)(2,1)}, bf16[256,512]{1,0:T(8,128)(2,1)S(1)}, u32[]{:S(2)}, u32[]{:S(2)}) collective-permute-start(bf16[256,512]{1,0:T(8,128)(2,1)} %bitcast.37), channel_id=1, source_target_pairs={{0,2},{1,3},{2,0},{3,1},{4,6},{5,7},{6,4},{7,5},{8,10},{9,11},{10,... | collective-permute-start | bytes 786440 | tf_op jit(solution)/shard_map/ppermute | solution.py:381
  3.8 17.4 %collective-permute-start.2 = (bf16[256,512]{1,0:T(8,128)(2,1)}, bf16[256,512]{1,0:T(8,128)(2,1)S(1)}, u32[]{:S(2)}, u32[]{:S(2)}) collective-permute-start(bf16[256,512]{1,0:T(8,128)(2,1)} %bitcast.38), channel_id=1, source_target_pairs={{0,4},{1,5},{2,6},{3,7},{4,0},{5,1},{6,2},{7,3},{8,12},{9,13},{10,... | collective-permute-start | bytes 786440 | tf_op jit(solution)/shard_map/ppermute | solution.py:381
  7.2 1.2 %copy-start.1 = (bf16[1,32,128,128]{3,2,1,0:T(8,128)(2,1)S(1)}, bf16[1,32,128,128]{3,2,1,0:T(8,128)(2,1)}, u32[]{:S(2)}) copy-start(bf16[1,32,128,128]{3,2,1,0:T(8,128)(2,1)} %param.13) | copy-start | bytes 3145732
  11.2 49.3 %copy-start.2 = (bf16[1,1024,512]{2,1,0:T(8,128)(2,1)S(1)}, bf16[1,1024,512]{2,1,0:T(8,128)(2,1)}, u32[]{:S(2)}) copy-start(bf16[1,1024,512]{2,1,0:T(8,128)(2,1)} %param.10) | copy-start | bytes 3145732
  11.2 12.2 %collective-permute-start.3 = (bf16[400,128]{1,0:T(8,128)(2,1)S(1)}, bf16[400,128]{1,0:T(8,128)(2,1)S(1)}, u32[]{:S(2)}, u32[]{:S(2)}) collective-permute-start(bf16[400,128]{1,0:T(8,128)(2,1)S(1)} %get-tuple-element.27), channel_id=1, source_target_pairs={{0,4},{1,5},{2,6},{3,7},{4,0},{5,1},{6,2},{7,3},{8,12},{9,13},{10,... | collective-permute-start | bytes 307208 | tf_op jit(solution)/shard_map/ppermute | solution.py:381
  23.4 16.3 %collective-permute-start.4 = (bf16[768,512]{1,0:T(8,128)(2,1)S(1)}, bf16[768,512]{1,0:T(8,128)(2,1)S(1)}, u32[]{:S(2)}, u32[]{:S(2)}) collective-permute-start(bf16[768,512]{1,0:T(8,128)(2,1)S(1)} %pad_maximum_fusion.refs_0_), channel_id=1, source_target_pairs={{0,8},{1,17},{2,10},{3,19},{4,12},{5,21},{6,14},{7,23},{8,0},{9,25... | collective-permute-start | bytes 2359304 | tf_op jit(solution)/shard_map/ppermute | solution.py:392
  24.9 12.8 %collective-permute-start.8 = (bf16[256,512]{1,0:T(8,128)(2,1)S(1)}, bf16[256,512]{1,0:T(8,128)(2,1)S(1)}, u32[]{:S(2)}, u32[]{:S(2)}) collective-permute-start(bf16[256,512]{1,0:T(8,128)(2,1)S(1)} %collective-permute-done.2), channel_id=1, source_target_pairs={{0,2},{1,3},{2,0},{3,1},{4,6},{5,7},{6,4},{7,5},{8,10},{9,11},{10,... | collective-permute-start | bytes 786440 | tf_op jit(solution)/shard_map/ppermute | solution.py:381
  24.9 34.2 %collective-permute-start.7 = (bf16[1664,128]{1,0:T(8,128)(2,1)S(1)}, bf16[1664,128]{1,0:T(8,128)(2,1)S(1)}, u32[]{:S(2)}, u32[]{:S(2)}) collective-permute-start(bf16[1664,128]{1,0:T(8,128)(2,1)S(1)} %get-tuple-element.31), channel_id=1, source_target_pairs={{0,4},{1,5},{2,6},{3,7},{4,0},{5,1},{6,2},{7,3},{8,12},{9,13},{10,... | collective-permute-start | bytes 1277960 | tf_op jit(solution)/shard_map/ppermute | solution.py:381
  37.6 9.2 %collective-permute-start.9 = (bf16[256,512]{1,0:T(8,128)(2,1)S(1)}, bf16[256,512]{1,0:T(8,128)(2,1)S(1)}, u32[]{:S(2)}, u32[]{:S(2)}) collective-permute-start(bf16[256,512]{1,0:T(8,128)(2,1)S(1)} %collective-permute-done.8), channel_id=1, source_target_pairs={{0,8},{1,17},{2,10},{3,19},{4,12},{5,21},{6,14},{7,23},{8,0},{9,25... | collective-permute-start | bytes 786440 | tf_op jit(solution)/shard_map/ppermute | solution.py:392
  39.1 22.0 %collective-permute-start.5 = (bf16[768,512]{1,0:T(8,128)(2,1)S(1)}, bf16[768,512]{1,0:T(8,128)(2,1)S(1)}, u32[]{:S(2)}, u32[]{:S(2)}) collective-permute-start(bf16[768,512]{1,0:T(8,128)(2,1)S(1)} %pad_maximum_fusion.refs_0_), channel_id=1, source_target_pairs={{0,16},{1,9},{2,18},{3,11},{4,20},{5,13},{6,22},{7,15},{8,24},{9,1... | collective-permute-start | bytes 2359304 | tf_op jit(solution)/shard_map/ppermute | solution.py:392
  39.6 21.5 %collective-permute-start.6 = (bf16[768,512]{1,0:T(8,128)(2,1)S(1)}, bf16[768,512]{1,0:T(8,128)(2,1)S(1)}, u32[]{:S(2)}, u32[]{:S(2)}) collective-permute-start(bf16[768,512]{1,0:T(8,128)(2,1)S(1)} %collective-permute-done.4.refs_1_), channel_id=1, source_target_pairs={{0,16},{1,9},{2,18},{3,11},{4,20},{5,13},{6,22},{7,15},{8,24},{9,1... | collective-permute-start | bytes 2359304 | tf_op jit(solution)/shard_map/ppermute | solution.py:392
  41.2 23.8 %collective-permute-start.12 = (bf16[2064,128]{1,0:T(8,128)(2,1)S(1)}, bf16[2064,128]{1,0:T(8,128)(2,1)S(1)}, u32[]{:S(2)}, u32[]{:S(2)}) collective-permute-start(bf16[2064,128]{1,0:T(8,128)(2,1)S(1)} %get-tuple-element.39), channel_id=1, source_target_pairs={{0,6},{1,7},{2,4},{3,5},{4,2},{5,3},{6,0},{7,1},{8,14},{9,15},{10,... | collective-permute-start | bytes 1585160 | tf_op jit(solution)/shard_map/ppermute | solution.py:381
  46.9 22.2 %collective-permute-start.11 = (bf16[2064,128]{1,0:T(8,128)(2,1)S(1)}, bf16[2064,128]{1,0:T(8,128)(2,1)S(1)}, u32[]{:S(2)}, u32[]{:S(2)}) collective-permute-start(bf16[2064,128]{1,0:T(8,128)(2,1)S(1)} %get-tuple-element.37), channel_id=1, source_target_pairs={{0,2},{1,3},{2,0},{3,1},{4,6},{5,7},{6,4},{7,5},{8,10},{9,11},{10,... | collective-permute-start | bytes 1585160 | tf_op jit(solution)/shard_map/ppermute | solution.py:381
  59.1 9.2 %collective-permute-start.10 = (bf16[512,512]{1,0:T(8,128)(2,1)S(1)}, bf16[512,512]{1,0:T(8,128)(2,1)S(1)}, u32[]{:S(2)}, u32[]{:S(2)}) collective-permute-start(bf16[512,512]{1,0:T(8,128)(2,1)S(1)} %constant_dynamic-update-slice_fusion.refs_0_), channel_id=1, source_target_pairs={{0,16},{1,9},{2,18},{3,11},{4,20},{5,13},{6,22},{7,15},{8,24},{9,1... | collective-permute-start | bytes 1572872 | tf_op jit(solution)/shard_map/ppermute | solution.py:392
  61.2 7.9 %copy-start.3 = (bf16[2,512,512]{2,1,0:T(8,128)(2,1)S(1)}, bf16[2,512,512]{2,1,0:T(8,128)(2,1)}, u32[]{:S(2)}) copy-start(bf16[2,512,512]{2,1,0:T(8,128)(2,1)} %weights_ref.1) | copy-start | bytes 3145732
  74.0 3.9 %collective-permute-start.17 = (bf16[4,256,512]{2,1,0:T(8,128)(2,1)S(1)}, bf16[4,256,512]{2,1,0:T(8,128)(2,1)S(1)}, u32[]{:S(2)}, u32[]{:S(2)}) collective-permute-start(bf16[4,256,512]{2,1,0:T(8,128)(2,1)S(1)} %get-tuple-element.43), channel_id=1, source_target_pairs={{0,1},{1,0},{2,3},{3,2},{4,5},{5,4},{6,7},{7,6},{8,9},{9,8},{10,11... | collective-permute-start | bytes 3145736 | tf_op jit(solution)/shard_map/ppermute | solution.py:381
  77.3 4.2 %collective-permute-start.13 = (bf16[4,2,64,512]{3,2,1,0:T(8,128)(2,1)S(1)}, bf16[4,2,64,512]{3,2,1,0:T(8,128)(2,1)S(1)}, u32[]{:S(2)}, u32[]{:S(2)}) collective-permute-start(bf16[4,2,64,512]{3,2,1,0:T(8,128)(2,1)S(1)} %get-tuple-element.42), channel_id=1, source_target_pairs={{0,1},{1,0},{2,3},{3,2},{4,5},{5,4},{6,7},{7,6},{8,9},{9,8},{10,11... | collective-permute-start | bytes 1572872 | tf_op jit(solution)/shard_map/ppermute | solution.py:381
  80.0 9.2 %collective-permute-start.18 = (bf16[2,256,512]{2,1,0:T(8,128)(2,1)S(1)}, bf16[2,256,512]{2,1,0:T(8,128)(2,1)S(1)}, u32[]{:S(2)}, u32[]{:S(2)}) collective-permute-start(bf16[2,256,512]{2,1,0:T(8,128)(2,1)S(1)} %get-tuple-element.45), channel_id=1, source_target_pairs={{0,8},{1,17},{2,10},{3,19},{4,12},{5,21},{6,14},{7,23},{8,0},{9,25... | collective-permute-start | bytes 1572872 | tf_op jit(solution)/shard_map/ppermute | solution.py:392
  81.8 8.7 %collective-permute-start.14 = (bf16[2,64,512]{2,1,0:T(8,128)(2,1)S(1)}, bf16[2,64,512]{2,1,0:T(8,128)(2,1)S(1)}, u32[]{:S(2)}, u32[]{:S(2)}) collective-permute-start(bf16[2,64,512]{2,1,0:T(8,128)(2,1)S(1)} %get-tuple-element.48), channel_id=1, source_target_pairs={{0,2},{1,3},{2,0},{3,1},{4,6},{5,7},{6,4},{7,5},{8,10},{9,11},{10,... | collective-permute-start | bytes 393224 | tf_op jit(solution)/shard_map/ppermute | solution.py:381
  82.5 11.8 %collective-permute-start.15 = (bf16[2,64,512]{2,1,0:T(8,128)(2,1)S(1)}, bf16[2,64,512]{2,1,0:T(8,128)(2,1)S(1)}, u32[]{:S(2)}, u32[]{:S(2)}) collective-permute-start(bf16[2,64,512]{2,1,0:T(8,128)(2,1)S(1)} %get-tuple-element.50), channel_id=1, source_target_pairs={{0,4},{1,5},{2,6},{3,7},{4,0},{5,1},{6,2},{7,3},{8,12},{9,13},{10,... | collective-permute-start | bytes 393224 | tf_op jit(solution)/shard_map/ppermute | solution.py:381
  84.2 10.1 %collective-permute-start.16 = (bf16[2,64,512]{2,1,0:T(8,128)(2,1)S(1)}, bf16[2,64,512]{2,1,0:T(8,128)(2,1)S(1)}, u32[]{:S(2)}, u32[]{:S(2)}) collective-permute-start(bf16[2,64,512]{2,1,0:T(8,128)(2,1)S(1)} %get-tuple-element.49), channel_id=1, source_target_pairs={{0,6},{1,7},{2,4},{3,5},{4,2},{5,3},{6,0},{7,1},{8,14},{9,15},{10,... | collective-permute-start | bytes 393224 | tf_op jit(solution)/shard_map/ppermute | solution.py:381
  89.4 6.4 %collective-permute-start.19 = (bf16[1,256,512]{2,1,0:T(8,128)(2,1)S(1)}, bf16[1,256,512]{2,1,0:T(8,128)(2,1)S(1)}, u32[]{:S(2)}, u32[]{:S(2)}) collective-permute-start(bf16[1,256,512]{2,1,0:T(8,128)(2,1)S(1)} %slice.54), channel_id=1, source_target_pairs={{0,16},{1,9},{2,18},{3,11},{4,20},{5,13},{6,22},{7,15},{8,24},{9,1... | collective-permute-start | bytes 786440 | tf_op jit(solution)/shard_map/ppermute | solution.py:392
  (1 other events, 1.0 us)

commit v5 on v4

--- a/solution.py
+++ b/solution.py
@@ -122,7 +122,7 @@
 
 def add_tiles(payload, j, first, size, adjoint, total, codes):
     edge = payload.shape[-1]
-    unroll = next(u for u in range(min(size, 8), 0, -1) if size % u == 0)
+    unroll = next(u for u in range(min(size, 16), 0, -1) if size % u == 0)
     if unroll == 1:
         unroll = size
 
@@ -201,24 +201,23 @@
     for h in range(CORES):
         for r in range(relations):
             part = total[pl.ds((h * relations + r) * blocks, blocks)].astype(jnp.bfloat16)
-            summed[h, r] = part.reshape(blocks * edge, part.shape[-1])
+            part = part.reshape(blocks * edge, part.shape[-1])
+            rows, feature = part.shape
+            summed[h * rows : (h + 1) * rows, r * feature : (r + 1) * feature] = part
     for spot, value in multiply_rows(place_ref, summed, weights_ref, groups, 1):
         rows_far[spot] = value.astype(rows_far.dtype)
 
 
 def multiply_rows(place_ref, summed, weights_ref, groups, far):
     group, core = place_ref[1], place_ref[2]
-    piece = summed.shape[2] // groups
+    rows = summed.shape[0] // CORES
+    piece = rows // groups
     steps = groups.bit_length() - 1
-    value = None
-    for r in range(summed.shape[1]):
-        term = lax.dot_general(
-            summed[core ^ far, r],
-            weights_ref[r],
-            (((1,), (1,)), ((), ())),
-            preferred_element_type=jnp.float32,
-        )
-        value = term if value is None else value + term
+    value = jnp.dot(
+        summed[pl.ds(pl.multiple_of((core ^ far) * rows, rows), rows), :],
+        weights_ref[...],
+        preferred_element_type=jnp.float32,
+    )
     pieces = []
     for q in range(groups):
         mask = group ^ q
@@ -241,7 +240,7 @@
         functools.partial(late_kernel, parts, held, segments, sizes),
         out_shape=[
             jax.ShapeDtypeStruct((groups, rows // groups, feature), jnp.bfloat16),
-            jax.ShapeDtypeStruct((CORES, relations, rows, feature), jnp.bfloat16),
+            jax.ShapeDtypeStruct((CORES * rows, relations * feature), jnp.bfloat16),
             jax.ShapeDtypeStruct(total.shape, total.dtype),
         ],
         in_specs=[SMEM] + [VMEM] * 2 + [ANY] * len(buffers) + [VMEM] * (1 + len(payloads)),
@@ -260,22 +259,35 @@
     )(place, adjoint, total, *buffers, *payloads, weights)
 
 
-def turn_kernel(*refs):
-    half = len(refs) // 2
-    for source, target in zip(refs[:half], refs[half:], strict=True):
-        target[...] = source[...].T
-
-
-def turned(*arrays):
+def turn_kernel(place_ref, near_ref, far_ref, weights_ref, inputs, weights):
+    core = place_ref[2]
+    rows, feature = near_ref.shape
+    near, far = near_ref[...].T, far_ref[...].T
+    for c in range(CORES):
+
+        @pl.when(core == c)
+        def _():
+            inputs[:, c * rows : (c + 1) * rows] = near
+            inputs[:, (1 - c) * rows : (2 - c) * rows] = far
+
+    for r in range(weights_ref.shape[0]):
+        weights[r * feature : (r + 1) * feature, :] = weights_ref[r].T
+
+
+def turned(place, near, far, weights):
+    rows, feature = near.shape
     return pl.pallas_call(
         turn_kernel,
-        out_shape=[jax.ShapeDtypeStruct(a.shape[::-1], a.dtype) for a in arrays],
-        in_specs=[VMEM] * len(arrays),
-        out_specs=[VMEM] * len(arrays),
+        out_shape=[
+            jax.ShapeDtypeStruct((feature, CORES * rows), near.dtype),
+            jax.ShapeDtypeStruct((weights.shape[0] * feature, feature), weights.dtype),
+        ],
+        in_specs=[SMEM] + [VMEM] * 3,
+        out_specs=[VMEM] * 2,
         compiler_params=pltpu.CompilerParams(vmem_limit_bytes=LIMIT),
         cost_estimate=pl.CostEstimate(flops=0, bytes_accessed=1_000_000, transcendentals=0),
         name="turn_inputs",
-    )(*arrays)
+    )(place, near, far, weights)
 
 
 def rows_kernel(groups, place_ref, summed, weights_ref, far_ref, kept, sent):
@@ -311,39 +323,40 @@
     )(place, summed, weights, far)
 
 
-def grad_kernel(chips, place_ref, summed, near_ref, far_ref, grad_far, grad_own):
+def grad_kernel(chips, relations, place_ref, summed, inputs_ref, grad_far, grad_own):
     chip, core = place_ref[0], place_ref[2]
-    _, relations, _, feature = summed.shape
+    feature = inputs_ref.shape[0]
     share = feature // (chips * CORES)
+    grad = jnp.dot(inputs_ref[...], summed[...], preferred_element_type=jnp.float32)
     for r in range(relations):
-        grad = jnp.dot(near_ref[...], summed[core, r], preferred_element_type=jnp.float32)
-        grad += jnp.dot(far_ref[...], summed[1 - core, r], preferred_element_type=jnp.float32)
         for far in range(CORES):
             out = grad_far if far else grad_own
             for c in range(chips):
                 for h in range(CORES):
-                    slab = grad[(c * CORES + h) * share : (c * CORES + h + 1) * share]
+                    start = (c * CORES + h) * share
+                    slab = grad[start : start + share, r * feature : (r + 1) * feature]
 
                     @pl.when(h == (core ^ far))
                     def _():
                         out[chip ^ c, r] = slab.astype(out.dtype)
 
 
-def grad_terms(place, summed, near, far, chips):
-    _, relations, rows, feature = summed.shape
+def grad_terms(place, summed, inputs, chips):
+    feature = inputs.shape[0]
+    relations = summed.shape[1] // feature
     shape = (chips, relations, feature // (chips * CORES), feature)
     return pl.pallas_call(
-        functools.partial(grad_kernel, chips),
+        functools.partial(grad_kernel, chips, relations),
         out_shape=[
             jax.ShapeDtypeStruct(shape, jnp.bfloat16),
             jax.ShapeDtypeStruct(shape, jnp.float32),
         ],
-        in_specs=[SMEM, VMEM, VMEM, VMEM],
+        in_specs=[SMEM, VMEM, VMEM],
         out_specs=[VMEM] * 2,
         compiler_params=pltpu.CompilerParams(vmem_limit_bytes=LIMIT),
         cost_estimate=pl.CostEstimate(flops=0, bytes_accessed=1_000_000, transcendentals=0),
         name="grad_terms",
-    )(place, summed, near, far)
+    )(place, summed, inputs)
 
 
 def plane_masks(groups, core):
@@ -448,11 +461,11 @@
     early = [i for i, (j, _, _) in enumerate(parts) if j in (0, mid)]
     late = [i for i in range(len(parts)) if i not in early][::-1]
     split = sum(level == levels[0] for level, _ in segments)
-    near, far = turned(near, far)
+    inputs, weights = turned(place, near, far, rel_weights)
     adjoint, total = early_tiles(
         tuple(parts[i] for i in early),
         segments[:split],
-        after(place, near, far),
+        after(place, inputs, weights),
         buffers[:split],
         [payloads[i] for i in early],
         sizes,
@@ -466,11 +479,11 @@
         total,
         buffers[split:],
         [payloads[i] for i in late],
-        rel_weights,
+        weights,
         sizes,
     )
     rows_far = across(rows_far, "node", nodes, 1)
-    sums, passed = row_terms(place, summed, rel_weights, rows_far)
+    sums, passed = row_terms(place, summed, weights, rows_far)
     for step in range(steps):
         if step:
             half = sums.shape[0] // 2
@@ -480,10 +493,10 @@
         "vj,ij->vi", own, self_weight, preferred_element_type=jnp.float32
     )
 
-    grad_far, grad_own = grad_terms(place, summed, near, far, chips)
+    grad_far, grad_own = grad_terms(place, summed, inputs, chips)
     grad_far = across(grad_far, "node", nodes, 1)
     grad = grad_own + grad_far.astype(jnp.float32)
-    others = [to_chip(grad[j].astype(jnp.bfloat16), j) for j in range(1, chips)]
+    others = [to_chip(grad[j].astype(jnp.bfloat16), j) for j in range(chips - 1, 0, -1)]
     rel_weight_grad = grad[0]
     for other in others:
         rel_weight_grad += other.astype(jnp.float32)

time: 96.9 us -> 96.4 us (level)
    ppermute x7, waiting for transfers between devices: 10.6 us -> 9.22 us  [in_plane(): return lax.ppermute(value, ('rel', 'node'), pairs)]
  transfers between devices with their start and end apart: 20 -> 20, of which waited for: 11 -> 11; matrix products, arithmetic and copies ran while one was open for 3% -> 3% of each run, Pallas kernels for 13% -> 14%
where the time goes in v5:
time: 96.4 us; the launch traced here: 96.2 us
  waiting for transfers between devices  47.2 us (49%)
  starting transfers between devices  25.1 us (26%)
  Pallas kernels  17.6 us (18%)
  other arithmetic  3.78 us (4%)
  local copies, waits for them, and re-layouts  1.34 us (1%)
    ppermute x13, waiting for transfers between devices, across(): return lax.ppermute(value, axis, [(i, i ^ mask) for i in range(size)])  38 us
    ppermute x13, starting transfers between devices, across(): return lax.ppermute(value, axis, [(i, i ^ mask) for i in range(size)])  16.4 us
    ppermute x7, waiting for transfers between devices, in_plane(): return lax.ppermute(value, ('rel', 'node'), pairs)  9.22 us
    ppermute x7, starting transfers between devices, in_plane(): return lax.ppermute(value, ('rel', 'node'), pairs)  8.7 us
    pallas_call x1, Pallas kernels, late_tiles_and_rows(): pl.pallas_call(functools.partial(late_kernel, parts, held, segments, size...  4.58 us
    pallas_call x1, Pallas kernels, early_tiles(): pl.pallas_call(functools.partial(early_kernel, parts, segments, groups),...  3.62 us
    pallas_call x1, Pallas kernels, grad_terms(): pl.pallas_call(functools.partial(grad_kernel, chips, relations), out_shap...  3.09 us
    pallas_call x1, Pallas kernels, place_tiles(): pl.pallas_call(functools.partial(place_kernel, parts, chips, blocks, rela...  2.74 us
  transfers between devices with their start and end apart: 20, of which 11 were waited for; matrix products, arithmetic and copies ran while one was open for 3% of the time, Pallas kernels for 14%

profile of v5, /device:TPU:0, one launch (start us, length us, event | category | flops | bytes accessed | tf_op | source)
XLA Modules:
  0.0 96.2 jit_solution(12879697164203787331)
XLA Ops:
  1.2 2.7 %collective-permute-start.1 = (bf16[256,512]{1,0:T(8,128)(2,1)}, bf16[256,512]{1,0:T(8,128)(2,1)S(1)}, u32[]{:S(2)}, u32[]{:S(2)}) collective-permute-start(bf16[256,512]{1,0:T(8,128)(2,1)} %bitcast.37), channel_id=1, source_target_pairs={{0,2},{1,3},{2,0},{3,1},{4,6},{5,7},{6,4},{7,5},{8,10},{9,11},{10,... | collective-permute-start | bytes 786440 | tf_op jit(solution)/shard_map/ppermute | solution.py:394
  3.8 2.6 %collective-permute-start.2 = (bf16[256,512]{1,0:T(8,128)(2,1)}, bf16[256,512]{1,0:T(8,128)(2,1)S(1)}, u32[]{:S(2)}, u32[]{:S(2)}) collective-permute-start(bf16[256,512]{1,0:T(8,128)(2,1)} %bitcast.38), channel_id=1, source_target_pairs={{0,4},{1,5},{2,6},{3,7},{4,0},{5,1},{6,2},{7,3},{8,12},{9,13},{10,... | collective-permute-start | bytes 786440 | tf_op jit(solution)/shard_map/ppermute | solution.py:394
  8.4 2.7 %place_tiles.1 = (bf16[2064,128]{1,0:T(8,128)(2,1)S(1)}, bf16[400,128]{1,0:T(8,128)(2,1)S(1)}, bf16[1664,128]{1,0:T(8,128)(2,1)S(1)}, bf16[2064,128]{1,0:T(8,128)(2,1)S(1)}, bf16[2064,128]{1,0:T(8,128)(2,1)S(1)}) custom-call(s32[4,32]{1,0:T(4,128)S(1)} %pad_add_fusion.refs_0_, bf16[32,128,128]{2,1,0:T(8,128)(2,1)S(1)} %bitcast.34, ...), custom_call_target="tpu_custom_call" | custom-call | bytes 4000000 | tf_op jit(solution)/shard_map/place_tiles/pallas_call | solution.py:73
  11.6 4.8 %collective-permute-done.1 = bf16[256,512]{1,0:T(8,128)(2,1)S(1)} collective-permute-done((bf16[256,512]{1,0:T(8,128)(2,1)}, bf16[256,512]{1,0:T(8,128)(2,1)S(1)}, u32[]{:S(2)}, u32[]{:S(2)}) %collective-permute-start.1) | collective-permute-done | bytes 262176 | tf_op jit(solution)/shard_map/ppermute | solution.py:394
  16.4 4.8 %collective-permute-done.2 = bf16[256,512]{1,0:T(8,128)(2,1)S(1)} collective-permute-done((bf16[256,512]{1,0:T(8,128)(2,1)}, bf16[256,512]{1,0:T(8,128)(2,1)S(1)}, u32[]{:S(2)}, u32[]{:S(2)}) %collective-permute-start.2) | collective-permute-done | bytes 262176 | tf_op jit(solution)/shard_map/ppermute | solution.py:394
  23.4 1.5 %collective-permute-start.4 = (bf16[768,512]{1,0:T(8,128)(2,1)S(1)}, bf16[768,512]{1,0:T(8,128)(2,1)S(1)}, u32[]{:S(2)}, u32[]{:S(2)}) collective-permute-start(bf16[768,512]{1,0:T(8,128)(2,1)S(1)} %pad_maximum_fusion.refs_0_), channel_id=1, source_target_pairs={{0,8},{1,17},{2,10},{3,19},{4,12},{5,21},{6,14},{7,23},{8,0},{9,25... | collective-permute-start | bytes 2359304 | tf_op jit(solution)/shard_map/ppermute | solution.py:405
  24.9 3.0 %collective-permute-start.7 = (bf16[1664,128]{1,0:T(8,128)(2,1)S(1)}, bf16[1664,128]{1,0:T(8,128)(2,1)S(1)}, u32[]{:S(2)}, u32[]{:S(2)}) collective-permute-start(bf16[1664,128]{1,0:T(8,128)(2,1)S(1)} %get-tuple-element.31), channel_id=1, source_target_pairs={{0,4},{1,5},{2,6},{3,7},{4,0},{5,1},{6,2},{7,3},{8,12},{9,13},{10,... | collective-permute-start | bytes 1277960 | tf_op jit(solution)/shard_map/ppermute | solution.py:394
  27.9 9.8 %collective-permute-done.8 = bf16[256,512]{1,0:T(8,128)(2,1)S(1)} collective-permute-done((bf16[256,512]{1,0:T(8,128)(2,1)S(1)}, bf16[256,512]{1,0:T(8,128)(2,1)S(1)}, u32[]{:S(2)}, u32[]{:S(2)}) %collective-permute-start.8) | collective-permute-done | bytes 262176 | tf_op jit(solution)/shard_map/ppermute | solution.py:394
  37.6 1.5 %collective-permute-start.9 = (bf16[256,512]{1,0:T(8,128)(2,1)S(1)}, bf16[256,512]{1,0:T(8,128)(2,1)S(1)}, u32[]{:S(2)}, u32[]{:S(2)}) collective-permute-start(bf16[256,512]{1,0:T(8,128)(2,1)S(1)} %collective-permute-done.8), channel_id=1, source_target_pairs={{0,8},{1,17},{2,10},{3,19},{4,12},{5,21},{6,14},{7,23},{8,0},{9,25... | collective-permute-start | bytes 786440 | tf_op jit(solution)/shard_map/ppermute | solution.py:405
  39.6 1.5 %collective-permute-start.6 = (bf16[768,512]{1,0:T(8,128)(2,1)S(1)}, bf16[768,512]{1,0:T(8,128)(2,1)S(1)}, u32[]{:S(2)}, u32[]{:S(2)}) collective-permute-start(bf16[768,512]{1,0:T(8,128)(2,1)S(1)} %collective-permute-done.4.refs_1_), channel_id=1, source_target_pairs={{0,16},{1,9},{2,18},{3,11},{4,20},{5,13},{6,22},{7,15},{8,24},{9,1... | collective-permute-start | bytes 2359304 | tf_op jit(solution)/shard_map/ppermute | solution.py:405
  41.2 2.0 %collective-permute-start.12 = (bf16[2064,128]{1,0:T(8,128)(2,1)S(1)}, bf16[2064,128]{1,0:T(8,128)(2,1)S(1)}, u32[]{:S(2)}, u32[]{:S(2)}) collective-permute-start(bf16[2064,128]{1,0:T(8,128)(2,1)S(1)} %get-tuple-element.39), channel_id=1, source_target_pairs={{0,6},{1,7},{2,4},{3,5},{4,2},{5,3},{6,0},{7,1},{8,14},{9,15},{10,... | collective-permute-start | bytes 1585160 | tf_op jit(solution)/shard_map/ppermute | solution.py:394
  43.2 3.7 %collective-permute-done.9 = bf16[256,512]{1,0:T(8,128)(2,1)S(1)} collective-permute-done((bf16[256,512]{1,0:T(8,128)(2,1)S(1)}, bf16[256,512]{1,0:T(8,128)(2,1)S(1)}, u32[]{:S(2)}, u32[]{:S(2)}) %collective-permute-start.9) | collective-permute-done | bytes 262176 | tf_op jit(solution)/shard_map/ppermute | solution.py:405
  47.0 12.1 %collective-permute-done.7.refs_6_ = bf16[1664,128]{1,0:T(8,128)(2,1)S(1)} collective-permute-done((bf16[1664,128]{1,0:T(8,128)(2,1)S(1)}, bf16[1664,128]{1,0:T(8,128)(2,1)S(1)}, u32[]{:S(2)}, u32[]{:S(2)}) %collective-permute-start.7) | collective-permute-done | bytes 426016 | tf_op jit(solution)/shard_map/ppermute | solution.py:394
  60.5 1.6 %turn_inputs.1 = (bf16[512,2048]{1,0:T(8,128)(2,1)S(1)}, bf16[1024,512]{1,0:T(8,128)(2,1)S(1)}) custom-call(s32[3]{0:T(128)S(1)} %pad_add_fusion.1.place_ref.refs_2_, bf16[1024,512]{1,0:T(8,128)(2,1)S(1)} %bitcast.36, bf16[1024,512]{1,0:T(8,128)(2,1)S(1)} %collective-permute-done.far_ref, bf16[2,512,512]{2,1,0:T(8,128)(2,1)S(1)} %copy-done.3), custom_call_target="tpu_custom_call" | custom-call | bytes 1000000 | tf_op jit(solution)/shard_map/turn_inputs/pallas_call | solution.py:279
  62.1 3.6 %early_tiles.1 = (bf16[3,1024,512]{2,1,0:T(8,128)(2,1)S(1)}, f32[32,128,512]{2,1,0:T(8,128)S(1)}) custom-call(s32[3]{0:T(128)S(1)} %pad_add_fusion.1.place_ref.refs_2_, bf16[768,512]{1,0:T(8,128)(2,1)S(1)} %pad_maximum_fusion.refs_0_, bf16[768,512]{1,0:T(8,128)(2,1)S(1)} %collective-permute-done.4.refs_1_, ...), custom_call_target="tpu_custom_call" | custom-call | bytes 1000000 | tf_op jit(solution)/shard_map/early_tiles/pallas_call | solution.py:165
  65.8 2.5 %collective-permute-done.10.refs_1_ = bf16[512,512]{1,0:T(8,128)(2,1)S(1)} collective-permute-done((bf16[512,512]{1,0:T(8,128)(2,1)S(1)}, bf16[512,512]{1,0:T(8,128)(2,1)S(1)}, u32[]{:S(2)}, u32[]{:S(2)}) %collective-permute-start.10) | collective-permute-done | bytes 524320 | tf_op jit(solution)/shard_map/ppermute | solution.py:405
  69.1 4.6 %late_tiles_and_rows.1 = (bf16[4,256,512]{2,1,0:T(8,128)(2,1)S(1)}, bf16[2048,1024]{1,0:T(8,128)(2,1)S(1)}, f32[32,128,512]{2,1,0:T(8,128)S(1)}) custom-call(s32[3]{0:T(128)S(1)} %pad_add_fusion.1.place_ref.refs_2_, bf16[3,1024,512]{2,1,0:T(8,128)(2,1)S(1)} %get-tuple-element.32.adjoint, ...), custom_call_target="tpu_custom_call", output_to_operand_aliasing={{2}: (2, {})} | custom-call | bytes 1000000 | tf_op jit(solution)/shard_map/late_tiles_and_rows/pallas_call | solution.py:239
  73.8 3.1 %grad_terms.1 = (bf16[4,2,64,512]{3,2,1,0:T(8,128)(2,1)S(1)}, f32[4,2,64,512]{3,2,1,0:T(8,128)S(1)}) custom-call(s32[3]{0:T(128)S(1)} %pad_add_fusion.1.place_ref.refs_2_, bf16[2048,1024]{1,0:T(8,128)(2,1)S(1)} %get-tuple-element.40.summed, bf16[512,2048]{1,0:T(8,128)(2,1)S(1)} %get-tuple-element.24.inputs_ref), custom_call_target="tpu_custom_call" | custom-call | bytes 1000000 | tf_op jit(solution)/shard_map/grad_terms/pallas_call | solution.py:348
  77.4 2.0 %row_terms.1 = (f32[2,256,512]{2,1,0:T(8,128)S(1)}, bf16[2,256,512]{2,1,0:T(8,128)(2,1)S(1)}) custom-call(s32[3]{0:T(128)S(1)} %pad_add_fusion.1.place_ref.refs_2_, bf16[2048,1024]{1,0:T(8,128)(2,1)S(1)} %get-tuple-element.40.summed, bf16[1024,512]{1,0:T(8,128)(2,1)S(1)} %get-tuple-element.25.refs_4_.weights_ref, ...), custom_call_target="tpu_custom_call" | custom-call | flops 2147483648 | bytes 4000000 | tf_op jit(solution)/shard_map/row_terms/pallas_call | solution.py:310
  79.5 1.6 %collective-permute-start.18 = (bf16[2,256,512]{2,1,0:T(8,128)(2,1)S(1)}, bf16[2,256,512]{2,1,0:T(8,128)(2,1)S(1)}, u32[]{:S(2)}, u32[]{:S(2)}) collective-permute-start(bf16[2,256,512]{2,1,0:T(8,128)(2,1)S(1)} %get-tuple-element.45), channel_id=1, source_target_pairs={{0,8},{1,17},{2,10},{3,19},{4,12},{5,21},{6,14},{7,23},{8,0},{9,25... | collective-permute-start | bytes 1572872 | tf_op jit(solution)/shard_map/ppermute | solution.py:405
  81.3 1.8 %collective-permute-start.14 = (bf16[2,64,512]{2,1,0:T(8,128)(2,1)S(1)}, bf16[2,64,512]{2,1,0:T(8,128)(2,1)S(1)}, u32[]{:S(2)}, u32[]{:S(2)}) collective-permute-start(bf16[2,64,512]{2,1,0:T(8,128)(2,1)S(1)} %get-tuple-element.48), channel_id=1, source_target_pairs={{0,6},{1,7},{2,4},{3,5},{4,2},{5,3},{6,0},{7,1},{8,14},{9,15},{10,... | collective-permute-start | bytes 393224 | tf_op jit(solution)/shard_map/ppermute | solution.py:394
  83.5 2.3 %collective-permute-start.16 = (bf16[2,64,512]{2,1,0:T(8,128)(2,1)S(1)}, bf16[2,64,512]{2,1,0:T(8,128)(2,1)S(1)}, u32[]{:S(2)}, u32[]{:S(2)}) collective-permute-start(bf16[2,64,512]{2,1,0:T(8,128)(2,1)S(1)} %get-tuple-element.49), channel_id=1, source_target_pairs={{0,2},{1,3},{2,0},{3,1},{4,6},{5,7},{6,4},{7,5},{8,10},{9,11},{10,... | collective-permute-start | bytes 393224 | tf_op jit(solution)/shard_map/ppermute | solution.py:394
  85.8 2.9 %collective-permute-done.18 = bf16[2,256,512]{2,1,0:T(8,128)(2,1)S(1)} collective-permute-done((bf16[2,256,512]{2,1,0:T(8,128)(2,1)S(1)}, bf16[2,256,512]{2,1,0:T(8,128)(2,1)S(1)}, u32[]{:S(2)}, u32[]{:S(2)}) %collective-permute-start.18) | collective-permute-done | bytes 524320 | tf_op jit(solution)/shard_map/ppermute | solution.py:405
  90.0 4.5 %collective-permute-done.15 = bf16[2,64,512]{2,1,0:T(8,128)(2,1)S(1)} collective-permute-done((bf16[2,64,512]{2,1,0:T(8,128)(2,1)S(1)}, bf16[2,64,512]{2,1,0:T(8,128)(2,1)S(1)}, u32[]{:S(2)}, u32[]{:S(2)}) %collective-permute-start.15) | collective-permute-done | bytes 131104 | tf_op jit(solution)/shard_map/ppermute | solution.py:394
  (44 shorter events, 12.1 us)
Async XLA Ops:
  0.6 89.0 %copy-start = (bf16[512,512]{1,0:T(8,128)(2,1)S(1)}, bf16[512,512]{1,0:T(8,128)(2,1)}, u32[]{:S(2)}) copy-start(bf16[512,512]{1,0:T(8,128)(2,1)} %param.12) | copy-start | bytes 1572868
  0.6 22.7 %collective-permute-start = (bf16[1024,512]{1,0:T(8,128)(2,1)}, bf16[1024,512]{1,0:T(8,128)(2,1)S(1)}, u32[]{:S(2)}, u32[]{:S(2)}) collective-permute-start(bf16[1024,512]{1,0:T(8,128)(2,1)} %bitcast.35), channel_id=1, source_target_pairs={{0,1},{1,0},{2,3},{3,2},{4,5},{5,4},{6,7},{7,6},{8,9},{9,8},{10,11... | collective-permute-start | bytes 3145736 | tf_op jit(solution)/shard_map/ppermute | solution.py:394
  1.2 15.2 %collective-permute-start.1 = (bf16[256,512]{1,0:T(8,128)(2,1)}, bf16[256,512]{1,0:T(8,128)(2,1)S(1)}, u32[]{:S(2)}, u32[]{:S(2)}) collective-permute-start(bf16[256,512]{1,0:T(8,128)(2,1)} %bitcast.37), channel_id=1, source_target_pairs={{0,2},{1,3},{2,0},{3,1},{4,6},{5,7},{6,4},{7,5},{8,10},{9,11},{10,... | collective-permute-start | bytes 786440 | tf_op jit(solution)/shard_map/ppermute | solution.py:394
  3.8 17.4 %collective-permute-start.2 = (bf16[256,512]{1,0:T(8,128)(2,1)}, bf16[256,512]{1,0:T(8,128)(2,1)S(1)}, u32[]{:S(2)}, u32[]{:S(2)}) collective-permute-start(bf16[256,512]{1,0:T(8,128)(2,1)} %bitcast.38), channel_id=1, source_target_pairs={{0,4},{1,5},{2,6},{3,7},{4,0},{5,1},{6,2},{7,3},{8,12},{9,13},{10,... | collective-permute-start | bytes 786440 | tf_op jit(solution)/shard_map/ppermute | solution.py:394
  8.4 52.1 %copy-start.2 = (bf16[1,1024,512]{2,1,0:T(8,128)(2,1)S(1)}, bf16[1,1024,512]{2,1,0:T(8,128)(2,1)}, u32[]{:S(2)}) copy-start(bf16[1,1024,512]{2,1,0:T(8,128)(2,1)} %param.10) | copy-start | bytes 3145732
  8.4 52.1 %copy-start.3 = (bf16[2,512,512]{2,1,0:T(8,128)(2,1)S(1)}, bf16[2,512,512]{2,1,0:T(8,128)(2,1)}, u32[]{:S(2)}) copy-start(bf16[2,512,512]{2,1,0:T(8,128)(2,1)} %weights_ref.1) | copy-start | bytes 3145732
  11.2 12.2 %collective-permute-start.3 = (bf16[400,128]{1,0:T(8,128)(2,1)S(1)}, bf16[400,128]{1,0:T(8,128)(2,1)S(1)}, u32[]{:S(2)}, u32[]{:S(2)}) collective-permute-start(bf16[400,128]{1,0:T(8,128)(2,1)S(1)} %get-tuple-element.27), channel_id=1, source_target_pairs={{0,4},{1,5},{2,6},{3,7},{4,0},{5,1},{6,2},{7,3},{8,12},{9,13},{10,... | collective-permute-start | bytes 307208 | tf_op jit(solution)/shard_map/ppermute | solution.py:394
  23.4 16.3 %collective-permute-start.4 = (bf16[768,512]{1,0:T(8,128)(2,1)S(1)}, bf16[768,512]{1,0:T(8,128)(2,1)S(1)}, u32[]{:S(2)}, u32[]{:S(2)}) collective-permute-start(bf16[768,512]{1,0:T(8,128)(2,1)S(1)} %pad_maximum_fusion.refs_0_), channel_id=1, source_target_pairs={{0,8},{1,17},{2,10},{3,19},{4,12},{5,21},{6,14},{7,23},{8,0},{9,25... | collective-permute-start | bytes 2359304 | tf_op jit(solution)/shard_map/ppermute | solution.py:405
  24.9 12.8 %collective-permute-start.8 = (bf16[256,512]{1,0:T(8,128)(2,1)S(1)}, bf16[256,512]{1,0:T(8,128)(2,1)S(1)}, u32[]{:S(2)}, u32[]{:S(2)}) collective-permute-start(bf16[256,512]{1,0:T(8,128)(2,1)S(1)} %collective-permute-done.2), channel_id=1, source_target_pairs={{0,2},{1,3},{2,0},{3,1},{4,6},{5,7},{6,4},{7,5},{8,10},{9,11},{10,... | collective-permute-start | bytes 786440 | tf_op jit(solution)/shard_map/ppermute | solution.py:394
  24.9 34.2 %collective-permute-start.7 = (bf16[1664,128]{1,0:T(8,128)(2,1)S(1)}, bf16[1664,128]{1,0:T(8,128)(2,1)S(1)}, u32[]{:S(2)}, u32[]{:S(2)}) collective-permute-start(bf16[1664,128]{1,0:T(8,128)(2,1)S(1)} %get-tuple-element.31), channel_id=1, source_target_pairs={{0,4},{1,5},{2,6},{3,7},{4,0},{5,1},{6,2},{7,3},{8,12},{9,13},{10,... | collective-permute-start | bytes 1277960 | tf_op jit(solution)/shard_map/ppermute | solution.py:394
  37.6 9.2 %collective-permute-start.9 = (bf16[256,512]{1,0:T(8,128)(2,1)S(1)}, bf16[256,512]{1,0:T(8,128)(2,1)S(1)}, u32[]{:S(2)}, u32[]{:S(2)}) collective-permute-start(bf16[256,512]{1,0:T(8,128)(2,1)S(1)} %collective-permute-done.8), channel_id=1, source_target_pairs={{0,8},{1,17},{2,10},{3,19},{4,12},{5,21},{6,14},{7,23},{8,0},{9,25... | collective-permute-start | bytes 786440 | tf_op jit(solution)/shard_map/ppermute | solution.py:405
  39.1 23.0 %collective-permute-start.5 = (bf16[768,512]{1,0:T(8,128)(2,1)S(1)}, bf16[768,512]{1,0:T(8,128)(2,1)S(1)}, u32[]{:S(2)}, u32[]{:S(2)}) collective-permute-start(bf16[768,512]{1,0:T(8,128)(2,1)S(1)} %pad_maximum_fusion.refs_0_), channel_id=1, source_target_pairs={{0,16},{1,9},{2,18},{3,11},{4,20},{5,13},{6,22},{7,15},{8,24},{9,1... | collective-permute-start | bytes 2359304 | tf_op jit(solution)/shard_map/ppermute | solution.py:405
  39.6 22.5 %collective-permute-start.6 = (bf16[768,512]{1,0:T(8,128)(2,1)S(1)}, bf16[768,512]{1,0:T(8,128)(2,1)S(1)}, u32[]{:S(2)}, u32[]{:S(2)}) collective-permute-start(bf16[768,512]{1,0:T(8,128)(2,1)S(1)} %collective-permute-done.4.refs_1_), channel_id=1, source_target_pairs={{0,16},{1,9},{2,18},{3,11},{4,20},{5,13},{6,22},{7,15},{8,24},{9,1... | collective-permute-start | bytes 2359304 | tf_op jit(solution)/shard_map/ppermute | solution.py:405
  41.2 24.6 %collective-permute-start.12 = (bf16[2064,128]{1,0:T(8,128)(2,1)S(1)}, bf16[2064,128]{1,0:T(8,128)(2,1)S(1)}, u32[]{:S(2)}, u32[]{:S(2)}) collective-permute-start(bf16[2064,128]{1,0:T(8,128)(2,1)S(1)} %get-tuple-element.39), channel_id=1, source_target_pairs={{0,6},{1,7},{2,4},{3,5},{4,2},{5,3},{6,0},{7,1},{8,14},{9,15},{10,... | collective-permute-start | bytes 1585160 | tf_op jit(solution)/shard_map/ppermute | solution.py:394
  46.9 22.2 %collective-permute-start.11 = (bf16[2064,128]{1,0:T(8,128)(2,1)S(1)}, bf16[2064,128]{1,0:T(8,128)(2,1)S(1)}, u32[]{:S(2)}, u32[]{:S(2)}) collective-permute-start(bf16[2064,128]{1,0:T(8,128)(2,1)S(1)} %get-tuple-element.37), channel_id=1, source_target_pairs={{0,2},{1,3},{2,0},{3,1},{4,6},{5,7},{6,4},{7,5},{8,10},{9,11},{10,... | collective-permute-start | bytes 1585160 | tf_op jit(solution)/shard_map/ppermute | solution.py:394
  59.1 9.2 %collective-permute-start.10 = (bf16[512,512]{1,0:T(8,128)(2,1)S(1)}, bf16[512,512]{1,0:T(8,128)(2,1)S(1)}, u32[]{:S(2)}, u32[]{:S(2)}) collective-permute-start(bf16[512,512]{1,0:T(8,128)(2,1)S(1)} %constant_dynamic-update-slice_fusion.refs_0_), channel_id=1, source_target_pairs={{0,16},{1,9},{2,18},{3,11},{4,20},{5,13},{6,22},{7,15},{8,24},{9,1... | collective-permute-start | bytes 1572872 | tf_op jit(solution)/shard_map/ppermute | solution.py:405
  73.7 3.7 %collective-permute-start.17 = (bf16[4,256,512]{2,1,0:T(8,128)(2,1)S(1)}, bf16[4,256,512]{2,1,0:T(8,128)(2,1)S(1)}, u32[]{:S(2)}, u32[]{:S(2)}) collective-permute-start(bf16[4,256,512]{2,1,0:T(8,128)(2,1)S(1)} %get-tuple-element.43), channel_id=1, source_target_pairs={{0,1},{1,0},{2,3},{3,2},{4,5},{5,4},{6,7},{7,6},{8,9},{9,8},{10,11... | collective-permute-start | bytes 3145736 | tf_op jit(solution)/shard_map/ppermute | solution.py:394
  76.9 4.2 %collective-permute-start.13 = (bf16[4,2,64,512]{3,2,1,0:T(8,128)(2,1)S(1)}, bf16[4,2,64,512]{3,2,1,0:T(8,128)(2,1)S(1)}, u32[]{:S(2)}, u32[]{:S(2)}) collective-permute-start(bf16[4,2,64,512]{3,2,1,0:T(8,128)(2,1)S(1)} %get-tuple-element.42), channel_id=1, source_target_pairs={{0,1},{1,0},{2,3},{3,2},{4,5},{5,4},{6,7},{7,6},{8,9},{9,8},{10,11... | collective-permute-start | bytes 1572872 | tf_op jit(solution)/shard_map/ppermute | solution.py:394
  79.5 9.2 %collective-permute-start.18 = (bf16[2,256,512]{2,1,0:T(8,128)(2,1)S(1)}, bf16[2,256,512]{2,1,0:T(8,128)(2,1)S(1)}, u32[]{:S(2)}, u32[]{:S(2)}) collective-permute-start(bf16[2,256,512]{2,1,0:T(8,128)(2,1)S(1)} %get-tuple-element.45), channel_id=1, source_target_pairs={{0,8},{1,17},{2,10},{3,19},{4,12},{5,21},{6,14},{7,23},{8,0},{9,25... | collective-permute-start | bytes 1572872 | tf_op jit(solution)/shard_map/ppermute | solution.py:405
  81.3 8.3 %copy-start.4 = (bf16[1,256,512]{2,1,0:T(8,128)(2,1)S(1)}, bf16[1,256,512]{2,1,0:T(8,128)(2,1)}, u32[]{:S(2)}) copy-start(bf16[1,256,512]{2,1,0:T(8,128)(2,1)} %param.9) | copy-start | bytes 786436
  81.3 8.6 %collective-permute-start.14 = (bf16[2,64,512]{2,1,0:T(8,128)(2,1)S(1)}, bf16[2,64,512]{2,1,0:T(8,128)(2,1)S(1)}, u32[]{:S(2)}, u32[]{:S(2)}) collective-permute-start(bf16[2,64,512]{2,1,0:T(8,128)(2,1)S(1)} %get-tuple-element.48), channel_id=1, source_target_pairs={{0,6},{1,7},{2,4},{3,5},{4,2},{5,3},{6,0},{7,1},{8,14},{9,15},{10,... | collective-permute-start | bytes 393224 | tf_op jit(solution)/shard_map/ppermute | solution.py:394
  83.1 11.4 %collective-permute-start.15 = (bf16[2,64,512]{2,1,0:T(8,128)(2,1)S(1)}, bf16[2,64,512]{2,1,0:T(8,128)(2,1)S(1)}, u32[]{:S(2)}, u32[]{:S(2)}) collective-permute-start(bf16[2,64,512]{2,1,0:T(8,128)(2,1)S(1)} %get-tuple-element.50), channel_id=1, source_target_pairs={{0,4},{1,5},{2,6},{3,7},{4,0},{5,1},{6,2},{7,3},{8,12},{9,13},{10,... | collective-permute-start | bytes 393224 | tf_op jit(solution)/shard_map/ppermute | solution.py:394
  83.5 11.0 %collective-permute-start.16 = (bf16[2,64,512]{2,1,0:T(8,128)(2,1)S(1)}, bf16[2,64,512]{2,1,0:T(8,128)(2,1)S(1)}, u32[]{:S(2)}, u32[]{:S(2)}) collective-permute-start(bf16[2,64,512]{2,1,0:T(8,128)(2,1)S(1)} %get-tuple-element.49), channel_id=1, source_target_pairs={{0,2},{1,3},{2,0},{3,1},{4,6},{5,7},{6,4},{7,5},{8,10},{9,11},{10,... | collective-permute-start | bytes 393224 | tf_op jit(solution)/shard_map/ppermute | solution.py:394
  88.9 6.4 %collective-permute-start.19 = (bf16[1,256,512]{2,1,0:T(8,128)(2,1)S(1)}, bf16[1,256,512]{2,1,0:T(8,128)(2,1)S(1)}, u32[]{:S(2)}, u32[]{:S(2)}) collective-permute-start(bf16[1,256,512]{2,1,0:T(8,128)(2,1)S(1)} %slice.54), channel_id=1, source_target_pairs={{0,16},{1,9},{2,18},{3,11},{4,20},{5,13},{6,22},{7,15},{8,24},{9,1... | collective-permute-start | bytes 786440 | tf_op jit(solution)/shard_map/ppermute | solution.py:405
  (1 other events, 1.2 us)

commit v6 on v5

--- a/solution.py
+++ b/solution.py
@@ -425,7 +425,7 @@
     for j in levels[0][1:]:
         by_chip[j] = to_chip(own, j)
     head = to_chip(placed[1], mid)
-    first = [head, far] + [by_chip[j] for j in levels[0][1:]]
+    first = [head] + [by_chip[j] for j in levels[0][1:]]
     body = to_chip(after(placed[2], *first), mid)
     payloads = [placed[0], head, body]
     for value, (j, _, _) in list(zip(placed, parts, strict=True))[3:-1]:
@@ -441,6 +441,8 @@
         held = held[0] if len(held) == 1 else jnp.concatenate(held)
         if n == 0:
             held = after(held, *first)
+        if n == 1:
+            held = after(held, far)
         held = [(held, ((0, 0),))]
         for step in range(steps):
             if n:

time: 96.4 us -> 95.7 us (level)
  transfers between devices with their start and end apart: 20 -> 20, of which waited for: 11 -> 11; matrix products, arithmetic and copies ran while one was open for 3% -> 4% of each run, Pallas kernels for 14% -> 14%
where the time goes in v6:
time: 95.7 us; the launch traced here: 95.5 us
  waiting for transfers between devices  46.9 us (49%)
  starting transfers between devices  24.7 us (26%)
  Pallas kernels  17.6 us (18%)
  other arithmetic  3.78 us (4%)
  local copies, waits for them, and re-layouts  1.34 us (1%)
    ppermute x13, waiting for transfers between devices, across(): return lax.ppermute(value, axis, [(i, i ^ mask) for i in range(size)])  37.4 us
    ppermute x13, starting transfers between devices, across(): return lax.ppermute(value, axis, [(i, i ^ mask) for i in range(size)])  16.6 us
    ppermute x7, waiting for transfers between devices, in_plane(): return lax.ppermute(value, ('rel', 'node'), pairs)  9.49 us
    ppermute x7, starting transfers between devices, in_plane(): return lax.ppermute(value, ('rel', 'node'), pairs)  8.15 us
    pallas_call x1, Pallas kernels, late_tiles_and_rows(): pl.pallas_call(functools.partial(late_kernel, parts, held, segments, size...  4.59 us
    pallas_call x1, Pallas kernels, early_tiles(): pl.pallas_call(functools.partial(early_kernel, parts, segments, groups),...  3.61 us
    pallas_call x1, Pallas kernels, grad_terms(): pl.pallas_call(functools.partial(grad_kernel, chips, relations), out_shap...  3.09 us
    pallas_call x1, Pallas kernels, place_tiles(): pl.pallas_call(functools.partial(place_kernel, parts, chips, blocks, rela...  2.74 us
  transfers between devices with their start and end apart: 20, of which 11 were waited for; matrix products, arithmetic and copies ran while one was open for 4% of the time, Pallas kernels for 14%

profile of v6, /device:TPU:0, one launch (start us, length us, event | category | flops | bytes accessed | tf_op | source)
XLA Modules:
  0.0 95.5 jit_solution(4954684244370547876)
XLA Ops:
  0.6 3.1 %collective-permute-start.1 = (bf16[256,512]{1,0:T(8,128)(2,1)}, bf16[256,512]{1,0:T(8,128)(2,1)S(1)}, u32[]{:S(2)}, u32[]{:S(2)}) collective-permute-start(bf16[256,512]{1,0:T(8,128)(2,1)} %bitcast.37), channel_id=1, source_target_pairs={{0,2},{1,3},{2,0},{3,1},{4,6},{5,7},{6,4},{7,5},{8,10},{9,11},{10,... | collective-permute-start | bytes 786440 | tf_op jit(solution)/shard_map/ppermute | solution.py:394
  3.7 2.6 %collective-permute-start.2 = (bf16[256,512]{1,0:T(8,128)(2,1)}, bf16[256,512]{1,0:T(8,128)(2,1)S(1)}, u32[]{:S(2)}, u32[]{:S(2)}) collective-permute-start(bf16[256,512]{1,0:T(8,128)(2,1)} %bitcast.38), channel_id=1, source_target_pairs={{0,4},{1,5},{2,6},{3,7},{4,0},{5,1},{6,2},{7,3},{8,12},{9,13},{10,... | collective-permute-start | bytes 786440 | tf_op jit(solution)/shard_map/ppermute | solution.py:394
  8.3 2.7 %place_tiles.1 = (bf16[2064,128]{1,0:T(8,128)(2,1)S(1)}, bf16[400,128]{1,0:T(8,128)(2,1)S(1)}, bf16[1664,128]{1,0:T(8,128)(2,1)S(1)}, bf16[2064,128]{1,0:T(8,128)(2,1)S(1)}, bf16[2064,128]{1,0:T(8,128)(2,1)S(1)}) custom-call(s32[4,32]{1,0:T(4,128)S(1)} %pad_add_fusion.refs_0_, bf16[32,128,128]{2,1,0:T(8,128)(2,1)S(1)} %bitcast.34, ...), custom_call_target="tpu_custom_call" | custom-call | bytes 4000000 | tf_op jit(solution)/shard_map/place_tiles/pallas_call | solution.py:73
  11.5 4.2 %collective-permute-done.1 = bf16[256,512]{1,0:T(8,128)(2,1)S(1)} collective-permute-done((bf16[256,512]{1,0:T(8,128)(2,1)}, bf16[256,512]{1,0:T(8,128)(2,1)S(1)}, u32[]{:S(2)}, u32[]{:S(2)}) %collective-permute-start.1) | collective-permute-done | bytes 262176 | tf_op jit(solution)/shard_map/ppermute | solution.py:394
  15.7 4.8 %collective-permute-done.2 = bf16[256,512]{1,0:T(8,128)(2,1)S(1)} collective-permute-done((bf16[256,512]{1,0:T(8,128)(2,1)}, bf16[256,512]{1,0:T(8,128)(2,1)S(1)}, u32[]{:S(2)}, u32[]{:S(2)}) %collective-permute-start.2) | collective-permute-done | bytes 262176 | tf_op jit(solution)/shard_map/ppermute | solution.py:394
  22.7 1.5 %collective-permute-start.4 = (bf16[768,512]{1,0:T(8,128)(2,1)S(1)}, bf16[768,512]{1,0:T(8,128)(2,1)S(1)}, u32[]{:S(2)}, u32[]{:S(2)}) collective-permute-start(bf16[768,512]{1,0:T(8,128)(2,1)S(1)} %pad_maximum_fusion.refs_0_), channel_id=1, source_target_pairs={{0,8},{1,17},{2,10},{3,19},{4,12},{5,21},{6,14},{7,23},{8,0},{9,25... | collective-permute-start | bytes 2359304 | tf_op jit(solution)/shard_map/ppermute | solution.py:405
  24.2 3.0 %collective-permute-start.7 = (bf16[1664,128]{1,0:T(8,128)(2,1)S(1)}, bf16[1664,128]{1,0:T(8,128)(2,1)S(1)}, u32[]{:S(2)}, u32[]{:S(2)}) collective-permute-start(bf16[1664,128]{1,0:T(8,128)(2,1)S(1)} %get-tuple-element.32), channel_id=1, source_target_pairs={{0,4},{1,5},{2,6},{3,7},{4,0},{5,1},{6,2},{7,3},{8,12},{9,13},{10,... | collective-permute-start | bytes 1277960 | tf_op jit(solution)/shard_map/ppermute | solution.py:394
  27.2 9.4 %collective-permute-done.8 = bf16[256,512]{1,0:T(8,128)(2,1)S(1)} collective-permute-done((bf16[256,512]{1,0:T(8,128)(2,1)S(1)}, bf16[256,512]{1,0:T(8,128)(2,1)S(1)}, u32[]{:S(2)}, u32[]{:S(2)}) %collective-permute-start.8) | collective-permute-done | bytes 262176 | tf_op jit(solution)/shard_map/ppermute | solution.py:394
  36.6 1.5 %collective-permute-start.9 = (bf16[256,512]{1,0:T(8,128)(2,1)S(1)}, bf16[256,512]{1,0:T(8,128)(2,1)S(1)}, u32[]{:S(2)}, u32[]{:S(2)}) collective-permute-start(bf16[256,512]{1,0:T(8,128)(2,1)S(1)} %collective-permute-done.8), channel_id=1, source_target_pairs={{0,8},{1,17},{2,10},{3,19},{4,12},{5,21},{6,14},{7,23},{8,0},{9,25... | collective-permute-start | bytes 786440 | tf_op jit(solution)/shard_map/ppermute | solution.py:405
  38.6 1.5 %collective-permute-start.6 = (bf16[768,512]{1,0:T(8,128)(2,1)S(1)}, bf16[768,512]{1,0:T(8,128)(2,1)S(1)}, u32[]{:S(2)}, u32[]{:S(2)}) collective-permute-start(bf16[768,512]{1,0:T(8,128)(2,1)S(1)} %collective-permute-done.4.refs_1_), channel_id=1, source_target_pairs={{0,16},{1,9},{2,18},{3,11},{4,20},{5,13},{6,22},{7,15},{8,24},{9,1... | collective-permute-start | bytes 2359304 | tf_op jit(solution)/shard_map/ppermute | solution.py:405
  40.1 2.3 %collective-permute-start.12 = (bf16[2064,128]{1,0:T(8,128)(2,1)S(1)}, bf16[2064,128]{1,0:T(8,128)(2,1)S(1)}, u32[]{:S(2)}, u32[]{:S(2)}) collective-permute-start(bf16[2064,128]{1,0:T(8,128)(2,1)S(1)} %get-tuple-element.41), channel_id=1, source_target_pairs={{0,6},{1,7},{2,4},{3,5},{4,2},{5,3},{6,0},{7,1},{8,14},{9,15},{10,... | collective-permute-start | bytes 1585160 | tf_op jit(solution)/shard_map/ppermute | solution.py:394
  42.4 3.4 %collective-permute-done.9 = bf16[256,512]{1,0:T(8,128)(2,1)S(1)} collective-permute-done((bf16[256,512]{1,0:T(8,128)(2,1)S(1)}, bf16[256,512]{1,0:T(8,128)(2,1)S(1)}, u32[]{:S(2)}, u32[]{:S(2)}) %collective-permute-start.9) | collective-permute-done | bytes 262176 | tf_op jit(solution)/shard_map/ppermute | solution.py:405
  45.9 12.5 %collective-permute-done.7.refs_6_ = bf16[1664,128]{1,0:T(8,128)(2,1)S(1)} collective-permute-done((bf16[1664,128]{1,0:T(8,128)(2,1)S(1)}, bf16[1664,128]{1,0:T(8,128)(2,1)S(1)}, u32[]{:S(2)}, u32[]{:S(2)}) %collective-permute-start.7) | collective-permute-done | bytes 426016 | tf_op jit(solution)/shard_map/ppermute | solution.py:394
  59.4 1.6 %turn_inputs.1 = (bf16[512,2048]{1,0:T(8,128)(2,1)S(1)}, bf16[1024,512]{1,0:T(8,128)(2,1)S(1)}) custom-call(s32[3]{0:T(128)S(1)} %pad_add_fusion.1.place_ref.refs_2_, bf16[1024,512]{1,0:T(8,128)(2,1)S(1)} %bitcast.36, bf16[1024,512]{1,0:T(8,128)(2,1)S(1)} %collective-permute-done.far_ref, bf16[2,512,512]{2,1,0:T(8,128)(2,1)S(1)} %copy-done.3), custom_call_target="tpu_custom_call" | custom-call | bytes 1000000 | tf_op jit(solution)/shard_map/turn_inputs/pallas_call | solution.py:279
  61.0 3.6 %early_tiles.1 = (bf16[3,1024,512]{2,1,0:T(8,128)(2,1)S(1)}, f32[32,128,512]{2,1,0:T(8,128)S(1)}) custom-call(s32[3]{0:T(128)S(1)} %pad_add_fusion.1.place_ref.refs_2_, bf16[768,512]{1,0:T(8,128)(2,1)S(1)} %pad_maximum_fusion.refs_0_, bf16[768,512]{1,0:T(8,128)(2,1)S(1)} %collective-permute-done.4.refs_1_, ...), custom_call_target="tpu_custom_call" | custom-call | bytes 1000000 | tf_op jit(solution)/shard_map/early_tiles/pallas_call | solution.py:165
  64.7 2.9 %collective-permute-done.10.refs_1_ = bf16[512,512]{1,0:T(8,128)(2,1)S(1)} collective-permute-done((bf16[512,512]{1,0:T(8,128)(2,1)S(1)}, bf16[512,512]{1,0:T(8,128)(2,1)S(1)}, u32[]{:S(2)}, u32[]{:S(2)}) %collective-permute-start.10) | collective-permute-done | bytes 524320 | tf_op jit(solution)/shard_map/ppermute | solution.py:405
  68.4 4.6 %late_tiles_and_rows.1 = (bf16[4,256,512]{2,1,0:T(8,128)(2,1)S(1)}, bf16[2048,1024]{1,0:T(8,128)(2,1)S(1)}, f32[32,128,512]{2,1,0:T(8,128)S(1)}) custom-call(s32[3]{0:T(128)S(1)} %pad_add_fusion.1.place_ref.refs_2_, bf16[3,1024,512]{2,1,0:T(8,128)(2,1)S(1)} %get-tuple-element.33.adjoint, ...), custom_call_target="tpu_custom_call", output_to_operand_aliasing={{2}: (2, {})} | custom-call | bytes 1000000 | tf_op jit(solution)/shard_map/late_tiles_and_rows/pallas_call | solution.py:239
  73.1 3.1 %grad_terms.1 = (bf16[4,2,64,512]{3,2,1,0:T(8,128)(2,1)S(1)}, f32[4,2,64,512]{3,2,1,0:T(8,128)S(1)}) custom-call(s32[3]{0:T(128)S(1)} %pad_add_fusion.1.place_ref.refs_2_, bf16[2048,1024]{1,0:T(8,128)(2,1)S(1)} %get-tuple-element.42.summed, bf16[512,2048]{1,0:T(8,128)(2,1)S(1)} %get-tuple-element.25.inputs_ref), custom_call_target="tpu_custom_call" | custom-call | bytes 1000000 | tf_op jit(solution)/shard_map/grad_terms/pallas_call | solution.py:348
  76.7 2.0 %row_terms.1 = (f32[2,256,512]{2,1,0:T(8,128)S(1)}, bf16[2,256,512]{2,1,0:T(8,128)(2,1)S(1)}) custom-call(s32[3]{0:T(128)S(1)} %pad_add_fusion.1.place_ref.refs_2_, bf16[2048,1024]{1,0:T(8,128)(2,1)S(1)} %get-tuple-element.42.summed, bf16[1024,512]{1,0:T(8,128)(2,1)S(1)} %get-tuple-element.26.refs_4_.weights_ref, ...), custom_call_target="tpu_custom_call" | custom-call | flops 2147483648 | bytes 4000000 | tf_op jit(solution)/shard_map/row_terms/pallas_call | solution.py:310
  78.8 1.5 %collective-permute-start.18 = (bf16[2,256,512]{2,1,0:T(8,128)(2,1)S(1)}, bf16[2,256,512]{2,1,0:T(8,128)(2,1)S(1)}, u32[]{:S(2)}, u32[]{:S(2)}) collective-permute-start(bf16[2,256,512]{2,1,0:T(8,128)(2,1)S(1)} %get-tuple-element.47), channel_id=1, source_target_pairs={{0,8},{1,17},{2,10},{3,19},{4,12},{5,21},{6,14},{7,23},{8,0},{9,25... | collective-permute-start | bytes 1572872 | tf_op jit(solution)/shard_map/ppermute | solution.py:405
  80.6 1.5 %collective-permute-start.14 = (bf16[2,64,512]{2,1,0:T(8,128)(2,1)S(1)}, bf16[2,64,512]{2,1,0:T(8,128)(2,1)S(1)}, u32[]{:S(2)}, u32[]{:S(2)}) collective-permute-start(bf16[2,64,512]{2,1,0:T(8,128)(2,1)S(1)} %get-tuple-element.50), channel_id=1, source_target_pairs={{0,6},{1,7},{2,4},{3,5},{4,2},{5,3},{6,0},{7,1},{8,14},{9,15},{10,... | collective-permute-start | bytes 393224 | tf_op jit(solution)/shard_map/ppermute | solution.py:394
  82.8 2.3 %collective-permute-start.16 = (bf16[2,64,512]{2,1,0:T(8,128)(2,1)S(1)}, bf16[2,64,512]{2,1,0:T(8,128)(2,1)S(1)}, u32[]{:S(2)}, u32[]{:S(2)}) collective-permute-start(bf16[2,64,512]{2,1,0:T(8,128)(2,1)S(1)} %get-tuple-element.51), channel_id=1, source_target_pairs={{0,2},{1,3},{2,0},{3,1},{4,6},{5,7},{6,4},{7,5},{8,10},{9,11},{10,... | collective-permute-start | bytes 393224 | tf_op jit(solution)/shard_map/ppermute | solution.py:394
  85.1 3.0 %collective-permute-done.18 = bf16[2,256,512]{2,1,0:T(8,128)(2,1)S(1)} collective-permute-done((bf16[2,256,512]{2,1,0:T(8,128)(2,1)S(1)}, bf16[2,256,512]{2,1,0:T(8,128)(2,1)S(1)}, u32[]{:S(2)}, u32[]{:S(2)}) %collective-permute-start.18) | collective-permute-done | bytes 524320 | tf_op jit(solution)/shard_map/ppermute | solution.py:405
  89.2 4.5 %collective-permute-done.15 = bf16[2,64,512]{2,1,0:T(8,128)(2,1)S(1)} collective-permute-done((bf16[2,64,512]{2,1,0:T(8,128)(2,1)S(1)}, bf16[2,64,512]{2,1,0:T(8,128)(2,1)S(1)}, u32[]{:S(2)}, u32[]{:S(2)}) %collective-permute-start.15) | collective-permute-done | bytes 131104 | tf_op jit(solution)/shard_map/ppermute | solution.py:394
  (44 shorter events, 11.5 us)
Async XLA Ops:
  0.6 88.2 %copy-start = (bf16[512,512]{1,0:T(8,128)(2,1)S(1)}, bf16[512,512]{1,0:T(8,128)(2,1)}, u32[]{:S(2)}) copy-start(bf16[512,512]{1,0:T(8,128)(2,1)} %param.12) | copy-start | bytes 1572868
  0.6 15.1 %collective-permute-start.1 = (bf16[256,512]{1,0:T(8,128)(2,1)}, bf16[256,512]{1,0:T(8,128)(2,1)S(1)}, u32[]{:S(2)}, u32[]{:S(2)}) collective-permute-start(bf16[256,512]{1,0:T(8,128)(2,1)} %bitcast.37), channel_id=1, source_target_pairs={{0,2},{1,3},{2,0},{3,1},{4,6},{5,7},{6,4},{7,5},{8,10},{9,11},{10,... | collective-permute-start | bytes 786440 | tf_op jit(solution)/shard_map/ppermute | solution.py:394
  3.7 16.8 %collective-permute-start.2 = (bf16[256,512]{1,0:T(8,128)(2,1)}, bf16[256,512]{1,0:T(8,128)(2,1)S(1)}, u32[]{:S(2)}, u32[]{:S(2)}) collective-permute-start(bf16[256,512]{1,0:T(8,128)(2,1)} %bitcast.38), channel_id=1, source_target_pairs={{0,4},{1,5},{2,6},{3,7},{4,0},{5,1},{6,2},{7,3},{8,12},{9,13},{10,... | collective-permute-start | bytes 786440 | tf_op jit(solution)/shard_map/ppermute | solution.py:394
  6.3 30.2 %collective-permute-start = (bf16[1024,512]{1,0:T(8,128)(2,1)}, bf16[1024,512]{1,0:T(8,128)(2,1)S(1)}, u32[]{:S(2)}, u32[]{:S(2)}) collective-permute-start(bf16[1024,512]{1,0:T(8,128)(2,1)} %bitcast.35), channel_id=1, source_target_pairs={{0,1},{1,0},{2,3},{3,2},{4,5},{5,4},{6,7},{7,6},{8,9},{9,8},{10,11... | collective-permute-start | bytes 3145736 | tf_op jit(solution)/shard_map/ppermute | solution.py:394
  8.3 51.1 %copy-start.2 = (bf16[1,1024,512]{2,1,0:T(8,128)(2,1)S(1)}, bf16[1,1024,512]{2,1,0:T(8,128)(2,1)}, u32[]{:S(2)}) copy-start(bf16[1,1024,512]{2,1,0:T(8,128)(2,1)} %param.10) | copy-start | bytes 3145732
  8.3 51.1 %copy-start.3 = (bf16[2,512,512]{2,1,0:T(8,128)(2,1)S(1)}, bf16[2,512,512]{2,1,0:T(8,128)(2,1)}, u32[]{:S(2)}) copy-start(bf16[2,512,512]{2,1,0:T(8,128)(2,1)} %weights_ref.1) | copy-start | bytes 3145732
  11.1 11.6 %collective-permute-start.3 = (bf16[400,128]{1,0:T(8,128)(2,1)S(1)}, bf16[400,128]{1,0:T(8,128)(2,1)S(1)}, u32[]{:S(2)}, u32[]{:S(2)}) collective-permute-start(bf16[400,128]{1,0:T(8,128)(2,1)S(1)} %get-tuple-element.28), channel_id=1, source_target_pairs={{0,4},{1,5},{2,6},{3,7},{4,0},{5,1},{6,2},{7,3},{8,12},{9,13},{10,... | collective-permute-start | bytes 307208 | tf_op jit(solution)/shard_map/ppermute | solution.py:394
  22.7 15.9 %collective-permute-start.4 = (bf16[768,512]{1,0:T(8,128)(2,1)S(1)}, bf16[768,512]{1,0:T(8,128)(2,1)S(1)}, u32[]{:S(2)}, u32[]{:S(2)}) collective-permute-start(bf16[768,512]{1,0:T(8,128)(2,1)S(1)} %pad_maximum_fusion.refs_0_), channel_id=1, source_target_pairs={{0,8},{1,17},{2,10},{3,19},{4,12},{5,21},{6,14},{7,23},{8,0},{9,25... | collective-permute-start | bytes 2359304 | tf_op jit(solution)/shard_map/ppermute | solution.py:405
  24.2 12.4 %collective-permute-start.8 = (bf16[256,512]{1,0:T(8,128)(2,1)S(1)}, bf16[256,512]{1,0:T(8,128)(2,1)S(1)}, u32[]{:S(2)}, u32[]{:S(2)}) collective-permute-start(bf16[256,512]{1,0:T(8,128)(2,1)S(1)} %collective-permute-done.2), channel_id=1, source_target_pairs={{0,2},{1,3},{2,0},{3,1},{4,6},{5,7},{6,4},{7,5},{8,10},{9,11},{10,... | collective-permute-start | bytes 786440 | tf_op jit(solution)/shard_map/ppermute | solution.py:394
  24.2 34.2 %collective-permute-start.7 = (bf16[1664,128]{1,0:T(8,128)(2,1)S(1)}, bf16[1664,128]{1,0:T(8,128)(2,1)S(1)}, u32[]{:S(2)}, u32[]{:S(2)}) collective-permute-start(bf16[1664,128]{1,0:T(8,128)(2,1)S(1)} %get-tuple-element.32), channel_id=1, source_target_pairs={{0,4},{1,5},{2,6},{3,7},{4,0},{5,1},{6,2},{7,3},{8,12},{9,13},{10,... | collective-permute-start | bytes 1277960 | tf_op jit(solution)/shard_map/ppermute | solution.py:394
  36.6 9.2 %collective-permute-start.9 = (bf16[256,512]{1,0:T(8,128)(2,1)S(1)}, bf16[256,512]{1,0:T(8,128)(2,1)S(1)}, u32[]{:S(2)}, u32[]{:S(2)}) collective-permute-start(bf16[256,512]{1,0:T(8,128)(2,1)S(1)} %collective-permute-done.8), channel_id=1, source_target_pairs={{0,8},{1,17},{2,10},{3,19},{4,12},{5,21},{6,14},{7,23},{8,0},{9,25... | collective-permute-start | bytes 786440 | tf_op jit(solution)/shard_map/ppermute | solution.py:405
  38.0 23.0 %collective-permute-start.5 = (bf16[768,512]{1,0:T(8,128)(2,1)S(1)}, bf16[768,512]{1,0:T(8,128)(2,1)S(1)}, u32[]{:S(2)}, u32[]{:S(2)}) collective-permute-start(bf16[768,512]{1,0:T(8,128)(2,1)S(1)} %pad_maximum_fusion.refs_0_), channel_id=1, source_target_pairs={{0,16},{1,9},{2,18},{3,11},{4,20},{5,13},{6,22},{7,15},{8,24},{9,1... | collective-permute-start | bytes 2359304 | tf_op jit(solution)/shard_map/ppermute | solution.py:405
  38.6 22.5 %collective-permute-start.6 = (bf16[768,512]{1,0:T(8,128)(2,1)S(1)}, bf16[768,512]{1,0:T(8,128)(2,1)S(1)}, u32[]{:S(2)}, u32[]{:S(2)}) collective-permute-start(bf16[768,512]{1,0:T(8,128)(2,1)S(1)} %collective-permute-done.4.refs_1_), channel_id=1, source_target_pairs={{0,16},{1,9},{2,18},{3,11},{4,20},{5,13},{6,22},{7,15},{8,24},{9,1... | collective-permute-start | bytes 2359304 | tf_op jit(solution)/shard_map/ppermute | solution.py:405
  40.1 24.6 %collective-permute-start.12 = (bf16[2064,128]{1,0:T(8,128)(2,1)S(1)}, bf16[2064,128]{1,0:T(8,128)(2,1)S(1)}, u32[]{:S(2)}, u32[]{:S(2)}) collective-permute-start(bf16[2064,128]{1,0:T(8,128)(2,1)S(1)} %get-tuple-element.41), channel_id=1, source_target_pairs={{0,6},{1,7},{2,4},{3,5},{4,2},{5,3},{6,0},{7,1},{8,14},{9,15},{10,... | collective-permute-start | bytes 1585160 | tf_op jit(solution)/shard_map/ppermute | solution.py:394
  45.8 22.6 %collective-permute-start.11 = (bf16[2064,128]{1,0:T(8,128)(2,1)S(1)}, bf16[2064,128]{1,0:T(8,128)(2,1)S(1)}, u32[]{:S(2)}, u32[]{:S(2)}) collective-permute-start(bf16[2064,128]{1,0:T(8,128)(2,1)S(1)} %get-tuple-element.39), channel_id=1, source_target_pairs={{0,2},{1,3},{2,0},{3,1},{4,6},{5,7},{6,4},{7,5},{8,10},{9,11},{10,... | collective-permute-start | bytes 1585160 | tf_op jit(solution)/shard_map/ppermute | solution.py:394
  58.4 9.2 %collective-permute-start.10 = (bf16[512,512]{1,0:T(8,128)(2,1)S(1)}, bf16[512,512]{1,0:T(8,128)(2,1)S(1)}, u32[]{:S(2)}, u32[]{:S(2)}) collective-permute-start(bf16[512,512]{1,0:T(8,128)(2,1)S(1)} %constant_dynamic-update-slice_fusion.refs_0_), channel_id=1, source_target_pairs={{0,16},{1,9},{2,18},{3,11},{4,20},{5,13},{6,22},{7,15},{8,24},{9,1... | collective-permute-start | bytes 1572872 | tf_op jit(solution)/shard_map/ppermute | solution.py:405
  73.0 3.7 %collective-permute-start.17 = (bf16[4,256,512]{2,1,0:T(8,128)(2,1)S(1)}, bf16[4,256,512]{2,1,0:T(8,128)(2,1)S(1)}, u32[]{:S(2)}, u32[]{:S(2)}) collective-permute-start(bf16[4,256,512]{2,1,0:T(8,128)(2,1)S(1)} %get-tuple-element.45), channel_id=1, source_target_pairs={{0,1},{1,0},{2,3},{3,2},{4,5},{5,4},{6,7},{7,6},{8,9},{9,8},{10,11... | collective-permute-start | bytes 3145736 | tf_op jit(solution)/shard_map/ppermute | solution.py:394
  76.2 4.2 %collective-permute-start.13 = (bf16[4,2,64,512]{3,2,1,0:T(8,128)(2,1)S(1)}, bf16[4,2,64,512]{3,2,1,0:T(8,128)(2,1)S(1)}, u32[]{:S(2)}, u32[]{:S(2)}) collective-permute-start(bf16[4,2,64,512]{3,2,1,0:T(8,128)(2,1)S(1)} %get-tuple-element.44), channel_id=1, source_target_pairs={{0,1},{1,0},{2,3},{3,2},{4,5},{5,4},{6,7},{7,6},{8,9},{9,8},{10,11... | collective-permute-start | bytes 1572872 | tf_op jit(solution)/shard_map/ppermute | solution.py:394
  78.8 9.2 %collective-permute-start.18 = (bf16[2,256,512]{2,1,0:T(8,128)(2,1)S(1)}, bf16[2,256,512]{2,1,0:T(8,128)(2,1)S(1)}, u32[]{:S(2)}, u32[]{:S(2)}) collective-permute-start(bf16[2,256,512]{2,1,0:T(8,128)(2,1)S(1)} %get-tuple-element.47), channel_id=1, source_target_pairs={{0,8},{1,17},{2,10},{3,19},{4,12},{5,21},{6,14},{7,23},{8,0},{9,25... | collective-permute-start | bytes 1572872 | tf_op jit(solution)/shard_map/ppermute | solution.py:405
  80.6 8.2 %copy-start.4 = (bf16[1,256,512]{2,1,0:T(8,128)(2,1)S(1)}, bf16[1,256,512]{2,1,0:T(8,128)(2,1)}, u32[]{:S(2)}) copy-start(bf16[1,256,512]{2,1,0:T(8,128)(2,1)} %param.9) | copy-start | bytes 786436
  80.6 8.5 %collective-permute-start.14 = (bf16[2,64,512]{2,1,0:T(8,128)(2,1)S(1)}, bf16[2,64,512]{2,1,0:T(8,128)(2,1)S(1)}, u32[]{:S(2)}, u32[]{:S(2)}) collective-permute-start(bf16[2,64,512]{2,1,0:T(8,128)(2,1)S(1)} %get-tuple-element.50), channel_id=1, source_target_pairs={{0,6},{1,7},{2,4},{3,5},{4,2},{5,3},{6,0},{7,1},{8,14},{9,15},{10,... | collective-permute-start | bytes 393224 | tf_op jit(solution)/shard_map/ppermute | solution.py:394
  82.2 11.5 %collective-permute-start.15 = (bf16[2,64,512]{2,1,0:T(8,128)(2,1)S(1)}, bf16[2,64,512]{2,1,0:T(8,128)(2,1)S(1)}, u32[]{:S(2)}, u32[]{:S(2)}) collective-permute-start(bf16[2,64,512]{2,1,0:T(8,128)(2,1)S(1)} %get-tuple-element.52), channel_id=1, source_target_pairs={{0,4},{1,5},{2,6},{3,7},{4,0},{5,1},{6,2},{7,3},{8,12},{9,13},{10,... | collective-permute-start | bytes 393224 | tf_op jit(solution)/shard_map/ppermute | solution.py:394
  82.8 10.9 %collective-permute-start.16 = (bf16[2,64,512]{2,1,0:T(8,128)(2,1)S(1)}, bf16[2,64,512]{2,1,0:T(8,128)(2,1)S(1)}, u32[]{:S(2)}, u32[]{:S(2)}) collective-permute-start(bf16[2,64,512]{2,1,0:T(8,128)(2,1)S(1)} %get-tuple-element.51), channel_id=1, source_target_pairs={{0,2},{1,3},{2,0},{3,1},{4,6},{5,7},{6,4},{7,5},{8,10},{9,11},{10,... | collective-permute-start | bytes 393224 | tf_op jit(solution)/shard_map/ppermute | solution.py:394
  88.2 6.4 %collective-permute-start.19 = (bf16[1,256,512]{2,1,0:T(8,128)(2,1)S(1)}, bf16[1,256,512]{2,1,0:T(8,128)(2,1)S(1)}, u32[]{:S(2)}, u32[]{:S(2)}) collective-permute-start(bf16[1,256,512]{2,1,0:T(8,128)(2,1)S(1)} %slice.54), channel_id=1, source_target_pairs={{0,16},{1,9},{2,18},{3,11},{4,20},{5,13},{6,22},{7,15},{8,24},{9,1... | collective-permute-start | bytes 786440 | tf_op jit(solution)/shard_map/ppermute | solution.py:405
  (1 other events, 1.2 us)

commit v7 on v6

--- a/solution.py
+++ b/solution.py
@@ -11,7 +11,7 @@
 CORES = 2
 SLOTS = CORES * CAPACITY
 LIMIT = 24 * 1024 * 1024
-HEAD = 3
+HEAD = 2
 SMEM = pl.BlockSpec(memory_space=pltpu.SMEM)
 VMEM = pl.BlockSpec(memory_space=pltpu.VMEM)
 ANY = pl.BlockSpec(memory_space=pl.ANY)

time: 95.7 us -> 95.7 us (level)
  no operation moved by 1% of the time
where the time goes in v7:
time: 95.7 us; the launch traced here: 95.5 us
  waiting for transfers between devices  46.9 us (49%)
  starting transfers between devices  24.7 us (26%)
  Pallas kernels  17.7 us (18%)
  other arithmetic  3.78 us (4%)
  local copies, waits for them, and re-layouts  1.34 us (1%)
    ppermute x13, waiting for transfers between devices, across(): return lax.ppermute(value, axis, [(i, i ^ mask) for i in range(size)])  37.1 us
    ppermute x13, starting transfers between devices, across(): return lax.ppermute(value, axis, [(i, i ^ mask) for i in range(size)])  16.9 us
    ppermute x7, waiting for transfers between devices, in_plane(): return lax.ppermute(value, ('rel', 'node'), pairs)  9.79 us
    ppermute x7, starting transfers between devices, in_plane(): return lax.ppermute(value, ('rel', 'node'), pairs)  7.78 us
    pallas_call x1, Pallas kernels, late_tiles_and_rows(): pl.pallas_call(functools.partial(late_kernel, parts, held, segments, size...  4.59 us
    pallas_call x1, Pallas kernels, early_tiles(): pl.pallas_call(functools.partial(early_kernel, parts, segments, groups),...  3.61 us
    pallas_call x1, Pallas kernels, grad_terms(): pl.pallas_call(functools.partial(grad_kernel, chips, relations), out_shap...  3.09 us
    pallas_call x1, Pallas kernels, place_tiles(): pl.pallas_call(functools.partial(place_kernel, parts, chips, blocks, rela...  2.76 us
  transfers between devices with their start and end apart: 20, of which 11 were waited for; matrix products, arithmetic and copies ran while one was open for 4% of the time, Pallas kernels for 14%

profile of v7, /device:TPU:0, one launch (start us, length us, event | category | flops | bytes accessed | tf_op | source)
XLA Modules:
  0.0 95.5 jit_solution(5606696732486878284)
XLA Ops:
  0.6 3.1 %collective-permute-start.1 = (bf16[256,512]{1,0:T(8,128)(2,1)}, bf16[256,512]{1,0:T(8,128)(2,1)S(1)}, u32[]{:S(2)}, u32[]{:S(2)}) collective-permute-start(bf16[256,512]{1,0:T(8,128)(2,1)} %bitcast.37), channel_id=1, source_target_pairs={{0,2},{1,3},{2,0},{3,1},{4,6},{5,7},{6,4},{7,5},{8,10},{9,11},{10,... | collective-permute-start | bytes 786440 | tf_op jit(solution)/shard_map/ppermute | solution.py:394
  3.7 2.6 %collective-permute-start.2 = (bf16[256,512]{1,0:T(8,128)(2,1)}, bf16[256,512]{1,0:T(8,128)(2,1)S(1)}, u32[]{:S(2)}, u32[]{:S(2)}) collective-permute-start(bf16[256,512]{1,0:T(8,128)(2,1)} %bitcast.38), channel_id=1, source_target_pairs={{0,4},{1,5},{2,6},{3,7},{4,0},{5,1},{6,2},{7,3},{8,12},{9,13},{10,... | collective-permute-start | bytes 786440 | tf_op jit(solution)/shard_map/ppermute | solution.py:394
  8.3 2.8 %place_tiles.1 = (bf16[2064,128]{1,0:T(8,128)(2,1)S(1)}, bf16[272,128]{1,0:T(8,128)(2,1)S(1)}, bf16[1792,128]{1,0:T(8,128)(2,1)S(1)}, bf16[2064,128]{1,0:T(8,128)(2,1)S(1)}, bf16[2064,128]{1,0:T(8,128)(2,1)S(1)}) custom-call(s32[4,32]{1,0:T(4,128)S(1)} %pad_add_fusion.refs_0_, bf16[32,128,128]{2,1,0:T(8,128)(2,1)S(1)} %bitcast.34, ...), custom_call_target="tpu_custom_call" | custom-call | bytes 4000000 | tf_op jit(solution)/shard_map/place_tiles/pallas_call | solution.py:73
  11.5 4.2 %collective-permute-done.1 = bf16[256,512]{1,0:T(8,128)(2,1)S(1)} collective-permute-done((bf16[256,512]{1,0:T(8,128)(2,1)}, bf16[256,512]{1,0:T(8,128)(2,1)S(1)}, u32[]{:S(2)}, u32[]{:S(2)}) %collective-permute-start.1) | collective-permute-done | bytes 262176 | tf_op jit(solution)/shard_map/ppermute | solution.py:394
  15.7 4.1 %collective-permute-done.2 = bf16[256,512]{1,0:T(8,128)(2,1)S(1)} collective-permute-done((bf16[256,512]{1,0:T(8,128)(2,1)}, bf16[256,512]{1,0:T(8,128)(2,1)S(1)}, u32[]{:S(2)}, u32[]{:S(2)}) %collective-permute-start.2) | collective-permute-done | bytes 262176 | tf_op jit(solution)/shard_map/ppermute | solution.py:394
  21.3 1.5 %collective-permute-start.4 = (bf16[768,512]{1,0:T(8,128)(2,1)S(1)}, bf16[768,512]{1,0:T(8,128)(2,1)S(1)}, u32[]{:S(2)}, u32[]{:S(2)}) collective-permute-start(bf16[768,512]{1,0:T(8,128)(2,1)S(1)} %pad_maximum_fusion.refs_0_), channel_id=1, source_target_pairs={{0,8},{1,17},{2,10},{3,19},{4,12},{5,21},{6,14},{7,23},{8,0},{9,25... | collective-permute-start | bytes 2359304 | tf_op jit(solution)/shard_map/ppermute | solution.py:405
  22.8 3.3 %collective-permute-start.7 = (bf16[1792,128]{1,0:T(8,128)(2,1)S(1)}, bf16[1792,128]{1,0:T(8,128)(2,1)S(1)}, u32[]{:S(2)}, u32[]{:S(2)}) collective-permute-start(bf16[1792,128]{1,0:T(8,128)(2,1)S(1)} %get-tuple-element.32), channel_id=1, source_target_pairs={{0,4},{1,5},{2,6},{3,7},{4,0},{5,1},{6,2},{7,3},{8,12},{9,13},{10,... | collective-permute-start | bytes 1376264 | tf_op jit(solution)/shard_map/ppermute | solution.py:394
  26.1 9.0 %collective-permute-done.8 = bf16[256,512]{1,0:T(8,128)(2,1)S(1)} collective-permute-done((bf16[256,512]{1,0:T(8,128)(2,1)S(1)}, bf16[256,512]{1,0:T(8,128)(2,1)S(1)}, u32[]{:S(2)}, u32[]{:S(2)}) %collective-permute-start.8) | collective-permute-done | bytes 262176 | tf_op jit(solution)/shard_map/ppermute | solution.py:394
  35.1 1.5 %collective-permute-start.9 = (bf16[256,512]{1,0:T(8,128)(2,1)S(1)}, bf16[256,512]{1,0:T(8,128)(2,1)S(1)}, u32[]{:S(2)}, u32[]{:S(2)}) collective-permute-start(bf16[256,512]{1,0:T(8,128)(2,1)S(1)} %collective-permute-done.8), channel_id=1, source_target_pairs={{0,8},{1,17},{2,10},{3,19},{4,12},{5,21},{6,14},{7,23},{8,0},{9,25... | collective-permute-start | bytes 786440 | tf_op jit(solution)/shard_map/ppermute | solution.py:405
  37.1 1.5 %collective-permute-start.6 = (bf16[768,512]{1,0:T(8,128)(2,1)S(1)}, bf16[768,512]{1,0:T(8,128)(2,1)S(1)}, u32[]{:S(2)}, u32[]{:S(2)}) collective-permute-start(bf16[768,512]{1,0:T(8,128)(2,1)S(1)} %collective-permute-done.4.refs_1_), channel_id=1, source_target_pairs={{0,16},{1,9},{2,18},{3,11},{4,20},{5,13},{6,22},{7,15},{8,24},{9,1... | collective-permute-start | bytes 2359304 | tf_op jit(solution)/shard_map/ppermute | solution.py:405
  38.7 2.4 %collective-permute-start.12 = (bf16[2064,128]{1,0:T(8,128)(2,1)S(1)}, bf16[2064,128]{1,0:T(8,128)(2,1)S(1)}, u32[]{:S(2)}, u32[]{:S(2)}) collective-permute-start(bf16[2064,128]{1,0:T(8,128)(2,1)S(1)} %get-tuple-element.41), channel_id=1, source_target_pairs={{0,6},{1,7},{2,4},{3,5},{4,2},{5,3},{6,0},{7,1},{8,14},{9,15},{10,... | collective-permute-start | bytes 1585160 | tf_op jit(solution)/shard_map/ppermute | solution.py:394
  41.1 3.3 %collective-permute-done.9 = bf16[256,512]{1,0:T(8,128)(2,1)S(1)} collective-permute-done((bf16[256,512]{1,0:T(8,128)(2,1)S(1)}, bf16[256,512]{1,0:T(8,128)(2,1)S(1)}, u32[]{:S(2)}, u32[]{:S(2)}) %collective-permute-start.9) | collective-permute-done | bytes 262176 | tf_op jit(solution)/shard_map/ppermute | solution.py:405
  44.5 14.3 %collective-permute-done.7.refs_6_ = bf16[1792,128]{1,0:T(8,128)(2,1)S(1)} collective-permute-done((bf16[1792,128]{1,0:T(8,128)(2,1)S(1)}, bf16[1792,128]{1,0:T(8,128)(2,1)S(1)}, u32[]{:S(2)}, u32[]{:S(2)}) %collective-permute-start.7) | collective-permute-done | bytes 458784 | tf_op jit(solution)/shard_map/ppermute | solution.py:394
  59.4 1.6 %turn_inputs.1 = (bf16[512,2048]{1,0:T(8,128)(2,1)S(1)}, bf16[1024,512]{1,0:T(8,128)(2,1)S(1)}) custom-call(s32[3]{0:T(128)S(1)} %pad_add_fusion.1.place_ref.refs_2_, bf16[1024,512]{1,0:T(8,128)(2,1)S(1)} %bitcast.36, bf16[1024,512]{1,0:T(8,128)(2,1)S(1)} %collective-permute-done.far_ref, bf16[2,512,512]{2,1,0:T(8,128)(2,1)S(1)} %copy-done.3), custom_call_target="tpu_custom_call" | custom-call | bytes 1000000 | tf_op jit(solution)/shard_map/turn_inputs/pallas_call | solution.py:279
  61.0 3.6 %early_tiles.1 = (bf16[3,1024,512]{2,1,0:T(8,128)(2,1)S(1)}, f32[32,128,512]{2,1,0:T(8,128)S(1)}) custom-call(s32[3]{0:T(128)S(1)} %pad_add_fusion.1.place_ref.refs_2_, bf16[768,512]{1,0:T(8,128)(2,1)S(1)} %pad_maximum_fusion.refs_0_, bf16[768,512]{1,0:T(8,128)(2,1)S(1)} %collective-permute-done.4.refs_1_, ...), custom_call_target="tpu_custom_call" | custom-call | bytes 1000000 | tf_op jit(solution)/shard_map/early_tiles/pallas_call | solution.py:165
  64.7 3.3 %collective-permute-done.10.refs_1_ = bf16[512,512]{1,0:T(8,128)(2,1)S(1)} collective-permute-done((bf16[512,512]{1,0:T(8,128)(2,1)S(1)}, bf16[512,512]{1,0:T(8,128)(2,1)S(1)}, u32[]{:S(2)}, u32[]{:S(2)}) %collective-permute-start.10) | collective-permute-done | bytes 524320 | tf_op jit(solution)/shard_map/ppermute | solution.py:405
  68.4 4.6 %late_tiles_and_rows.1 = (bf16[4,256,512]{2,1,0:T(8,128)(2,1)S(1)}, bf16[2048,1024]{1,0:T(8,128)(2,1)S(1)}, f32[32,128,512]{2,1,0:T(8,128)S(1)}) custom-call(s32[3]{0:T(128)S(1)} %pad_add_fusion.1.place_ref.refs_2_, bf16[3,1024,512]{2,1,0:T(8,128)(2,1)S(1)} %get-tuple-element.33.adjoint, ...), custom_call_target="tpu_custom_call", output_to_operand_aliasing={{2}: (2, {})} | custom-call | bytes 1000000 | tf_op jit(solution)/shard_map/late_tiles_and_rows/pallas_call | solution.py:239
  73.1 3.1 %grad_terms.1 = (bf16[4,2,64,512]{3,2,1,0:T(8,128)(2,1)S(1)}, f32[4,2,64,512]{3,2,1,0:T(8,128)S(1)}) custom-call(s32[3]{0:T(128)S(1)} %pad_add_fusion.1.place_ref.refs_2_, bf16[2048,1024]{1,0:T(8,128)(2,1)S(1)} %get-tuple-element.42.summed, bf16[512,2048]{1,0:T(8,128)(2,1)S(1)} %get-tuple-element.25.inputs_ref), custom_call_target="tpu_custom_call" | custom-call | bytes 1000000 | tf_op jit(solution)/shard_map/grad_terms/pallas_call | solution.py:348
  76.7 2.0 %row_terms.1 = (f32[2,256,512]{2,1,0:T(8,128)S(1)}, bf16[2,256,512]{2,1,0:T(8,128)(2,1)S(1)}) custom-call(s32[3]{0:T(128)S(1)} %pad_add_fusion.1.place_ref.refs_2_, bf16[2048,1024]{1,0:T(8,128)(2,1)S(1)} %get-tuple-element.42.summed, bf16[1024,512]{1,0:T(8,128)(2,1)S(1)} %get-tuple-element.26.refs_4_.weights_ref, ...), custom_call_target="tpu_custom_call" | custom-call | flops 2147483648 | bytes 4000000 | tf_op jit(solution)/shard_map/row_terms/pallas_call | solution.py:310
  78.8 1.5 %collective-permute-start.18 = (bf16[2,256,512]{2,1,0:T(8,128)(2,1)S(1)}, bf16[2,256,512]{2,1,0:T(8,128)(2,1)S(1)}, u32[]{:S(2)}, u32[]{:S(2)}) collective-permute-start(bf16[2,256,512]{2,1,0:T(8,128)(2,1)S(1)} %get-tuple-element.47), channel_id=1, source_target_pairs={{0,8},{1,17},{2,10},{3,19},{4,12},{5,21},{6,14},{7,23},{8,0},{9,25... | collective-permute-start | bytes 1572872 | tf_op jit(solution)/shard_map/ppermute | solution.py:405
  80.6 1.5 %collective-permute-start.14 = (bf16[2,64,512]{2,1,0:T(8,128)(2,1)S(1)}, bf16[2,64,512]{2,1,0:T(8,128)(2,1)S(1)}, u32[]{:S(2)}, u32[]{:S(2)}) collective-permute-start(bf16[2,64,512]{2,1,0:T(8,128)(2,1)S(1)} %get-tuple-element.50), channel_id=1, source_target_pairs={{0,6},{1,7},{2,4},{3,5},{4,2},{5,3},{6,0},{7,1},{8,14},{9,15},{10,... | collective-permute-start | bytes 393224 | tf_op jit(solution)/shard_map/ppermute | solution.py:394
  82.8 2.3 %collective-permute-start.16 = (bf16[2,64,512]{2,1,0:T(8,128)(2,1)S(1)}, bf16[2,64,512]{2,1,0:T(8,128)(2,1)S(1)}, u32[]{:S(2)}, u32[]{:S(2)}) collective-permute-start(bf16[2,64,512]{2,1,0:T(8,128)(2,1)S(1)} %get-tuple-element.51), channel_id=1, source_target_pairs={{0,2},{1,3},{2,0},{3,1},{4,6},{5,7},{6,4},{7,5},{8,10},{9,11},{10,... | collective-permute-start | bytes 393224 | tf_op jit(solution)/shard_map/ppermute | solution.py:394
  85.1 3.0 %collective-permute-done.18 = bf16[2,256,512]{2,1,0:T(8,128)(2,1)S(1)} collective-permute-done((bf16[2,256,512]{2,1,0:T(8,128)(2,1)S(1)}, bf16[2,256,512]{2,1,0:T(8,128)(2,1)S(1)}, u32[]{:S(2)}, u32[]{:S(2)}) %collective-permute-start.18) | collective-permute-done | bytes 524320 | tf_op jit(solution)/shard_map/ppermute | solution.py:405
  89.2 4.5 %collective-permute-done.15 = bf16[2,64,512]{2,1,0:T(8,128)(2,1)S(1)} collective-permute-done((bf16[2,64,512]{2,1,0:T(8,128)(2,1)S(1)}, bf16[2,64,512]{2,1,0:T(8,128)(2,1)S(1)}, u32[]{:S(2)}, u32[]{:S(2)}) %collective-permute-start.15) | collective-permute-done | bytes 131104 | tf_op jit(solution)/shard_map/ppermute | solution.py:394
  (44 shorter events, 10.1 us)
Async XLA Ops:
  0.6 88.2 %copy-start = (bf16[512,512]{1,0:T(8,128)(2,1)S(1)}, bf16[512,512]{1,0:T(8,128)(2,1)}, u32[]{:S(2)}) copy-start(bf16[512,512]{1,0:T(8,128)(2,1)} %param.12) | copy-start | bytes 1572868
  0.6 15.1 %collective-permute-start.1 = (bf16[256,512]{1,0:T(8,128)(2,1)}, bf16[256,512]{1,0:T(8,128)(2,1)S(1)}, u32[]{:S(2)}, u32[]{:S(2)}) collective-permute-start(bf16[256,512]{1,0:T(8,128)(2,1)} %bitcast.37), channel_id=1, source_target_pairs={{0,2},{1,3},{2,0},{3,1},{4,6},{5,7},{6,4},{7,5},{8,10},{9,11},{10,... | collective-permute-start | bytes 786440 | tf_op jit(solution)/shard_map/ppermute | solution.py:394
  3.7 16.1 %collective-permute-start.2 = (bf16[256,512]{1,0:T(8,128)(2,1)}, bf16[256,512]{1,0:T(8,128)(2,1)S(1)}, u32[]{:S(2)}, u32[]{:S(2)}) collective-permute-start(bf16[256,512]{1,0:T(8,128)(2,1)} %bitcast.38), channel_id=1, source_target_pairs={{0,4},{1,5},{2,6},{3,7},{4,0},{5,1},{6,2},{7,3},{8,12},{9,13},{10,... | collective-permute-start | bytes 786440 | tf_op jit(solution)/shard_map/ppermute | solution.py:394
  6.3 28.8 %collective-permute-start = (bf16[1024,512]{1,0:T(8,128)(2,1)}, bf16[1024,512]{1,0:T(8,128)(2,1)S(1)}, u32[]{:S(2)}, u32[]{:S(2)}) collective-permute-start(bf16[1024,512]{1,0:T(8,128)(2,1)} %bitcast.35), channel_id=1, source_target_pairs={{0,1},{1,0},{2,3},{3,2},{4,5},{5,4},{6,7},{7,6},{8,9},{9,8},{10,11... | collective-permute-start | bytes 3145736 | tf_op jit(solution)/shard_map/ppermute | solution.py:394
  8.3 51.1 %copy-start.2 = (bf16[1,1024,512]{2,1,0:T(8,128)(2,1)S(1)}, bf16[1,1024,512]{2,1,0:T(8,128)(2,1)}, u32[]{:S(2)}) copy-start(bf16[1,1024,512]{2,1,0:T(8,128)(2,1)} %param.10) | copy-start | bytes 3145732
  8.3 51.1 %copy-start.3 = (bf16[2,512,512]{2,1,0:T(8,128)(2,1)S(1)}, bf16[2,512,512]{2,1,0:T(8,128)(2,1)}, u32[]{:S(2)}) copy-start(bf16[2,512,512]{2,1,0:T(8,128)(2,1)} %weights_ref.1) | copy-start | bytes 3145732
  11.1 10.2 %collective-permute-start.3 = (bf16[272,128]{1,0:T(8,128)(2,1)S(1)}, bf16[272,128]{1,0:T(8,128)(2,1)S(1)}, u32[]{:S(2)}, u32[]{:S(2)}) collective-permute-start(bf16[272,128]{1,0:T(8,128)(2,1)S(1)} %get-tuple-element.28), channel_id=1, source_target_pairs={{0,4},{1,5},{2,6},{3,7},{4,0},{5,1},{6,2},{7,3},{8,12},{9,13},{10,... | collective-permute-start | bytes 208904 | tf_op jit(solution)/shard_map/ppermute | solution.py:394
  21.3 15.9 %collective-permute-start.4 = (bf16[768,512]{1,0:T(8,128)(2,1)S(1)}, bf16[768,512]{1,0:T(8,128)(2,1)S(1)}, u32[]{:S(2)}, u32[]{:S(2)}) collective-permute-start(bf16[768,512]{1,0:T(8,128)(2,1)S(1)} %pad_maximum_fusion.refs_0_), channel_id=1, source_target_pairs={{0,8},{1,17},{2,10},{3,19},{4,12},{5,21},{6,14},{7,23},{8,0},{9,25... | collective-permute-start | bytes 2359304 | tf_op jit(solution)/shard_map/ppermute | solution.py:405
  22.8 12.4 %collective-permute-start.8 = (bf16[256,512]{1,0:T(8,128)(2,1)S(1)}, bf16[256,512]{1,0:T(8,128)(2,1)S(1)}, u32[]{:S(2)}, u32[]{:S(2)}) collective-permute-start(bf16[256,512]{1,0:T(8,128)(2,1)S(1)} %collective-permute-done.2), channel_id=1, source_target_pairs={{0,2},{1,3},{2,0},{3,1},{4,6},{5,7},{6,4},{7,5},{8,10},{9,11},{10,... | collective-permute-start | bytes 786440 | tf_op jit(solution)/shard_map/ppermute | solution.py:394
  22.8 35.9 %collective-permute-start.7 = (bf16[1792,128]{1,0:T(8,128)(2,1)S(1)}, bf16[1792,128]{1,0:T(8,128)(2,1)S(1)}, u32[]{:S(2)}, u32[]{:S(2)}) collective-permute-start(bf16[1792,128]{1,0:T(8,128)(2,1)S(1)} %get-tuple-element.32), channel_id=1, source_target_pairs={{0,4},{1,5},{2,6},{3,7},{4,0},{5,1},{6,2},{7,3},{8,12},{9,13},{10,... | collective-permute-start | bytes 1376264 | tf_op jit(solution)/shard_map/ppermute | solution.py:394
  35.1 9.2 %collective-permute-start.9 = (bf16[256,512]{1,0:T(8,128)(2,1)S(1)}, bf16[256,512]{1,0:T(8,128)(2,1)S(1)}, u32[]{:S(2)}, u32[]{:S(2)}) collective-permute-start(bf16[256,512]{1,0:T(8,128)(2,1)S(1)} %collective-permute-done.8), channel_id=1, source_target_pairs={{0,8},{1,17},{2,10},{3,19},{4,12},{5,21},{6,14},{7,23},{8,0},{9,25... | collective-permute-start | bytes 786440 | tf_op jit(solution)/shard_map/ppermute | solution.py:405
  36.6 24.4 %collective-permute-start.5 = (bf16[768,512]{1,0:T(8,128)(2,1)S(1)}, bf16[768,512]{1,0:T(8,128)(2,1)S(1)}, u32[]{:S(2)}, u32[]{:S(2)}) collective-permute-start(bf16[768,512]{1,0:T(8,128)(2,1)S(1)} %pad_maximum_fusion.refs_0_), channel_id=1, source_target_pairs={{0,16},{1,9},{2,18},{3,11},{4,20},{5,13},{6,22},{7,15},{8,24},{9,1... | collective-permute-start | bytes 2359304 | tf_op jit(solution)/shard_map/ppermute | solution.py:405
  37.1 23.9 %collective-permute-start.6 = (bf16[768,512]{1,0:T(8,128)(2,1)S(1)}, bf16[768,512]{1,0:T(8,128)(2,1)S(1)}, u32[]{:S(2)}, u32[]{:S(2)}) collective-permute-start(bf16[768,512]{1,0:T(8,128)(2,1)S(1)} %collective-permute-done.4.refs_1_), channel_id=1, source_target_pairs={{0,16},{1,9},{2,18},{3,11},{4,20},{5,13},{6,22},{7,15},{8,24},{9,1... | collective-permute-start | bytes 2359304 | tf_op jit(solution)/shard_map/ppermute | solution.py:405
  38.7 26.0 %collective-permute-start.12 = (bf16[2064,128]{1,0:T(8,128)(2,1)S(1)}, bf16[2064,128]{1,0:T(8,128)(2,1)S(1)}, u32[]{:S(2)}, u32[]{:S(2)}) collective-permute-start(bf16[2064,128]{1,0:T(8,128)(2,1)S(1)} %get-tuple-element.41), channel_id=1, source_target_pairs={{0,6},{1,7},{2,4},{3,5},{4,2},{5,3},{6,0},{7,1},{8,14},{9,15},{10,... | collective-permute-start | bytes 1585160 | tf_op jit(solution)/shard_map/ppermute | solution.py:394
  44.4 24.0 %collective-permute-start.11 = (bf16[2064,128]{1,0:T(8,128)(2,1)S(1)}, bf16[2064,128]{1,0:T(8,128)(2,1)S(1)}, u32[]{:S(2)}, u32[]{:S(2)}) collective-permute-start(bf16[2064,128]{1,0:T(8,128)(2,1)S(1)} %get-tuple-element.39), channel_id=1, source_target_pairs={{0,2},{1,3},{2,0},{3,1},{4,6},{5,7},{6,4},{7,5},{8,10},{9,11},{10,... | collective-permute-start | bytes 1585160 | tf_op jit(solution)/shard_map/ppermute | solution.py:394
  58.8 9.2 %collective-permute-start.10 = (bf16[512,512]{1,0:T(8,128)(2,1)S(1)}, bf16[512,512]{1,0:T(8,128)(2,1)S(1)}, u32[]{:S(2)}, u32[]{:S(2)}) collective-permute-start(bf16[512,512]{1,0:T(8,128)(2,1)S(1)} %constant_dynamic-update-slice_fusion.refs_0_), channel_id=1, source_target_pairs={{0,16},{1,9},{2,18},{3,11},{4,20},{5,13},{6,22},{7,15},{8,24},{9,1... | collective-permute-start | bytes 1572872 | tf_op jit(solution)/shard_map/ppermute | solution.py:405
  73.0 3.7 %collective-permute-start.17 = (bf16[4,256,512]{2,1,0:T(8,128)(2,1)S(1)}, bf16[4,256,512]{2,1,0:T(8,128)(2,1)S(1)}, u32[]{:S(2)}, u32[]{:S(2)}) collective-permute-start(bf16[4,256,512]{2,1,0:T(8,128)(2,1)S(1)} %get-tuple-element.45), channel_id=1, source_target_pairs={{0,1},{1,0},{2,3},{3,2},{4,5},{5,4},{6,7},{7,6},{8,9},{9,8},{10,11... | collective-permute-start | bytes 3145736 | tf_op jit(solution)/shard_map/ppermute | solution.py:394
  76.2 4.2 %collective-permute-start.13 = (bf16[4,2,64,512]{3,2,1,0:T(8,128)(2,1)S(1)}, bf16[4,2,64,512]{3,2,1,0:T(8,128)(2,1)S(1)}, u32[]{:S(2)}, u32[]{:S(2)}) collective-permute-start(bf16[4,2,64,512]{3,2,1,0:T(8,128)(2,1)S(1)} %get-tuple-element.44), channel_id=1, source_target_pairs={{0,1},{1,0},{2,3},{3,2},{4,5},{5,4},{6,7},{7,6},{8,9},{9,8},{10,11... | collective-permute-start | bytes 1572872 | tf_op jit(solution)/shard_map/ppermute | solution.py:394
  78.8 9.2 %collective-permute-start.18 = (bf16[2,256,512]{2,1,0:T(8,128)(2,1)S(1)}, bf16[2,256,512]{2,1,0:T(8,128)(2,1)S(1)}, u32[]{:S(2)}, u32[]{:S(2)}) collective-permute-start(bf16[2,256,512]{2,1,0:T(8,128)(2,1)S(1)} %get-tuple-element.47), channel_id=1, source_target_pairs={{0,8},{1,17},{2,10},{3,19},{4,12},{5,21},{6,14},{7,23},{8,0},{9,25... | collective-permute-start | bytes 1572872 | tf_op jit(solution)/shard_map/ppermute | solution.py:405
  80.6 8.2 %copy-start.4 = (bf16[1,256,512]{2,1,0:T(8,128)(2,1)S(1)}, bf16[1,256,512]{2,1,0:T(8,128)(2,1)}, u32[]{:S(2)}) copy-start(bf16[1,256,512]{2,1,0:T(8,128)(2,1)} %param.9) | copy-start | bytes 786436
  80.6 8.5 %collective-permute-start.14 = (bf16[2,64,512]{2,1,0:T(8,128)(2,1)S(1)}, bf16[2,64,512]{2,1,0:T(8,128)(2,1)S(1)}, u32[]{:S(2)}, u32[]{:S(2)}) collective-permute-start(bf16[2,64,512]{2,1,0:T(8,128)(2,1)S(1)} %get-tuple-element.50), channel_id=1, source_target_pairs={{0,6},{1,7},{2,4},{3,5},{4,2},{5,3},{6,0},{7,1},{8,14},{9,15},{10,... | collective-permute-start | bytes 393224 | tf_op jit(solution)/shard_map/ppermute | solution.py:394
  82.2 11.5 %collective-permute-start.15 = (bf16[2,64,512]{2,1,0:T(8,128)(2,1)S(1)}, bf16[2,64,512]{2,1,0:T(8,128)(2,1)S(1)}, u32[]{:S(2)}, u32[]{:S(2)}) collective-permute-start(bf16[2,64,512]{2,1,0:T(8,128)(2,1)S(1)} %get-tuple-element.52), channel_id=1, source_target_pairs={{0,4},{1,5},{2,6},{3,7},{4,0},{5,1},{6,2},{7,3},{8,12},{9,13},{10,... | collective-permute-start | bytes 393224 | tf_op jit(solution)/shard_map/ppermute | solution.py:394
  82.8 10.9 %collective-permute-start.16 = (bf16[2,64,512]{2,1,0:T(8,128)(2,1)S(1)}, bf16[2,64,512]{2,1,0:T(8,128)(2,1)S(1)}, u32[]{:S(2)}, u32[]{:S(2)}) collective-permute-start(bf16[2,64,512]{2,1,0:T(8,128)(2,1)S(1)} %get-tuple-element.51), channel_id=1, source_target_pairs={{0,2},{1,3},{2,0},{3,1},{4,6},{5,7},{6,4},{7,5},{8,10},{9,11},{10,... | collective-permute-start | bytes 393224 | tf_op jit(solution)/shard_map/ppermute | solution.py:394
  88.2 6.4 %collective-permute-start.19 = (bf16[1,256,512]{2,1,0:T(8,128)(2,1)S(1)}, bf16[1,256,512]{2,1,0:T(8,128)(2,1)S(1)}, u32[]{:S(2)}, u32[]{:S(2)}) collective-permute-start(bf16[1,256,512]{2,1,0:T(8,128)(2,1)S(1)} %slice.54), channel_id=1, source_target_pairs={{0,16},{1,9},{2,18},{3,11},{4,20},{5,13},{6,22},{7,15},{8,24},{9,1... | collective-permute-start | bytes 786440 | tf_op jit(solution)/shard_map/ppermute | solution.py:405
  (1 other events, 1.2 us)
